TPU v7x, 32 devices: a whole 2x2x4 slice. The times are simulated.
32 devices in a mesh: row: 8 (over z, x), col: 4 (over y, core).
Axes of the slice: x: 2, y: 2, z: 4, core: 2. Of those that a mesh axis runs over, the one named last changes fastest.
Arguments:
- tokens: bfloat16 [256, 128, 384], P('row', 'col'), may hold values from -6 to 6
- first_gain: float32 [384], replicated, may hold values from 0.1 to 1.9
- second_gain: float32 [384], replicated, may hold values from 0.1 to 1.9
- joint_weight: bfloat16 [384, 1152], replicated, may hold values from -0.3125 to 0.3125
- merge_weight: bfloat16 [384, 384], replicated, may hold values from -0.3125 to 0.3125
- expand_weight: bfloat16 [384, 1536], replicated, may hold values from -0.3125 to 0.3125
- shrink_weight: bfloat16 [1536, 384], replicated, may hold values from -0.15625 to 0.15625
- relative_bias: float32 [12, 64, 64], replicated, may hold values from -4 to 270
- lateral_weight: bfloat16 [384, 256], replicated, may hold values from -0.3125 to 0.3125
- conv_weight: bfloat16 [4, 2304, 256], replicated, may hold values from -0.125 to 0.125
- mask_weight: bfloat16 [256], replicated, may hold values from -0.375 to 0.375
- box_geometry: int32 [8, 4, 16, 4], P('row', 'col'), may hold values from 0 to 18, as said below
- box_counts: int32 [8, 4], P('row', 'col'), may hold values from 0 to 16, as said below
- box_owner: int32 [8, 4, 16], P('row', 'col'), may hold values from -1 to 7, as said below
- soft_target: bfloat16 [8, 4, 16, 196], P('row', 'col'), may hold values from 0 to 1
Outputs:
- features: bfloat16 [256, 128, 256], P('row', 'col')
- feature_grad: float32 [256, 128, 256], P('row', 'col')
- mask_logits: float32 [8, 4, 8, 196], P('row', 'col')
Inputs may be any that keep to these rules, and one draw needn't show every extreme that they name: `box_geometry`: components are top from 0 to 18, left from 0 to 18, height and width from 4 to 14; every slot, used or not, holds such a box. `box_counts`: the counts of one tile column sum to 8 times the tiles along the column; some tile of every column holds exactly 16 boxes. `box_owner`: A slot at or beyond its tile's count holds -1, a used slot an owner in its tile column; every owner is named by exactly 8 boxes of its column, and a tile names one owner at most 2 times, a bound reached by every tile holding 16 boxes.
All inputs are finite; a program needn't handle non-finite values.
Results may differ from a plain program's by a relative error of at most 0.02.
Values may be sent and summed in bfloat16 or wider, within the bound.
No kernel may reach another device: no remote copies, remote signals or barrier semaphores. Data moves between devices by JAX's collectives and lax.ppermute only.
A program may use at most 128 MiB of HBM per device.

v0:
```python
import functools
import jax
import jax.numpy as jnp
from jax import lax
from jax.experimental import pallas as pl
from jax.experimental.pallas import tpu as pltpu
from jax.sharding import PartitionSpec as P

CROP = 14
PAD = CROP + 2
GELU_A = 0.7978845608028654
GELU_B = 0.044715
loss_scale = 128.0
NT = (((1,), (1,)), ((), ()))
TN = (((0,), (0,)), ((), ()))


def gelu_parts(x):
    square = x * x
    inner = x * (GELU_A + (GELU_A * GELU_B) * square)
    half = 0.5 + 0.5 * jnp.tanh(inner)
    value = x * half
    slope = half + value * (1.0 - half) * (2.0 * GELU_A + (6.0 * GELU_A * GELU_B) * square)
    return value, slope


def gelu_value(x):
    inner = x * (GELU_A + (GELU_A * GELU_B) * (x * x))
    return x * (0.5 + 0.5 * jnp.tanh(inner))


def clear_border(ref):
    blank = jnp.zeros((PAD,) + ref.shape[2:], ref.dtype)
    ref[0] = blank
    ref[PAD - 1] = blank

    def body(row, carry):
        ref[row, 0] = jnp.zeros(ref.shape[2:], ref.dtype)
        ref[row, PAD - 1] = jnp.zeros(ref.shape[2:], ref.dtype)
        return carry

    lax.fori_loop(1, PAD - 1, body, 0)


def taps_of(ref, row, rows, flip):
    boxes, channels = ref.shape[2:]
    pieces = []
    for s in range(3):
        for t in range(3):
            s0, t0 = (2 - s, 2 - t) if flip else (s, t)
            part = ref[pl.ds(row + s0, rows), t0 : t0 + CROP]
            pieces.append(part.reshape(rows * CROP * boxes, channels))
    return pieces


def mask_forward_kernel(
    rows, geom_ref, count_ref, geomv_ref, features_ref, weight_ref, mask_ref,
    logits_ref, slope_ref, a_ref, b_ref, strip_ref, pick_ref,
):
    boxes, tile_cols, channels = strip_ref.shape
    layers = weight_ref.shape[0]
    clear_border(a_ref)
    clear_border(b_ref)
    lane = lax.broadcasted_iota(jnp.int32, (boxes, boxes * tile_cols), 1)
    sub = lax.broadcasted_iota(jnp.int32, (boxes, boxes * tile_cols), 0)
    mine = (lane // tile_cols == sub) & (sub < count_ref[0])
    away = jnp.where(mine, lane % tile_cols - geomv_ref[:, 1:2], -1)
    away = jnp.where(away < geomv_ref[:, 3:4], away, -1)
    for v in range(CROP):
        pick_ref[v * boxes : (v + 1) * boxes, :] = (away == v).astype(jnp.bfloat16)

    def cut(u, carry):
        for n in range(boxes):
            row = features_ref[geom_ref[n, 0] + u]
            strip_ref[n] = jnp.where(u < geom_ref[n, 2], row, jnp.zeros_like(row))
        crop = jnp.dot(
            pick_ref[...], strip_ref[...].reshape(-1, channels), preferred_element_type=jnp.float32
        )
        a_ref[u + 1, 1 : 1 + CROP] = crop.astype(jnp.bfloat16).reshape(CROP, boxes, channels)
        return carry

    lax.fori_loop(0, CROP, cut, 0)
    steps = CROP // rows
    source, target = a_ref, b_ref
    for layer in range(layers):
        last = layer == layers - 1

        def product(step):
            return jnp.dot(
                jnp.concatenate(taps_of(source, step * rows, rows, False), axis=1),
                weight_ref[layer],
                preferred_element_type=jnp.float32,
            )

        def finish(before, step):
            value, slope = gelu_parts(before)
            value = value.astype(jnp.bfloat16)
            slope_ref[layer, pl.ds(step * rows, rows)] = slope.astype(jnp.bfloat16).reshape(
                rows, CROP * boxes, channels
            )
            if last:
                for r in range(rows):
                    line = value[r * CROP * boxes : (r + 1) * CROP * boxes]
                    logits_ref[pl.ds(step * rows + r, 1), :] = lax.dot_general(
                        mask_ref[...], line, NT, preferred_element_type=jnp.float32
                    )[0:1]
            else:
                target[pl.ds(step * rows + 1, rows), 1 : 1 + CROP] = value.reshape(
                    rows, CROP, boxes, channels
                )

        def body(step, before):
            after = product(step)
            finish(before, step - 1)
            return after

        before = lax.fori_loop(1, steps, body, product(0))
        finish(before, steps - 1)
        source, target = target, source


def mask_backward_kernel(
    rows, geom_ref, count_ref, logits_ref, soft_ref, slope_ref, weight_ref, mask_ref,
    grad_ref, a_ref, b_ref, spread_ref, pick_ref, lead_ref,
):
    boxes, channels = a_ref.shape[2:]
    tile_cols = grad_ref.shape[1]
    layers = weight_ref.shape[0]
    lanes = CROP * boxes
    clear_border(a_ref)
    clear_border(b_ref)
    grad_ref[...] = jnp.zeros_like(grad_ref)
    lane = lax.broadcasted_iota(jnp.int32, (1, lanes), 1)
    box, col = lane % boxes, lane // boxes
    height = jnp.zeros((1, lanes), jnp.int32)
    offset = jnp.zeros((1, lanes), jnp.int32)
    kept = jnp.zeros((1, lanes), jnp.bool_)
    for n in range(boxes):
        here = box == n
        valid = n < count_ref[0]
        height = jnp.where(here, jnp.where(valid, geom_ref[n, 2], 0), height)
        offset = jnp.where(here, jnp.where(valid, geom_ref[n, 1], -tile_cols), offset)
        offset = jnp.where(here & (col >= geom_ref[n, 3]), -tile_cols, offset)
    inside = (lax.broadcasted_iota(jnp.int32, (CROP, lanes), 0) < height) & (offset >= 0)
    for n in range(boxes):
        cell = lax.broadcasted_iota(jnp.int32, (tile_cols, lanes), 0)
        pick_ref[n * tile_cols : (n + 1) * tile_cols, :] = (
            (cell == col + offset) & (box == n)
        ).astype(jnp.bfloat16)
    grad_logits = jnp.where(
        inside, loss_scale * (jax.nn.sigmoid(logits_ref[...]) - soft_ref[...]), 0.0
    )
    high = grad_logits.astype(jnp.bfloat16).astype(jnp.float32)
    lead_ref[0] = high
    lead_ref[1] = grad_logits - high

    def top(u, carry):
        pair = jnp.concatenate(
            [lead_ref[0, pl.ds(u, 1)], lead_ref[1, pl.ds(u, 1)], jnp.zeros((6, lanes), jnp.float32)],
            axis=0,
        ).astype(jnp.bfloat16)
        grad = lax.dot_general(pair, mask_ref[...], TN, preferred_element_type=jnp.float32)
        grad = grad * slope_ref[layers - 1, u].astype(jnp.float32)
        a_ref[u + 1, 1 : 1 + CROP] = grad.astype(jnp.bfloat16).reshape(CROP, boxes, channels)
        return carry

    lax.fori_loop(0, CROP, top, 0)
    steps = CROP // rows
    source, target = a_ref, b_ref
    for layer in reversed(range(layers)):

        def product(step):
            total = None
            for tap, piece in enumerate(taps_of(source, step * rows, rows, True)):
                part = lax.dot_general(
                    piece,
                    weight_ref[layer, tap * channels : (tap + 1) * channels, :],
                    NT,
                    preferred_element_type=jnp.float32,
                )
                total = part if total is None else total + part
            return total

        def finish(grad, step):
            if layer > 0:
                slope = slope_ref[layer - 1, pl.ds(step * rows, rows)].astype(jnp.float32)
                grad = (grad * slope.reshape(-1, channels)).astype(jnp.bfloat16)
                target[pl.ds(step * rows + 1, rows), 1 : 1 + CROP] = grad.reshape(
                    rows, CROP, boxes, channels
                )
                return
            grad = grad.astype(jnp.bfloat16)
            for r in range(rows):
                u = step * rows + r
                spread_ref[...] = jnp.dot(
                    pick_ref[...], grad[r * lanes : (r + 1) * lanes], preferred_element_type=jnp.float32
                )
                for n in range(boxes):
                    row = geom_ref[n, 0] + u
                    part = spread_ref[n * tile_cols : (n + 1) * tile_cols]
                    grad_ref[row] = grad_ref[row] + jnp.where(u < geom_ref[n, 2], part, 0.0)

        def body(step, before):
            after = product(step)
            finish(before, step - 1)
            return after

        before = lax.fori_loop(1, steps, body, product(0))
        finish(before, steps - 1)
        source, target = target, source


VMEM = pl.BlockSpec(memory_space=pltpu.VMEM)
SMEM = pl.BlockSpec(memory_space=pltpu.SMEM)


def mask_forward(features, geometry, count, weight, mask_pad, rows=1):
    tile_rows, tile_cols, channels = features.shape
    boxes = geometry.shape[0]
    layers = weight.shape[0]
    lanes = CROP * boxes
    return pl.pallas_call(
        functools.partial(mask_forward_kernel, rows),
        out_shape=(
            jax.ShapeDtypeStruct((CROP, lanes), jnp.float32),
            jax.ShapeDtypeStruct((layers, CROP, lanes, channels), jnp.bfloat16),
        ),
        in_specs=[SMEM, SMEM, VMEM, VMEM, VMEM, VMEM],
        out_specs=(VMEM, VMEM),
        scratch_shapes=[
            pltpu.VMEM((PAD, PAD, boxes, channels), jnp.bfloat16),
            pltpu.VMEM((PAD, PAD, boxes, channels), jnp.bfloat16),
            pltpu.VMEM((boxes, tile_cols, channels), jnp.bfloat16),
            pltpu.VMEM((lanes, boxes * tile_cols), jnp.bfloat16),
        ],
        compiler_params=pltpu.CompilerParams(vmem_limit_bytes=40 * 2**20),
        name="mask_forward",
    )(geometry, count, geometry, features, weight, mask_pad)


def mask_backward(logits, soft, slope, geometry, count, weight, mask_pad, tile, rows=1):
    layers, _, lanes, channels = slope.shape
    boxes = geometry.shape[0]
    tile_rows, tile_cols = tile
    return pl.pallas_call(
        functools.partial(mask_backward_kernel, rows),
        out_shape=jax.ShapeDtypeStruct((tile_rows, tile_cols, channels), jnp.float32),
        in_specs=[SMEM, SMEM, VMEM, VMEM, VMEM, VMEM, VMEM],
        out_specs=VMEM,
        scratch_shapes=[
            pltpu.VMEM((PAD, PAD, boxes, channels), jnp.bfloat16),
            pltpu.VMEM((PAD, PAD, boxes, channels), jnp.bfloat16),
            pltpu.VMEM((boxes * tile_cols, channels), jnp.float32),
            pltpu.VMEM((boxes * tile_cols, lanes), jnp.bfloat16),
            pltpu.VMEM((2, CROP, lanes), jnp.float32),
        ],
        compiler_params=pltpu.CompilerParams(vmem_limit_bytes=40 * 2**20),
        name="mask_backward",
    )(geometry, count, logits, soft, slope, weight, mask_pad)


HEADS = 12
WIN = 8
SUB = WIN // 2
CELL = SUB * SUB
AREA = WIN * WIN
GROUP = 4
EPSILON = 1e-05
BLOCKED = -1000000000.0
HIGHEST = lax.Precision.HIGHEST


def norm_rows(values, gain):
    centered = values - jnp.mean(values, axis=-1, keepdims=True)
    variance = jnp.mean(centered * centered, axis=-1, keepdims=True)
    return (centered * lax.rsqrt(variance + EPSILON) * gain).astype(jnp.bfloat16)


def one_hot(equal, dtype=jnp.bfloat16):
    return equal.astype(jnp.float32).astype(dtype)


def strip_order(width):
    size = SUB * width
    cell_pos = lax.broadcasted_iota(jnp.int32, (size, size), 0)
    token = lax.broadcasted_iota(jnp.int32, (size, size), 1)
    cell, row, col = cell_pos // CELL, cell_pos // SUB % SUB, cell_pos % SUB
    return one_hot(token == row * width + cell * SUB + col)


def window_order():
    place = lax.broadcasted_iota(jnp.int32, (AREA, AREA), 0)
    token = lax.broadcasted_iota(jnp.int32, (AREA, AREA), 1)
    cell, row, col = place // CELL, place // SUB % SUB, place % SUB
    return one_hot(token == (cell // 2 * SUB + row) * WIN + cell % 2 * SUB + col, jnp.float32)


def head_blocks(lanes):
    row = lax.broadcasted_iota(jnp.int32, (GROUP * AREA, lanes), 0)
    col = lax.broadcasted_iota(jnp.int32, (GROUP * AREA, lanes), 1)
    return one_hot(row // AREA == col // (lanes // GROUP))


def attend(queries, key_rows, value_rows, bias, blocks, key_mask):
    lanes = blocks.shape[1]
    scale = (lanes // GROUP) ** (-0.5)
    first = lax.broadcasted_iota(jnp.int32, (1, 2 * AREA), 1) < AREA
    mixed = []
    for group in range(len(bias)):
        cut = slice(group * lanes, (group + 1) * lanes)
        keys = jnp.concatenate([key_rows[:, cut]] * GROUP, axis=0) * blocks
        values = jnp.concatenate([value_rows[:, cut]] * GROUP, axis=0) * blocks
        scores = lax.dot_general(queries[:, cut], keys, NT, preferred_element_type=jnp.float32)
        scores = scores * scale + bias[group]
        if key_mask is not None:
            scores = scores + key_mask
        weights = []
        for pair in range(GROUP // 2):
            part = scores[:, pair * 2 * AREA : (pair + 1) * 2 * AREA]
            low = jnp.max(jnp.where(first, part, -jnp.inf), axis=-1, keepdims=True)
            high = jnp.max(jnp.where(first, -jnp.inf, part), axis=-1, keepdims=True)
            weights.append(jnp.exp(part - jnp.where(first, low, high)))
        weights = jnp.concatenate(weights, axis=1).astype(jnp.bfloat16)
        both = jnp.dot(
            weights, jnp.concatenate([values, blocks], axis=1), preferred_element_type=jnp.float32
        )
        mixed.append((both[:, :lanes] / both[:, lanes:]).astype(jnp.bfloat16))
    return jnp.concatenate(mixed, axis=1)


def joint_kernel(tokens_ref, gain_ref, joint_ref, relative_ref, out_ref, bias_ref, order_ref):
    width = order_ref.shape[0] // SUB
    strip = SUB * width
    order_ref[...] = strip_order(width)
    place = window_order()
    turned = lax.dot_general(
        relative_ref[...], place, NT, precision=HIGHEST, preferred_element_type=jnp.float32
    )
    for group in range(HEADS // GROUP):
        rows = [
            turned[(group * GROUP + h) * AREA : (group * GROUP + h + 1) * AREA]
            for h in range(GROUP)
        ]
        bias_ref[group] = jnp.dot(
            place,
            jnp.concatenate(rows, axis=1),
            precision=HIGHEST,
            preferred_element_type=jnp.float32,
        )

    def body(step, carry):
        normed = []
        for part in range(2):
            begin = pl.multiple_of((2 * step + part) * strip, strip)
            ordered = jnp.dot(
                order_ref[...], tokens_ref[pl.ds(begin, strip)], preferred_element_type=jnp.float32
            )
            normed.append(norm_rows(ordered, gain_ref[...]))
        normed = jnp.concatenate(normed, axis=0)
        begin = pl.multiple_of(2 * step * strip, 2 * strip)
        out_ref[pl.ds(begin, 2 * strip)] = jnp.dot(
            normed, joint_ref[...], preferred_element_type=jnp.float32
        ).astype(jnp.bfloat16)
        return carry

    lax.fori_loop(0, tokens_ref.shape[0] // (2 * strip), body, 0)


def inner_kernel(joint_ref, bias_ref, out_ref):
    cells_down, cells_across, _, triple = joint_ref.shape
    model = triple // 3
    blocks = head_blocks(GROUP * model // HEADS)
    bias = [bias_ref[group] for group in range(bias_ref.shape[0])]

    def body(i, carry):
        for j in range(cells_across // 2 - 1):
            rows = joint_ref[pl.ds(2 * i + 1, 2), 2 * j + 1 : 2 * j + 3].reshape(AREA, triple)
            mixed = attend(
                rows[:, :model], rows[:, model : 2 * model], rows[:, 2 * model :], bias, blocks, None
            )
            out_ref[pl.ds(2 * i + 1, 2), 2 * j + 1 : 2 * j + 3] = mixed.reshape(2, 2, CELL, model)
        return carry

    lax.fori_loop(0, cells_down // 2 - 1, body, 0)


def outer_kernel(
    edge_ref, tokens_ref, joint_out_ref, inner_ref, up_ref, down_ref, left_ref, right_ref,
    bias_ref, first_ref, second_ref, joint_ref, merge_ref, expand_ref, shrink_ref, lateral_ref,
    features_ref, pairs_ref, mixed_ref, order_ref,
):
    cells_down, cells_across, _, triple = joint_out_ref.shape
    model = triple // 3
    width = cells_across * SUB
    strip = SUB * width
    order_ref[...] = strip_order(width)
    blocks = head_blocks(GROUP * model // HEADS)
    groups = bias_ref.shape[0]
    ends = [
        jnp.dot(order_ref[...], ref[...], preferred_element_type=jnp.float32)
        for ref in (up_ref, down_ref)
    ]
    ends += [ref[...].astype(jnp.float32) for ref in (left_ref, right_ref)]
    halo = norm_rows(jnp.concatenate(ends, axis=0), first_ref[...])
    halo = jnp.dot(halo, joint_ref[:, model:], preferred_element_type=jnp.float32)
    halo = halo.astype(jnp.bfloat16)
    tall = left_ref.shape[0]
    pairs_ref[0, 1:-1] = halo[:strip].reshape(cells_across, CELL, 2 * model)
    pairs_ref[cells_down + 1, 1:-1] = halo[strip : 2 * strip].reshape(cells_across, CELL, 2 * model)
    pairs_ref[:, 0] = halo[2 * strip : 2 * strip + tall].reshape(-1, CELL, 2 * model)
    pairs_ref[:, cells_across + 1] = halo[2 * strip + tall :].reshape(-1, CELL, 2 * model)
    for c in (0, 1, cells_across - 2, cells_across - 1):
        pairs_ref[1:-1, c + 1] = joint_out_ref[:, c, :, model:]
    for r in (0, 1, cells_down - 2, cells_down - 1):
        pairs_ref[r + 1, 1:-1] = joint_out_ref[r, :, :, model:]
    mixed_ref[1:-1, 1:-1] = inner_ref[1:-1, 1:-1]
    key_cell = lax.broadcasted_iota(jnp.int32, (1, GROUP * AREA), 1) // CELL % (2 * 2)
    key_down, key_across = key_cell // 2, key_cell % 2

    def window(i, j, side_down, side_across):
        pairs = pairs_ref[pl.ds(2 * i, 2), pl.ds(2 * j, 2)].reshape(AREA, 2 * model)
        hidden = jnp.zeros((1, GROUP * AREA), jnp.bool_)
        down = [0, 1] if side_down is None else [1 - side_down]
        across = [0, 1] if side_across is None else [1 - side_across]
        if side_down is not None:
            hidden = hidden | ((key_down == side_down) & (edge_ref[side_down] > 0))
        if side_across is not None:
            hidden = hidden | ((key_across == side_across) & (edge_ref[2 + side_across] > 0))
        key_mask = jnp.where(hidden, BLOCKED, 0.0)
        queries, bias_rows = [], []
        for d in down:
            for a in across:
                queries.append(joint_out_ref[2 * i + d - 1, 2 * j + a - 1, :, :model])
                bias_rows.append((2 * d + a) * CELL)
        bias = [
            jnp.concatenate([bias_ref[g, b : b + CELL] for b in bias_rows], axis=0)
            for g in range(groups)
        ]
        mixed = attend(
            jnp.concatenate(queries, axis=0), pairs[:, :model], pairs[:, model:], bias, blocks, key_mask
        )
        place = 0
        for d in down:
            for a in across:
                mixed_ref[2 * i + d - 1, 2 * j + a - 1] = mixed[place : place + CELL]
                place += CELL

    last_down, last_across = cells_down // 2, cells_across // 2
    for side, i in enumerate((0, last_down)):
        for other, j in enumerate((0, last_across)):
            window(i, j, side, other)

    def along(j, carry):
        window(0, j, 0, None)
        window(last_down, j, 1, None)
        return carry

    def beside(i, carry):
        window(i, 0, None, 0)
        window(i, last_across, None, 1)
        return carry

    lax.fori_loop(1, last_across, along, 0)
    lax.fori_loop(1, last_down, beside, 0)

    def body(step, carry):
        tokens = []
        for part in range(2):
            begin = pl.multiple_of((2 * step + part) * strip, strip)
            tokens.append(
                jnp.dot(
                    order_ref[...],
                    tokens_ref[pl.ds(begin, strip)],
                    preferred_element_type=jnp.float32,
                )
            )
        mixed = mixed_ref[pl.ds(2 * step, 2)].reshape(2 * strip, model)
        residual = jnp.concatenate(tokens, axis=0) + jnp.dot(
            mixed, merge_ref[...], preferred_element_type=jnp.float32
        )
        normed = norm_rows(residual, second_ref[...])
        hidden = gelu_value(jnp.dot(normed, expand_ref[...], preferred_element_type=jnp.float32))
        block_out = (
            residual
            + jnp.dot(
                hidden.astype(jnp.bfloat16), shrink_ref[...], preferred_element_type=jnp.float32
            )
        ).astype(jnp.bfloat16)
        features = jnp.dot(block_out, lateral_ref[...], preferred_element_type=jnp.float32)
        features = features.astype(jnp.bfloat16)
        for part in range(2):
            begin = pl.multiple_of((2 * step + part) * strip, strip)
            features_ref[pl.ds(begin, strip)] = lax.dot_general(
                order_ref[...],
                features[part * strip : (part + 1) * strip],
                TN,
                preferred_element_type=jnp.float32,
            ).astype(jnp.bfloat16)
        return carry

    lax.fori_loop(0, cells_down // 2, body, 0)


def params(mebibytes):
    return pltpu.CompilerParams(vmem_limit_bytes=mebibytes * 2**20)


def joint_rows(tokens, gain, weight, relative, width):
    strip = SUB * width
    return pl.pallas_call(
        joint_kernel,
        out_shape=(
            jax.ShapeDtypeStruct((tokens.shape[0], weight.shape[1]), jnp.bfloat16),
            jax.ShapeDtypeStruct((HEADS // GROUP, AREA, GROUP * AREA), jnp.float32),
        ),
        in_specs=[VMEM] * 4,
        out_specs=(VMEM, VMEM),
        scratch_shapes=[pltpu.VMEM((strip, strip), jnp.bfloat16)],
        compiler_params=params(24),
        name="joint_rows",
    )(tokens, gain, weight, relative)


def inner_windows(joint, bias):
    return pl.pallas_call(
        inner_kernel,
        out_shape=jax.ShapeDtypeStruct(joint.shape[:3] + (joint.shape[3] // 3,), jnp.bfloat16),
        in_specs=[VMEM] * 2,
        out_specs=VMEM,
        compiler_params=params(24),
        name="inner_windows",
    )(joint, bias)


def outer_windows(edges, tokens, joint, inner, halos, bias, gains, weights):
    cells_down, cells_across, _, triple = joint.shape
    strip = SUB * SUB * cells_across
    return pl.pallas_call(
        outer_kernel,
        out_shape=jax.ShapeDtypeStruct((tokens.shape[0], weights[-1].shape[1]), jnp.bfloat16),
        in_specs=[SMEM] + [VMEM] * 15,
        out_specs=VMEM,
        scratch_shapes=[
            pltpu.VMEM((cells_down + 2, cells_across + 2, CELL, triple * 2 // 3), jnp.bfloat16),
            pltpu.VMEM((cells_down, cells_across, CELL, triple // 3), jnp.bfloat16),
            pltpu.VMEM((strip, strip), jnp.bfloat16),
        ],
        compiler_params=params(40),
        name="outer_windows",
    )(edges, tokens, joint, inner, *halos, bias, *gains, *weights)


BOX_OWN = 8


def shift(x, axis, step):
    size = lax.axis_size(axis)
    pairs = [(i, i + step) for i in range(size) if 0 <= i + step < size]
    return lax.ppermute(x, axis, pairs)


def shards(
    tokens, first_gain, second_gain, joint_weight, merge_weight, expand_weight, shrink_weight,
    relative_bias, lateral_weight, conv_weight, mask_weight, box_geometry, box_counts, box_owner,
    soft_target,
):
    tile_rows, tile_cols, model = tokens.shape
    cells_down, cells_across = tile_rows // SUB, tile_cols // SUB
    rows_size, cols_size = lax.axis_size("row"), lax.axis_size("col")
    row_index, col_index = lax.axis_index("row"), lax.axis_index("col")
    up = shift(tokens[-SUB:], "row", 1)
    down = shift(tokens[:SUB], "row", -1)
    flat = tokens.reshape(-1, model)
    joint, bias = joint_rows(
        flat, first_gain[None], joint_weight, relative_bias.reshape(-1, AREA), tile_cols
    )
    joint = joint.reshape(cells_down, cells_across, CELL, -1)
    east = jnp.concatenate([up[:, -SUB:], tokens[:, -SUB:], down[:, -SUB:]], axis=0)
    west = jnp.concatenate([up[:, :SUB], tokens[:, :SUB], down[:, :SUB]], axis=0)
    left = shift(east.reshape(-1, model), "col", 1)
    right = shift(west.reshape(-1, model), "col", -1)
    inner = inner_windows(joint, bias)
    edges = jnp.stack(
        [row_index == 0, row_index == rows_size - 1, col_index == 0, col_index == cols_size - 1]
    ).astype(jnp.int32)
    features = outer_windows(
        edges, flat, joint, inner, (up.reshape(-1, model), down.reshape(-1, model), left, right),
        bias, (first_gain[None], second_gain[None]),
        (joint_weight, merge_weight, expand_weight, shrink_weight, lateral_weight),
    )
    features = features.reshape(tile_rows, tile_cols, -1)
    geometry = box_geometry.reshape(-1, 4)
    capacity = geometry.shape[0]
    count = box_counts.reshape(1)
    row8 = lambda *rows: jnp.concatenate(
        [jnp.stack(rows), jnp.zeros((8 - len(rows),) + rows[0].shape, rows[0].dtype)], axis=0
    )
    logits, slope = mask_forward(
        features, geometry, count, conv_weight, row8(mask_weight), rows=2
    )
    soft = soft_target.reshape(capacity, CROP, CROP).transpose(1, 2, 0).astype(jnp.float32)
    feature_grad = mask_backward(
        logits, soft.reshape(CROP, -1), slope, geometry, count, conv_weight,
        row8(mask_weight, mask_weight), (tile_rows, tile_cols), rows=2,
    )
    local = logits.reshape(CROP * CROP, capacity)
    slots = jnp.arange(capacity, dtype=jnp.int32)
    valid = slots < count
    owner = box_owner.reshape(-1)
    rank = jnp.sum((owner[:, None] == owner[None, :]) & (slots[None, :] < slots[:, None]), axis=1)
    each = max(1, capacity // rows_size)
    send = rows_size * each
    routing = (
        (owner * each + rank)[None, :] == jnp.arange(send, dtype=jnp.int32)[:, None]
    ) & valid[None, :]
    packed = jnp.concatenate(
        [local, jnp.ones((1, capacity), jnp.float32)], axis=0
    )
    outgoing = lax.dot_general(
        routing.astype(jnp.float32), packed, NT, precision=HIGHEST
    ).reshape(rows_size, each, -1)
    arriving = lax.all_to_all(outgoing, "row", split_axis=0, concat_axis=0, tiled=True)
    arriving = arriving.reshape(send, -1)
    present = arriving[:, -1] > 0.5
    position = jnp.cumsum(present.astype(jnp.int32)) - 1
    picker = (
        position[None, :] == jnp.arange(BOX_OWN, dtype=jnp.int32)[:, None]
    ) & present[None, :]
    mask_logits = jnp.dot(picker.astype(jnp.float32), arriving[:, :-1], precision=HIGHEST)
    return features, feature_grad, mask_logits.reshape(1, 1, BOX_OWN, -1)


def solution(mesh):
    tile = P("row", "col", None)
    placed = (tile,) + (P(),) * 10 + (
        P("row", "col", None, None), P("row", "col"), tile, P("row", "col", None, None),
    )
    return jax.shard_map(
        shards,
        mesh=mesh,
        in_specs=placed,
        out_specs=(tile, tile, P("row", "col", None, None)),
        check_vma=False,
    )
```

profile of v0, /device:TPU:4, one launch (start us, length us, event | category | flops | bytes accessed | tf_op | source)
XLA Modules:
  0.0 119.8 jit_solution(3844943576131298484)
XLA Ops:
  0.6 0.0 copy-start.3
  0.6 0.0 copy-start.4
  0.7 1.1 fusion.15
  1.7 3.4 %collective-permute-start = (bf16[4,32,384]{2,1,0:T(8,128)(2,1)S(1)}, bf16[4,32,384]{2,1,0:T(8,128)(2,1)S(1)}, u32[]{:S(2)}, u32[]{:S(2)}) collective-permute-start(bf16[4,32,384]{2,1,0:T(8,128)(2,1)S(1)} %get-tuple-element.16), channel_id=1, source_target_pairs={{0,4},{4,8},{8,12},{12,16},{16,20},{20,24},{24,28},{1,5},{5,9},{9,... | collective-permute-start | bytes 294920 | tf_op jit(solution)/shard_map/ppermute | solution.py:559
  5.1 1.3 %collective-permute-start.1 = (bf16[4,32,384]{2,1,0:T(8,128)(2,1)S(1)}, bf16[4,32,384]{2,1,0:T(8,128)(2,1)S(1)}, u32[]{:S(2)}, u32[]{:S(2)}) collective-permute-start(bf16[4,32,384]{2,1,0:T(8,128)(2,1)S(1)} %get-tuple-element.15), channel_id=1, source_target_pairs={{4,0},{8,4},{12,8},{16,12},{20,16},{24,20},{28,24},{5,1},{9,5},{13... | collective-permute-start | bytes 294920 | tf_op jit(solution)/shard_map/ppermute | solution.py:559
  6.4 1.1 fusion.14
  7.6 0.7 stack.25
  8.2 0.9 convert_reduce_fusion
  9.1 0.1 pad.4.clone
  9.2 0.1 maximum_maximum_fusion
  9.3 0.7 multiply_add_fusion
  10.6 1.1 collective-permute-done.1
  11.7 0.0 collective-permute-done
  11.7 0.1 pad_maximum_fusion
  11.8 1.9 %collective-permute-start.2 = (bf16[160,384]{1,0:T(8,128)(2,1)S(1)}, bf16[160,384]{1,0:T(8,128)(2,1)S(1)}, u32[]{:S(2)}, u32[]{:S(2)}) collective-permute-start(bf16[160,384]{1,0:T(8,128)(2,1)S(1)} %reshape.108), channel_id=1, source_target_pairs={{0,1},{1,2},{2,3},{4,5},{5,6},{6,7},{8,9},{9,10},{10,11},{12,13},{... | collective-permute-start | bytes 368648 | tf_op jit(solution)/shard_map/ppermute | solution.py:559
  13.8 0.1 pad_maximum_fusion.1
  13.9 3.6 %collective-permute-start.3 = (bf16[160,384]{1,0:T(8,128)(2,1)S(1)}, bf16[160,384]{1,0:T(8,128)(2,1)S(1)}, u32[]{:S(2)}, u32[]{:S(2)}) collective-permute-start(bf16[160,384]{1,0:T(8,128)(2,1)S(1)} %reshape.109), channel_id=1, source_target_pairs={{1,0},{2,1},{3,2},{5,4},{6,5},{7,6},{9,8},{10,9},{11,10},{13,12},{... | collective-permute-start | bytes 368648 | tf_op jit(solution)/shard_map/ppermute | solution.py:559
  17.6 0.7 broadcast_in_dim.6.gain_ref.first_ref
  18.3 0.7 broadcast_in_dim.7.second_ref
  19.0 0.8 copy.35.geom_ref.geomv_ref
  19.7 0.0 copy-done.3
  19.7 1.0 copy-done.8
  20.7 4.4 %joint_rows.1 = (bf16[1024,1152]{1,0:T(8,128)(2,1)S(1)}, f32[3,64,256]{2,1,0:T(8,128)S(1)}) custom-call(bf16[1024,384]{1,0:T(8,128)(2,1)S(1)} %bitcast.27, f32[1,384]{1,0:T(1,128)S(1)} %broadcast_in_dim.6.gain_ref.first_ref, bf16[384,1152]{1,0:T(8,128)(2,1)S(1)} %copy-done.4, f32[768,64]{1,0:T(8,128)S(1)} %bitcast.31), custom_call_target="tpu_custom_call" | custom-call | tf_op jit(solution)/shard_map/joint_rows/pallas_call | solution.py:510
  25.1 2.1 %inner_windows.1.inner_ref = bf16[8,8,16,384]{3,2,1,0:T(8,128)(2,1)S(1)} custom-call(bf16[8,8,16,1152]{3,2,1,0:T(8,128)(2,1)S(1)} %bitcast.25, f32[3,64,256]{2,1,0:T(8,128)S(1)} %get-tuple-element.8.bias_ref), custom_call_target="tpu_custom_call" | custom-call | tf_op jit(solution)/shard_map/inner_windows/pallas_call | solution.py:525
  27.3 0.1 add_convert_fusion.edge_ref
  27.4 0.0 collective-permute-done.2.left_ref
  27.4 0.0 collective-permute-done.3.right_ref
  27.4 0.0 slice-start.1
  27.4 14.7 %outer_windows.1 = bf16[1024,256]{1,0:T(8,128)(2,1)} custom-call(s32[4]{0:T(128)S(1)} %add_convert_fusion.edge_ref, bf16[1024,384]{1,0:T(8,128)(2,1)S(1)} %bitcast.28, bf16[8,8,16,1152]{3,2,1,0:T(8,128)(2,1)S(1)} %bitcast.26, bf16[8,8,16,384]{3,2,1,0:T(8,128)(2,1)S(1)} %inner_windows.1.inner_ref, bf16[128,384]{1,0:T(8,128)(2,1)S(1)} %bitcast.32, ...), custom_call_target="tpu_custom_call" | custom-call | tf_op jit(solution)/shard_map/outer_windows/pallas_call | solution.py:538
  42.2 0.0 slice-done
  42.2 1.0 copy-done.5
  43.2 31.6 %mask_forward.1 = (f32[14,224]{1,0:T(8,128)S(1)}, bf16[4,14,224,256]{3,2,1,0:T(8,128)(2,1)S(1)}) custom-call(s32[16,4]{1,0:T(8,128)S(1)} %copy.35.geom_ref.geomv_ref, s32[1]{0:T(128)} %bitcast.20.count_ref, s32[16,4]{1,0:T(8,128)S(1)} %copy.35.geom_ref.geomv_ref, bf16[32,32,256]{2,1,0:T(8,128)(2,1)S(1)} %bitcast.30, bf16[4,2304,256]{2,1,0:T(8,128)(2,1)S(1)} %bitcast.24, ...), custom_call_target="tpu_custom_call" | custom-call | tf_op jit(solution)/shard_map/mask_forward/pallas_call | solution.py:222
  74.8 2.7 %copy-done.1 = bf16[4,14,224,256]{3,2,1,0:T(8,128)(2,1)} copy-done((bf16[4,14,224,256]{3,2,1,0:T(8,128)(2,1)}, bf16[4,14,224,256]{3,2,1,0:T(8,128)(2,1)S(1)}, u32[]{:S(2)}) %copy-start.1) | copy-done | bytes 6422552
  77.5 0.1 reshape.116
  77.6 0.2 fusion
  77.7 0.7 reshape.117
  78.4 5.9 %all-to-all-start = ((f32[8,2,197]{2,1,0:T(2,128)}), f32[8,2,197]{2,1,0:T(2,128)S(1)}, u32[]{:S(2)}, u32[]{:S(2)}) async-start(f32[8,2,197]{2,1,0:T(2,128)} %reshape.117), calls=%async_computation | async-start | bytes 32768 | tf_op jit(solution)/shard_map/all_to_all | solution.py:622
  84.4 0.1 reshape.124
  84.5 0.2 copy.34
  84.6 0.1 reshape.121.soft_ref
  84.7 0.0 copy-start
  84.7 2.3 %copy-done = bf16[4,2304,256]{2,1,0:T(8,128)(2,1)S(1)} copy-done((bf16[4,2304,256]{2,1,0:T(8,128)(2,1)S(1)}, bf16[4,2304,256]{2,1,0:T(8,128)(2,1)}, u32[]{:S(2)}) %copy-start) | copy-done | bytes 4718616
  87.1 2.8 %copy-done.2 = bf16[4,14,224,256]{3,2,1,0:T(8,128)(2,1)S(1)} copy-done((bf16[4,14,224,256]{3,2,1,0:T(8,128)(2,1)S(1)}, bf16[4,14,224,256]{3,2,1,0:T(8,128)(2,1)}, u32[]{:S(2)}) %copy-start.2) | copy-done | bytes 6422552
  89.9 28.8 %mask_backward.1 = f32[32,32,256]{2,1,0:T(8,128)} custom-call(s32[16,4]{1,0:T(8,128)S(1)} %copy.35.geom_ref.geomv_ref, s32[1]{0:T(128)} %bitcast.21.count_ref, f32[14,224]{1,0:T(8,128)S(1)} %get-tuple-element.9.logits_ref, f32[14,224]{1,0:T(8,128)S(1)} %reshape.121.soft_ref, bf16[4,14,224,256]{3,2,1,0:T(8,128)(2,1)S(1)} %copy-done.2, ...), custom_call_target="tpu_custom_call" | custom-call | tf_op jit(solution)/shard_map/mask_backward/pallas_call | solution.py:245
  118.7 0.0 all-to-all-done
  118.7 0.2 fusion.13
  118.9 0.1 add_reduce_fusion
  119.0 0.7 convolution_bitcast_fusion
  (27 shorter events, 0.2 us)
Async XLA Ops:
  0.6 19.1 %copy-start.3 = (bf16[32,32,384]{2,1,0:T(8,128)(2,1)S(1)}, bf16[32,32,384]{2,1,0:T(8,128)(2,1)}, u32[]{:S(2)}) copy-start(bf16[32,32,384]{2,1,0:T(8,128)(2,1)} %param.15) | copy-start | bytes 2359300
  0.6 19.1 %copy-start.4 = (bf16[384,1152]{1,0:T(8,128)(2,1)S(1)}, bf16[384,1152]{1,0:T(8,128)(2,1)}, u32[]{:S(2)}) copy-start(bf16[384,1152]{1,0:T(8,128)(2,1)} %joint_ref.3) | copy-start | bytes 2654212
  1.7 9.9 %collective-permute-start = (bf16[4,32,384]{2,1,0:T(8,128)(2,1)S(1)}, bf16[4,32,384]{2,1,0:T(8,128)(2,1)S(1)}, u32[]{:S(2)}, u32[]{:S(2)}) collective-permute-start(bf16[4,32,384]{2,1,0:T(8,128)(2,1)S(1)} %get-tuple-element.16), channel_id=1, source_target_pairs={{0,4},{4,8},{8,12},{12,16},{16,20},{20,24},{24,28},{1,5},{5,9},{9,... | collective-permute-start | bytes 294920 | tf_op jit(solution)/shard_map/ppermute | solution.py:559
  5.1 6.5 %collective-permute-start.1 = (bf16[4,32,384]{2,1,0:T(8,128)(2,1)S(1)}, bf16[4,32,384]{2,1,0:T(8,128)(2,1)S(1)}, u32[]{:S(2)}, u32[]{:S(2)}) collective-permute-start(bf16[4,32,384]{2,1,0:T(8,128)(2,1)S(1)} %get-tuple-element.15), channel_id=1, source_target_pairs={{4,0},{8,4},{12,8},{16,12},{20,16},{24,20},{28,24},{5,1},{9,5},{13... | collective-permute-start | bytes 294920 | tf_op jit(solution)/shard_map/ppermute | solution.py:559
  11.8 15.5 %collective-permute-start.2 = (bf16[160,384]{1,0:T(8,128)(2,1)S(1)}, bf16[160,384]{1,0:T(8,128)(2,1)S(1)}, u32[]{:S(2)}, u32[]{:S(2)}) collective-permute-start(bf16[160,384]{1,0:T(8,128)(2,1)S(1)} %reshape.108), channel_id=1, source_target_pairs={{0,1},{1,2},{2,3},{4,5},{5,6},{6,7},{8,9},{9,10},{10,11},{12,13},{... | collective-permute-start | bytes 368648 | tf_op jit(solution)/shard_map/ppermute | solution.py:559
  13.9 13.5 %collective-permute-start.3 = (bf16[160,384]{1,0:T(8,128)(2,1)S(1)}, bf16[160,384]{1,0:T(8,128)(2,1)S(1)}, u32[]{:S(2)}, u32[]{:S(2)}) collective-permute-start(bf16[160,384]{1,0:T(8,128)(2,1)S(1)} %reshape.109), channel_id=1, source_target_pairs={{1,0},{2,1},{3,2},{5,4},{6,5},{7,6},{9,8},{10,9},{11,10},{13,12},{... | collective-permute-start | bytes 368648 | tf_op jit(solution)/shard_map/ppermute | solution.py:559
  19.7 1.0 copy-start.8
  20.7 6.7 %copy-start.6 = (bf16[384,1536]{1,0:T(8,128)(2,1)S(1)}, bf16[384,1536]{1,0:T(8,128)(2,1)}, u32[]{:S(2)}) copy-start(bf16[384,1536]{1,0:T(8,128)(2,1)} %expand_ref.1) | copy-start | bytes 3538948
  20.7 6.7 %copy-start.7 = (bf16[1536,384]{1,0:T(8,128)(2,1)S(1)}, bf16[1536,384]{1,0:T(8,128)(2,1)}, u32[]{:S(2)}) copy-start(bf16[1536,384]{1,0:T(8,128)(2,1)} %shrink_ref.1) | copy-start | bytes 3538948
  20.7 6.7 %copy-start.9 = (bf16[384,384]{1,0:T(8,128)(2,1)S(1)}, bf16[384,384]{1,0:T(8,128)(2,1)}, u32[]{:S(2)}) copy-start(bf16[384,384]{1,0:T(8,128)(2,1)} %merge_ref.1) | copy-start | bytes 884740
  20.7 6.7 %copy-start.10 = (bf16[384,256]{1,0:T(8,128)(2,1)S(1)}, bf16[384,256]{1,0:T(8,128)(2,1)}, u32[]{:S(2)}) copy-start(bf16[384,256]{1,0:T(8,128)(2,1)} %lateral_ref.1) | copy-start | bytes 589828
  27.4 14.8 %slice-start = ((s8[4718592]{0:T(1024)(128)(4,1)}), s8[4194304]{0:T(1024)(128)(4,1)S(1)}, s32[]{:S(2)}) async-start(s8[4718592]{0:T(1024)(128)(4,1)} %bitcast.23), calls=%async_computation.1 | async-start | bytes 8388608
  27.4 14.8 %slice-start.1 = ((s8[4718592]{0:T(1024)(128)(4,1)}), s8[524288]{0:T(1024)(128)(4,1)S(1)}, s32[]{:S(2)}) async-start(s8[4718592]{0:T(1024)(128)(4,1)} %bitcast.23), calls=%async_computation.2 | async-start | bytes 1048576
  42.2 1.0 copy-start.5
  43.2 41.1 %copy-start.11 = (bf16[1,1,16,196]{3,2,1,0:T(8,128)(2,1)S(1)}, bf16[1,1,16,196]{3,2,1,0:T(8,128)(2,1)}, u32[]{:S(2)}) copy-start(bf16[1,1,16,196]{3,2,1,0:T(8,128)(2,1)} %param.29) | copy-start | bytes 18820
  74.8 2.7 %copy-start.1 = (bf16[4,14,224,256]{3,2,1,0:T(8,128)(2,1)}, bf16[4,14,224,256]{3,2,1,0:T(8,128)(2,1)S(1)}, u32[]{:S(2)}) copy-start(bf16[4,14,224,256]{3,2,1,0:T(8,128)(2,1)S(1)} %get-tuple-element.10.slope_ref) | copy-start | bytes 19267588
  78.4 40.2 %all-to-all-start = ((f32[8,2,197]{2,1,0:T(2,128)}), f32[8,2,197]{2,1,0:T(2,128)S(1)}, u32[]{:S(2)}, u32[]{:S(2)}) async-start(f32[8,2,197]{2,1,0:T(2,128)} %reshape.117), calls=%async_computation | async-start | bytes 32768 | tf_op jit(solution)/shard_map/all_to_all | solution.py:622
  84.7 2.3 %copy-start = (bf16[4,2304,256]{2,1,0:T(8,128)(2,1)S(1)}, bf16[4,2304,256]{2,1,0:T(8,128)(2,1)}, u32[]{:S(2)}) copy-start(bf16[4,2304,256]{2,1,0:T(8,128)(2,1)} %weight_ref.3) | copy-start | bytes 14155780
  87.1 2.8 %copy-start.2 = (bf16[4,14,224,256]{3,2,1,0:T(8,128)(2,1)S(1)}, bf16[4,14,224,256]{3,2,1,0:T(8,128)(2,1)}, u32[]{:S(2)}) copy-start(bf16[4,14,224,256]{3,2,1,0:T(8,128)(2,1)} %copy-done.1) | copy-start | bytes 19267588
where the time goes:
time: 121 us; the launch traced here: 120 us
  Pallas kernels  81.6 us (67%)
  local copies, waits for them, and re-layouts  16.2 us (13%)
  starting transfers between devices  16.2 us (13%)
  other arithmetic  2.26 us (2%)
  between operations  1.53 us (1%)
    pallas_call x1, Pallas kernels, mask_forward(): pl.pallas_call(functools.partial(mask_forward_kernel, rows), out_shape=(j...  31.6 us
    pallas_call x1, Pallas kernels, mask_backward(): pl.pallas_call(functools.partial(mask_backward_kernel, rows), out_shape=j...  28.8 us
    pallas_call x1, Pallas kernels, outer_windows(): pl.pallas_call(outer_kernel, out_shape=jax.ShapeDtypeStruct((tokens.shape...  14.7 us
    ppermute x4, starting transfers between devices, shift(): return lax.ppermute(x, axis, pairs)  10.3 us
    unnamed x28, local copies, waits for them, and re-layouts  9.92 us
    all_to_all x1, starting transfers between devices, shards(): lax.all_to_all(outgoing, 'row', split_axis=0, concat_axis=0, tiled=True)  5.92 us
    pallas_call x1, Pallas kernels, joint_rows(): pl.pallas_call(joint_kernel, out_shape=(jax.ShapeDtypeStruct((tokens.shap...  4.4 us
  transfers between devices with their start and end apart: 5, of which 1 were waited for; matrix products, arithmetic and copies ran while one was open for 5% of the time, Pallas kernels for 29%

commit v1 on v0

v1 whole, which is shorter than its diff:
```python
import functools
import jax
import jax.numpy as jnp
from jax import lax
from jax.experimental import pallas as pl
from jax.experimental.pallas import tpu as pltpu
from jax.sharding import PartitionSpec as P

CROP = 14
ROWS = 2
PAD = CROP + 2
GELU_A = 0.7978845608028654
GELU_B = 0.044715
loss_scale = 128.0
NT = (((1,), (1,)), ((), ()))
TN = (((0,), (0,)), ((), ()))
VMEM = pl.BlockSpec(memory_space=pltpu.VMEM)
SMEM = pl.BlockSpec(memory_space=pltpu.SMEM)


def gelu_value(x):
    inner = x * (GELU_A + (GELU_A * GELU_B) * (x * x))
    return x * (0.5 + 0.5 * jnp.tanh(inner))


def gelu_parts(x):
    square = x * x
    inner = x * (GELU_A + (GELU_A * GELU_B) * square)
    half = 0.5 + 0.5 * jnp.tanh(inner)
    value = x * half
    slope = half + value * (1.0 - half) * (2.0 * GELU_A + (6.0 * GELU_A * GELU_B) * square)
    return value, slope


def clear_border(ref):
    blank = jnp.zeros((PAD,) + ref.shape[2:], ref.dtype)
    ref[0] = blank
    ref[PAD - 1] = blank
    for row in range(1, PAD - 1):
        ref[row, 0] = blank[0]
        ref[row, PAD - 1] = blank[0]


def taps_of(ref, begin, end, flip):
    boxes, channels = ref.shape[2:]
    pieces = []
    for s in range(3):
        for t in range(3):
            s0, t0 = (2 - s, 2 - t) if flip else (s, t)
            part = ref[begin + s0 : end + s0, t0 : t0 + CROP]
            pieces.append(part.reshape((end - begin) * CROP * boxes, channels))
    return pieces


def mask_kernel(
    geom_ref, count_ref, features_ref, weight_ref, mask_ref, soft_ref,
    logits_ref, grad_ref,
    a_ref, b_ref, slope_ref, strip_ref, spread_ref, pick_ref, place_ref, before_ref,
):
    _, boxes, tile_cols, channels = strip_ref.shape
    layers = weight_ref.shape[0]
    lanes = CROP * boxes
    count = count_ref[0, 0]
    top = [geom_ref[0, 0, n, 0] for n in range(boxes)]
    left = [geom_ref[0, 0, n, 1] for n in range(boxes)]
    tall = [jnp.where(n < count, geom_ref[0, 0, n, 2], 0) for n in range(boxes)]
    broad = [geom_ref[0, 0, n, 3] for n in range(boxes)]
    clear_border(a_ref)
    clear_border(b_ref)
    lane = lax.broadcasted_iota(jnp.int32, (boxes, boxes * tile_cols), 1)
    sub = lax.broadcasted_iota(jnp.int32, (boxes, boxes * tile_cols), 0)
    start = jnp.zeros((boxes, boxes * tile_cols), jnp.int32)
    width = jnp.zeros((boxes, boxes * tile_cols), jnp.int32)
    for n in range(boxes):
        start = jnp.where(sub == n, left[n], start)
        width = jnp.where(sub == n, broad[n], width)
    away = jnp.where(lane // tile_cols == sub, lane % tile_cols - start, -1)
    away = jnp.where(away < width, away, -1)
    for v in range(CROP):
        pick_ref[v * boxes : (v + 1) * boxes, :] = (away == v).astype(jnp.bfloat16)
    for n in range(boxes):
        rows = features_ref[pl.ds(top[n], CROP)]
        for u in range(CROP):
            strip_ref[u, n] = jnp.where(u < tall[n], rows[u], jnp.zeros_like(rows[u]))
    for u in range(CROP):
        crop = jnp.dot(
            pick_ref[...], strip_ref[u].reshape(-1, channels), preferred_element_type=jnp.float32
        )
        a_ref[u + 1, 1 : 1 + CROP] = crop.astype(jnp.bfloat16).reshape(CROP, boxes, channels)

    lane = lax.broadcasted_iota(jnp.int32, (1, lanes), 1)
    box, col = lane % boxes, lane // boxes
    height = jnp.zeros((1, lanes), jnp.int32)
    for n in range(boxes):
        height = jnp.where((box == n) & (col < broad[n]), tall[n], height)
    cell = lax.broadcasted_iota(jnp.int32, (tile_cols, lanes), 0)
    for n in range(boxes):
        place_ref[n * tile_cols : (n + 1) * tile_cols, :] = (
            (cell == col + left[n]) & (box == n) & (col < broad[n])
        ).astype(jnp.bfloat16)
    vector = jnp.broadcast_to(
        mask_ref[...].astype(jnp.float32).reshape(1, channels), (8, channels)
    ).astype(jnp.bfloat16)

    def forward(layer, source, begin, end):
        return jnp.dot(
            jnp.concatenate(taps_of(source, begin, end, False), axis=1),
            weight_ref[layer],
            preferred_element_type=jnp.float32,
        )

    def activate(layer, before, target, begin, end):
        for u in range(begin, end):
            for v in range(CROP):
                piece = slice(v * boxes, (v + 1) * boxes)
                value, slope = gelu_parts(before[u, piece])
                slope_ref[layer + 1, u, piece] = slope.astype(jnp.bfloat16)
                target[u + 1, 1 + v] = value.astype(jnp.bfloat16)

    def backward(layer, source, begin, end):
        total = None
        for tap, piece in enumerate(taps_of(source, begin, end, True)):
            part = lax.dot_general(
                piece,
                weight_ref[layer, tap * channels : (tap + 1) * channels, :],
                NT,
                preferred_element_type=jnp.float32,
            )
            total = part if total is None else total + part
        return total

    def descend(layer, before, target, begin, end):
        for u in range(begin, end):
            for v in range(CROP):
                piece = slice(v * boxes, (v + 1) * boxes)
                slope = slope_ref[layer, u, piece].astype(jnp.float32)
                target[u + 1, 1 + v] = (before[u, piece] * slope).astype(jnp.bfloat16)

    def chain(product, finish, stages):
        late = None
        for number, (layer, source, target) in enumerate(stages):
            before = before_ref.at[number % 2]
            for begin in range(0, CROP, ROWS):
                end = min(begin + ROWS, CROP)
                before[begin:end] = product(layer, source, begin, end).reshape(
                    end - begin, lanes, channels
                )
                if late is not None:
                    late()
                late = functools.partial(finish, layer, before, target, begin, end)
        late()

    def up(pair, carry):
        chain(forward, activate, [(2 * pair, a_ref, b_ref), (2 * pair + 1, b_ref, a_ref)])
        return carry

    def down(pair, carry):
        layer = layers - 1 - 2 * pair
        chain(backward, descend, [(layer, b_ref, a_ref), (layer - 1, a_ref, b_ref)])
        return carry

    slope_ref[0] = jnp.ones(slope_ref.shape[1:], slope_ref.dtype)
    lax.fori_loop(0, layers // 2, up, 0)
    for u in range(CROP):
        line = lax.dot_general(
            vector, a_ref[u + 1, 1 : 1 + CROP].reshape(lanes, channels), NT,
            preferred_element_type=jnp.float32,
        )[0:1]
        logits_ref[u : u + 1, :] = line
    grad = loss_scale * (jax.nn.sigmoid(logits_ref[...]) - soft_ref[...])
    grad = jnp.where(lax.broadcasted_iota(jnp.int32, (CROP, lanes), 0) < height, grad, 0.0)
    high = grad.astype(jnp.bfloat16).astype(jnp.float32)
    for u in range(CROP):
        pair = jnp.concatenate(
            [high[u : u + 1], (grad - high)[u : u + 1], jnp.zeros((6, lanes), jnp.float32)], axis=0
        )
        lead = lax.dot_general(
            pair.astype(jnp.bfloat16), vector, TN, preferred_element_type=jnp.float32
        )
        b_ref[u + 1, 1 : 1 + CROP] = (
            (lead * slope_ref[layers, u].astype(jnp.float32))
            .astype(jnp.bfloat16)
            .reshape(CROP, boxes, channels)
        )
    lax.fori_loop(0, layers // 2, down, 0)
    for u in range(CROP):
        spread_ref[u] = jnp.dot(
            place_ref[...],
            b_ref[u + 1, 1 : 1 + CROP].reshape(lanes, channels),
            preferred_element_type=jnp.float32,
        ).reshape(boxes, tile_cols, channels)
    grad_ref[...] = jnp.zeros_like(grad_ref)
    for n in range(boxes):
        kept = lax.broadcasted_iota(jnp.int32, (CROP, 1, 1), 0) < tall[n]
        rows = pl.ds(top[n], CROP)
        grad_ref[rows] = grad_ref[rows] + jnp.where(kept, spread_ref[:, n], 0.0)


def mask_head(features, geometry, count, weight, mask, soft):
    tile_rows, tile_cols, channels = features.shape
    boxes = geometry.shape[2]
    layers = weight.shape[0]
    lanes = CROP * boxes
    return pl.pallas_call(
        mask_kernel,
        out_shape=(
            jax.ShapeDtypeStruct((CROP, lanes), jnp.float32),
            jax.ShapeDtypeStruct((tile_rows, tile_cols, channels), jnp.float32),
        ),
        in_specs=[SMEM, SMEM, VMEM, VMEM, VMEM, VMEM],
        out_specs=(VMEM, VMEM),
        scratch_shapes=[
            pltpu.VMEM((PAD, PAD, boxes, channels), jnp.bfloat16),
            pltpu.VMEM((PAD, PAD, boxes, channels), jnp.bfloat16),
            pltpu.VMEM((layers + 1, CROP, lanes, channels), jnp.bfloat16),
            pltpu.VMEM((CROP, boxes, tile_cols, channels), jnp.bfloat16),
            pltpu.VMEM((CROP, boxes, tile_cols, channels), jnp.float32),
            pltpu.VMEM((lanes, boxes * tile_cols), jnp.bfloat16),
            pltpu.VMEM((boxes * tile_cols, lanes), jnp.bfloat16),
            pltpu.VMEM((2, CROP, lanes, channels), jnp.float32),
        ],
        compiler_params=pltpu.CompilerParams(vmem_limit_bytes=48 * 2**20),
        name="mask_head",
    )(geometry, count, features, weight, mask, soft)


HEADS = 12
WIN = 8
SUB = WIN // 2
CELL = SUB * SUB
AREA = WIN * WIN
GROUP = 4
EPSILON = 1e-05
BLOCKED = -1000000000.0
HIGHEST = lax.Precision.HIGHEST


def norm_rows(values, gain):
    centered = values - jnp.mean(values, axis=-1, keepdims=True)
    variance = jnp.mean(centered * centered, axis=-1, keepdims=True)
    return (centered * lax.rsqrt(variance + EPSILON) * gain).astype(jnp.bfloat16)


def one_hot(equal, dtype=jnp.bfloat16):
    return equal.astype(jnp.float32).astype(dtype)


def strip_order(width):
    size = SUB * width
    cell_pos = lax.broadcasted_iota(jnp.int32, (size, size), 0)
    token = lax.broadcasted_iota(jnp.int32, (size, size), 1)
    cell, row, col = cell_pos // CELL, cell_pos // SUB % SUB, cell_pos % SUB
    return one_hot(token == row * width + cell * SUB + col)


def window_order():
    place = lax.broadcasted_iota(jnp.int32, (AREA, AREA), 0)
    token = lax.broadcasted_iota(jnp.int32, (AREA, AREA), 1)
    cell, row, col = place // CELL, place // SUB % SUB, place % SUB
    return one_hot(token == (cell // 2 * SUB + row) * WIN + cell % 2 * SUB + col, jnp.float32)


def head_blocks(lanes):
    row = lax.broadcasted_iota(jnp.int32, (GROUP * AREA, lanes), 0)
    col = lax.broadcasted_iota(jnp.int32, (GROUP * AREA, lanes), 1)
    return one_hot(row // AREA == col // (lanes // GROUP))


def attend(queries, key_rows, value_rows, bias, blocks, key_mask):
    lanes = blocks.shape[1]
    scale = (lanes // GROUP) ** (-0.5)
    first = lax.broadcasted_iota(jnp.int32, (1, 2 * AREA), 1) < AREA
    mixed = []
    for group in range(len(bias)):
        cut = slice(group * lanes, (group + 1) * lanes)
        keys = jnp.concatenate([key_rows[:, cut]] * GROUP, axis=0) * blocks
        values = jnp.concatenate([value_rows[:, cut]] * GROUP, axis=0) * blocks
        scores = lax.dot_general(queries[:, cut], keys, NT, preferred_element_type=jnp.float32)
        scores = scores * scale + bias[group]
        if key_mask is not None:
            scores = scores + key_mask
        weights = []
        for pair in range(GROUP // 2):
            part = scores[:, pair * 2 * AREA : (pair + 1) * 2 * AREA]
            low = jnp.max(jnp.where(first, part, -jnp.inf), axis=-1, keepdims=True)
            high = jnp.max(jnp.where(first, -jnp.inf, part), axis=-1, keepdims=True)
            weights.append(jnp.exp(part - jnp.where(first, low, high)))
        weights = jnp.concatenate(weights, axis=1).astype(jnp.bfloat16)
        both = jnp.dot(
            weights, jnp.concatenate([values, blocks], axis=1), preferred_element_type=jnp.float32
        )
        mixed.append((both[:, :lanes] / both[:, lanes:]).astype(jnp.bfloat16))
    return jnp.concatenate(mixed, axis=1)


def joint_kernel(
    tokens_ref, gain_ref, joint_ref, relative_ref,
    out_ref, bias_ref, ordered_ref, north_ref, south_ref, west_ref, east_ref, order_ref,
):
    cells_down, cells_across, _, model = ordered_ref.shape
    strip = order_ref.shape[0]
    order_ref[...] = strip_order(strip // SUB)
    place = window_order()
    turned = lax.dot_general(
        relative_ref[...].reshape(-1, AREA), place, NT,
        precision=HIGHEST, preferred_element_type=jnp.float32,
    )
    for group in range(HEADS // GROUP):
        rows = [
            turned[(group * GROUP + h) * AREA : (group * GROUP + h + 1) * AREA]
            for h in range(GROUP)
        ]
        bias_ref[group] = jnp.dot(
            place,
            jnp.concatenate(rows, axis=1),
            precision=HIGHEST,
            preferred_element_type=jnp.float32,
        )
    gain = gain_ref[...].reshape(1, model)

    def body(step, carry):
        normed = []
        for part in range(2):
            down = 2 * step + part
            ordered = jnp.dot(
                order_ref[...],
                tokens_ref[pl.ds(down * SUB, SUB)].reshape(strip, model),
                preferred_element_type=jnp.float32,
            )
            ordered_ref[down] = ordered.astype(jnp.bfloat16).reshape(cells_across, CELL, model)
            normed.append(norm_rows(ordered, gain))
        out_ref[pl.ds(2 * step, 2)] = (
            jnp.dot(
                jnp.concatenate(normed, axis=0), joint_ref[...], preferred_element_type=jnp.float32
            )
            .astype(jnp.bfloat16)
            .reshape(2, cells_across, CELL, 3 * model)
        )
        return carry

    lax.fori_loop(0, cells_down // 2, body, 0)
    north_ref[...] = ordered_ref[0]
    south_ref[...] = ordered_ref[cells_down - 1]
    west_ref[...] = ordered_ref[:, 0]
    east_ref[...] = ordered_ref[:, cells_across - 1]


def inner_kernel(joint_ref, bias_ref, out_ref):
    cells_down, cells_across, _, triple = joint_ref.shape
    model = triple // 3
    blocks = head_blocks(GROUP * model // HEADS)
    bias = [bias_ref[group] for group in range(bias_ref.shape[0])]

    def body(i, carry):
        for j in range(cells_across // 2 - 1):
            rows = joint_ref[pl.ds(2 * i + 1, 2), 2 * j + 1 : 2 * j + 3].reshape(AREA, triple)
            mixed = attend(
                rows[:, :model], rows[:, model : 2 * model], rows[:, 2 * model :], bias, blocks, None
            )
            out_ref[pl.ds(2 * i + 1, 2), 2 * j + 1 : 2 * j + 3] = mixed.reshape(2, 2, CELL, model)
        return carry

    lax.fori_loop(0, cells_down // 2 - 1, body, 0)


def hidden_keys(down_side, down_edge, across_side, across_edge):
    cell = lax.broadcasted_iota(jnp.int32, (1, GROUP * AREA), 1) // CELL % 4
    hidden = jnp.zeros((1, GROUP * AREA), jnp.bool_)
    if down_side is not None:
        hidden = hidden | ((cell // 2 == down_side) & down_edge)
    if across_side is not None:
        hidden = hidden | ((cell % 2 == across_side) & across_edge)
    return jnp.where(hidden, BLOCKED, 0.0)


def at_end(axis, side):
    return lax.axis_index(axis) == (lax.axis_size(axis) - 1 if side else 0)


def window_bias(bias_ref, cells):
    return [
        jnp.concatenate([bias_ref[g, c * CELL : (c + 1) * CELL] for c in cells], axis=0)
        for g in range(bias_ref.shape[0])
    ]


def halo_pairs(halo, gain, joint_ref):
    model = halo.shape[-1]
    normed = norm_rows(halo.astype(jnp.float32), gain)
    return jnp.dot(normed, joint_ref[:, model:], preferred_element_type=jnp.float32).astype(
        jnp.bfloat16
    )


def ends_kernel(joint_out_ref, up_ref, down_ref, bias_ref, gain_ref, joint_ref, pairs_ref, out_ref):
    cells_down, cells_across, _, triple = joint_out_ref.shape
    model = triple // 3
    blocks = head_blocks(GROUP * model // HEADS)
    gain = gain_ref[...].reshape(1, model)
    halo = jnp.concatenate([ref[...].reshape(-1, model) for ref in (up_ref, down_ref)], axis=0)
    pairs_ref[...] = halo_pairs(halo, gain, joint_ref).reshape(2, cells_across, CELL, 2 * model)
    for side in range(2):
        row = side * (cells_down - 1)
        bias = window_bias(bias_ref, [2 - 2 * side, 3 - 2 * side])
        key_mask = hidden_keys(side, at_end("row", side), None, None)
        for j in range(1, cells_across // 2):
            cut = slice(2 * j - 1, 2 * j + 1)
            own = joint_out_ref[row, cut].reshape(2 * CELL, triple)
            other = pairs_ref[side, cut].reshape(2 * CELL, 2 * model)
            both = [own[:, model:], other] if side else [other, own[:, model:]]
            both = jnp.concatenate(both, axis=0)
            mixed = attend(own[:, :model], both[:, :model], both[:, model:], bias, blocks, key_mask)
            out_ref[side, cut] = mixed.reshape(2, CELL, model)


def sides_kernel(
    ordered_ref, joint_out_ref, inner_ref, pairs_ref, ends_ref, left_ref, right_ref,
    bias_ref, first_ref, second_ref, joint_ref, merge_ref, expand_ref, shrink_ref, lateral_ref,
    features_ref, mixed_ref, halo_ref, order_ref, residual_ref, normed_ref, wide_ref, hidden_ref,
):
    cells_down, cells_across, _, triple = joint_out_ref.shape
    model = triple // 3
    strip = cells_across * CELL
    order_ref[...] = strip_order(cells_across * SUB)
    blocks = head_blocks(GROUP * model // HEADS)
    halo = jnp.concatenate([ref[...].reshape(-1, model) for ref in (left_ref, right_ref)], axis=0)
    halo = halo_pairs(halo, first_ref[...].reshape(1, model), joint_ref)
    halo_ref[...] = halo.reshape(2, cells_down + 2, CELL, 2 * model)
    mixed_ref[1:-1, 1:-1] = inner_ref[1:-1, 1:-1]
    mixed_ref[0, 1:-1] = ends_ref[0, 1:-1]
    mixed_ref[cells_down - 1, 1:-1] = ends_ref[1, 1:-1]

    for across in range(2):
        col = across * (cells_across - 1)
        bias = window_bias(bias_ref, [1 - across, 3 - across])
        key_mask = hidden_keys(None, None, across, at_end("col", across))

        def keys(pieces):
            rows = []
            for own, other in pieces:
                rows += [own, other] if across else [other, own]
            return jnp.concatenate(rows, axis=0)

        for i in range(1, cells_down // 2):
            cells = [2 * i - 1, 2 * i]
            both = keys(
                [(joint_out_ref[c, col, :, model:], halo_ref[across, c + 1]) for c in cells]
            )
            queries = jnp.concatenate([joint_out_ref[c, col, :, :model] for c in cells], axis=0)
            mixed = attend(queries, both[:, :model], both[:, model:], bias, blocks, key_mask)
            for place, c in enumerate(cells):
                mixed_ref[c, col] = mixed[place * CELL : (place + 1) * CELL]
        for down in range(2):
            row = down * (cells_down - 1)
            near = (joint_out_ref[row, col, :, model:], halo_ref[across, row + 1])
            far = (pairs_ref[down, col], halo_ref[across, down * (cells_down + 1)])
            both = keys([near, far] if down else [far, near])
            mixed_ref[row, col] = attend(
                joint_out_ref[row, col, :, :model], both[:, :model], both[:, model:],
                window_bias(bias_ref, [3 - 2 * down - across]), blocks,
                hidden_keys(down, at_end("row", down), across, at_end("col", across)),
            )

    second = second_ref[...].reshape(1, model)
    rows = hidden_ref.shape[1]
    group = rows // strip
    steps = cells_down // group

    def merge(step):
        residual = residual_ref.at[step % 2]
        cells = slice(step * group, (step + 1) * group)
        residual[...] = jnp.dot(
            mixed_ref[cells].reshape(rows, model), merge_ref[...], preferred_element_type=jnp.float32
        )
        for part in range(0, rows, PART):
            cut = slice(part, part + PART)
            c, a = divmod(part // CELL, cells_across)
            own = ordered_ref[step * group + c, a : a + PART // CELL].reshape(PART, model)
            total = residual[cut] + own.astype(jnp.float32)
            residual[cut] = total
            normed_ref[step % 2, cut] = norm_rows(total, second)

    def expand(step):
        wide_ref[step % 2] = jnp.dot(
            normed_ref[step % 2], expand_ref[...], preferred_element_type=jnp.float32
        )

    def activate(step):
        for part in range(0, rows, CELL):
            cut = slice(part, part + CELL)
            for lane in range(0, wide_ref.shape[2], 512):
                hidden_ref[step % 2, cut, lane : lane + 512] = gelu_value(
                    wide_ref[step % 2, cut, lane : lane + 512]
                ).astype(jnp.bfloat16)

    def shrink(step):
        block_out = residual_ref[step % 2] + jnp.dot(
            hidden_ref[step % 2], shrink_ref[...], preferred_element_type=jnp.float32
        )
        features = jnp.dot(
            block_out.astype(jnp.bfloat16), lateral_ref[...], preferred_element_type=jnp.float32
        ).astype(jnp.bfloat16)
        for part in range(group):
            natural = lax.dot_general(
                order_ref[...], features[part * strip : (part + 1) * strip], TN,
                preferred_element_type=jnp.float32,
            ).astype(jnp.bfloat16)
            first = (step * group + part) * SUB
            features_ref[first : first + SUB] = natural.reshape((SUB,) + features_ref.shape[1:])

    merge(0)
    expand(0)
    for step in range(steps):
        if step + 1 < steps:
            merge(step + 1)
        activate(step)
        if step + 1 < steps:
            expand(step + 1)
        shrink(step)


PART = 64


def params(mebibytes):
    return pltpu.CompilerParams(vmem_limit_bytes=mebibytes * 2**20)


def cells_of(count_down, count_across, channels, dtype=jnp.bfloat16):
    return jax.ShapeDtypeStruct((count_down, count_across, CELL, channels), dtype)


def joint_rows(tokens, gain, weight, relative):
    tile_rows, tile_cols, model = tokens.shape
    down, across = tile_rows // SUB, tile_cols // SUB
    lone = lambda n: jax.ShapeDtypeStruct((n, CELL, model), jnp.bfloat16)
    return pl.pallas_call(
        joint_kernel,
        out_shape=(
            cells_of(down, across, weight.shape[1]),
            jax.ShapeDtypeStruct((HEADS // GROUP, AREA, GROUP * AREA), jnp.float32),
            cells_of(down, across, model),
            lone(across), lone(across), lone(down), lone(down),
        ),
        in_specs=[VMEM] * 4,
        out_specs=(VMEM,) * 7,
        scratch_shapes=[pltpu.VMEM((SUB * tile_cols, SUB * tile_cols), jnp.bfloat16)],
        compiler_params=params(20),
        cost_estimate=cost(tokens.shape[0] * tile_cols, model * weight.shape[1]),
        name="joint_rows",
    )(tokens, gain, weight, relative)


def cost(rows, weights):
    return pl.CostEstimate(flops=4 * rows * weights, bytes_accessed=4 * 2**20, transcendentals=0)


def inner_windows(joint, bias):
    return pl.pallas_call(
        inner_kernel,
        out_shape=jax.ShapeDtypeStruct(joint.shape[:3] + (joint.shape[3] // 3,), jnp.bfloat16),
        in_specs=[VMEM] * 2,
        out_specs=VMEM,
        compiler_params=params(20),
        cost_estimate=cost(joint.shape[0] * joint.shape[1] * CELL, 2**19),
        name="inner_windows",
    )(joint, bias)


def end_windows(joint, up, down, bias, gain, weight):
    _, across, _, triple = joint.shape
    return pl.pallas_call(
        ends_kernel,
        out_shape=(cells_of(2, across, triple * 2 // 3), cells_of(2, across, triple // 3)),
        in_specs=[VMEM] * 6,
        out_specs=(VMEM, VMEM),
        compiler_params=params(20),
        cost_estimate=cost(joint.shape[0] * joint.shape[1] * CELL, 2**19),
        name="end_windows",
    )(joint, up, down, bias, gain, weight)


def side_windows(ordered, joint, inner, pairs, ends, left, right, bias, gains, weights):
    down, across, _, triple = joint.shape
    model = triple // 3
    strip = CELL * across
    rows = 2 * strip
    wide = weights[2].shape[1]
    return pl.pallas_call(
        sides_kernel,
        out_shape=jax.ShapeDtypeStruct((down * SUB, across * SUB, weights[-1].shape[1]), jnp.bfloat16),
        in_specs=[VMEM] * 15,
        out_specs=VMEM,
        scratch_shapes=[
            pltpu.VMEM((down, across, CELL, model), jnp.bfloat16),
            pltpu.VMEM((2, down + 2, CELL, 2 * model), jnp.bfloat16),
            pltpu.VMEM((strip, strip), jnp.bfloat16),
            pltpu.VMEM((2, rows, model), jnp.float32),
            pltpu.VMEM((2, rows, model), jnp.bfloat16),
            pltpu.VMEM((2, rows, wide), jnp.float32),
            pltpu.VMEM((2, rows, wide), jnp.bfloat16),
        ],
        compiler_params=params(28),
        name="side_windows",
    )(ordered, joint, inner, pairs, ends, left, right, bias, *gains, *weights)


BOX_OWN = 8


def shift(x, axis, step):
    size = lax.axis_size(axis)
    pairs = [(i, i + step) for i in range(size) if 0 <= i + step < size]
    return lax.ppermute(x, axis, pairs)


def shards(
    tokens, first_gain, second_gain, joint_weight, merge_weight, expand_weight, shrink_weight,
    relative_bias, lateral_weight, conv_weight, mask_weight, box_geometry, box_counts, box_owner,
    soft_target,
):
    tile_rows, tile_cols, model = tokens.shape
    rows_size = lax.axis_size("row")
    joint, bias, ordered, north, south, west, east = joint_rows(
        tokens, first_gain, joint_weight, relative_bias
    )
    up = shift(south, "row", 1)
    down = shift(north, "row", -1)
    inner = inner_windows(joint, bias)
    left = shift(jnp.concatenate([up[-1:], east, down[-1:]], axis=0), "col", 1)
    right = shift(jnp.concatenate([up[:1], west, down[:1]], axis=0), "col", -1)
    pairs, ends = end_windows(joint, up, down, bias, first_gain, joint_weight)
    features = side_windows(
        ordered, joint, inner, pairs, ends, left, right, bias, (first_gain, second_gain),
        (joint_weight, merge_weight, expand_weight, shrink_weight, lateral_weight),
    )
    capacity = box_geometry.shape[2]
    count = box_counts.reshape(1)
    soft = soft_target.reshape(capacity, CROP, CROP).transpose(1, 2, 0).astype(jnp.float32)
    logits, feature_grad = mask_head(
        features, box_geometry, box_counts, conv_weight, mask_weight, soft.reshape(CROP, -1)
    )
    local = logits.reshape(CROP * CROP, capacity)
    slots = jnp.arange(capacity, dtype=jnp.int32)
    valid = slots < count
    owner = box_owner.reshape(-1)
    rank = jnp.sum((owner[:, None] == owner[None, :]) & (slots[None, :] < slots[:, None]), axis=1)
    each = max(1, capacity // rows_size)
    send = rows_size * each
    routing = (
        (owner * each + rank)[None, :] == jnp.arange(send, dtype=jnp.int32)[:, None]
    ) & valid[None, :]
    packed = jnp.concatenate(
        [local, jnp.ones((1, capacity), jnp.float32)], axis=0
    )
    outgoing = lax.dot_general(
        routing.astype(jnp.float32), packed, NT, precision=HIGHEST
    ).reshape(rows_size, each, -1)
    arriving = lax.all_to_all(outgoing, "row", split_axis=0, concat_axis=0, tiled=True)
    arriving = arriving.reshape(send, -1)
    present = arriving[:, -1] > 0.5
    position = jnp.cumsum(present.astype(jnp.int32)) - 1
    picker = (
        position[None, :] == jnp.arange(BOX_OWN, dtype=jnp.int32)[:, None]
    ) & present[None, :]
    mask_logits = jnp.dot(picker.astype(jnp.float32), arriving[:, :-1], precision=HIGHEST)
    return features, feature_grad, mask_logits.reshape(1, 1, BOX_OWN, -1)


def solution(mesh):
    tile = P("row", "col", None)
    placed = (tile,) + (P(),) * 10 + (
        P("row", "col", None, None), P("row", "col"), tile, P("row", "col", None, None),
    )
    return jax.shard_map(
        shards,
        mesh=mesh,
        in_specs=placed,
        out_specs=(tile, tile, P("row", "col", None, None)),
        check_vma=False,
    )
```

time: 121 us -> 101 us (0.83)
  Pallas kernels: 81.6 us -> 58.5 us
  blocking collectives: 0 us -> 13.3 us
  starting transfers between devices: 16.2 us -> 10.1 us
  local copies, waits for them, and re-layouts: 16.2 us -> 11.5 us
    pallas_call x4, Pallas kernels: 79.5 us -> 56.4 us  [the longest x1 39.2 us: mask_head(): pl.pallas_call(mask_kernel, out_shape=(jax.ShapeDtypeStruct((CROP, lanes)...]
    all_to_all x0 -> x1, blocking collectives: none -> 13.3 us  [shards(): lax.all_to_all(outgoing, 'row', split_axis=0, concat_axis=0, tiled=True)]
    all_to_all x1 -> x0, starting transfers between devices: 5.92 us -> none  [shards(): lax.all_to_all(outgoing, 'row', split_axis=0, concat_axis=0, tiled=True)]
    unnamed x28 -> x39, local copies, waits for them, and re-layouts: 9.92 us -> 6.44 us
    reshape x3, local copies, waits for them, and re-layouts: 0.37 us -> 3.46 us  [shards(): soft.reshape(CROP, -1)]
    broadcast_in_dim x3 -> x0, local copies, waits for them, and re-layouts: 1.37 us -> none  [the longest x1 0.69 us: shards(): first_gain[None]]
  transfers between devices with their start and end apart: 5 -> 4, of which waited for: 1 -> 1; matrix products, arithmetic and copies ran while one was open for 5% -> 8% of each run, Pallas kernels for 29% -> 5%
where the time goes in v1:
time: 101 us; the launch traced here: 100 us
  Pallas kernels  58.5 us (58%)
  blocking collectives  13.3 us (13%)
  local copies, waits for them, and re-layouts  11.5 us (11%)
  starting transfers between devices  10.1 us (10%)
  other arithmetic  3.06 us (3%)
  between operations  1.52 us (2%)
  waiting for transfers between devices  1.04 us (1%)
    pallas_call x1, Pallas kernels, mask_head(): pl.pallas_call(mask_kernel, out_shape=(jax.ShapeDtypeStruct((CROP, lanes)...  39.2 us
    all_to_all x1, blocking collectives, shards(): lax.all_to_all(outgoing, 'row', split_axis=0, concat_axis=0, tiled=True)  13.3 us
    ppermute x4, starting transfers between devices, shift(): return lax.ppermute(x, axis, pairs)  10.1 us
    pallas_call x1, Pallas kernels, side_windows(): pl.pallas_call(sides_kernel, out_shape=jax.ShapeDtypeStruct((down * SUB,...  9.53 us
    unnamed x39, local copies, waits for them, and re-layouts  6.44 us
    pallas_call x1, Pallas kernels, joint_rows(): pl.pallas_call(joint_kernel, out_shape=(cells_of(down, across, weight.sha...  5.09 us
    reshape x3, local copies, waits for them, and re-layouts, shards(): soft.reshape(CROP, -1)  3.46 us
    pallas_call x1, Pallas kernels, end_windows(): pl.pallas_call(ends_kernel, out_shape=(cells_of(2, across, triple * 2 //...  2.53 us
  transfers between devices with their start and end apart: 4, of which 1 were waited for; matrix products, arithmetic and copies ran while one was open for 8% of the time, Pallas kernels for 5%

profile of v1, /device:TPU:4, one launch (start us, length us, event | category | flops | bytes accessed | tf_op | source)
XLA Modules:
  0.0 100.0 jit_solution(5144506953093833546)
XLA Ops:
  0.6 0.0 copy-start.3
  0.6 1.2 %copy-done.3 = bf16[384,1152]{1,0:T(8,128)(2,1)S(1)} copy-done((bf16[384,1152]{1,0:T(8,128)(2,1)S(1)}, bf16[384,1152]{1,0:T(8,128)(2,1)}, u32[]{:S(2)}) %copy-start.3) | copy-done | bytes 884760
  1.8 0.7 copy-done.8
  2.5 1.1 %copy-done.12 = bf16[32,32,384]{2,1,0:T(8,128)(2,1)S(1)} copy-done((bf16[32,32,384]{2,1,0:T(8,128)(2,1)S(1)}, bf16[32,32,384]{2,1,0:T(8,128)(2,1)}, u32[]{:S(2)}) %copy-start.12) | copy-done | bytes 786456
  3.6 1.0 copy-done.13
  4.6 5.1 %joint_rows.1 = (bf16[8,8,16,1152]{3,2,1,0:T(8,128)(2,1)S(1)}, f32[3,64,256]{2,1,0:T(8,128)S(1)}, bf16[8,8,16,384]{3,2,1,0:T(8,128)(2,1)S(1)}, bf16[8,16,384]{2,...) custom-call(bf16[32,32,384]{2,1,0:T(8,128)(2,1)S(1)} %copy-done.12, ...), custom_call_target="tpu_custom_call" | custom-call | flops 1811939328 | bytes 4194304 | tf_op jit(solution)/shard_map/joint_rows/pallas_call | solution.py:537
  9.7 4.0 %collective-permute-start = (bf16[8,16,384]{2,1,0:T(8,128)(2,1)}, bf16[8,16,384]{2,1,0:T(8,128)(2,1)}, u32[]{:S(2)}, u32[]{:S(2)}) collective-permute-start(bf16[8,16,384]{2,1,0:T(8,128)(2,1)} %get-tuple-element.17), channel_id=1, source_target_pairs={{0,4},{4,8},{8,12},{12,16},{16,20},{20,24},{24,28},{1,5},{5,9},{9,... | collective-permute-start | bytes 294920 | tf_op jit(solution)/shard_map/ppermute | solution.py:614
  13.7 1.3 %collective-permute-start.1 = (bf16[8,16,384]{2,1,0:T(8,128)(2,1)}, bf16[8,16,384]{2,1,0:T(8,128)(2,1)}, u32[]{:S(2)}, u32[]{:S(2)}) collective-permute-start(bf16[8,16,384]{2,1,0:T(8,128)(2,1)} %get-tuple-element.18), channel_id=1, source_target_pairs={{4,0},{8,4},{12,8},{16,12},{20,16},{24,20},{28,24},{5,1},{9,5},{13... | collective-permute-start | bytes 294920 | tf_op jit(solution)/shard_map/ppermute | solution.py:614
  15.7 0.8 reshape.85
  16.4 1.7 %copy.26 = f32[14,14,16]{2,1,0:T(8,128)} copy(f32[14,14,16]{1,0,2:T(8,128)} %bitcast.11) | data formatting | bytes 25088 | tf_op jit(solution)/shard_map/reshape | solution.py:641
  18.1 1.0 reshape.82.soft_ref
  19.1 1.4 %copy.27.geom_ref = s32[1,1,16,4]{3,2,1,0:T(8,128)} copy(s32[1,1,16,4]{2,3,1,0:T(4,128)} %param.26) | data formatting | bytes 512 | tf_op args[11]
  20.5 0.9 convert_reduce_fusion
  21.4 1.2 %multiply_add_fusion = s32[16]{0:T(128)} fusion(s32[16]{0:T(128)S(1)} %convert_reduce_fusion, s32[1,1,16]{2,1,0:T(1,128)} %param.28), kind=kLoop, calls=%fused_computation.20 | loop fusion | flops 32 | bytes 192 | tf_op jit(solution)/shard_map/add | solution.py:651
  22.6 2.1 %inner_windows.1.inner_ref = bf16[8,8,16,384]{3,2,1,0:T(8,128)(2,1)S(1)} custom-call(bf16[8,8,16,1152]{3,2,1,0:T(8,128)(2,1)S(1)} %get-tuple-element.15.joint_ref.joint_out_ref, f32[3,64,256]{2,1,0:T(8,128)S(1)} %get-tuple-element.16.bias_ref), custom_call_target="tpu_custom_call" | custom-call | flops 2147483648 | bytes 4194304 | tf_op jit(solution)/shard_map/inner_windows/pallas_call | solution.py:559
  24.7 0.6 iota_compare_fusion.3
  25.3 0.0 collective-permute-done.up_ref
  25.3 0.7 fusion.14
  26.1 0.0 collective-permute-done.1.down_ref
  26.1 0.7 fusion.15
  26.8 1.9 %collective-permute-start.3 = (bf16[10,16,384]{2,1,0:T(8,128)(2,1)S(1)}, bf16[10,16,384]{2,1,0:T(8,128)(2,1)S(1)}, u32[]{:S(2)}, u32[]{:S(2)}) collective-permute-start(bf16[10,16,384]{2,1,0:T(8,128)(2,1)S(1)} %pad_maximum_fusion.1), channel_id=1, source_target_pairs={{1,0},{2,1},{3,2},{5,4},{6,5},{7,6},{9,8},{10,9},{11,10},{13,12},{... | collective-permute-start | bytes 368648 | tf_op jit(solution)/shard_map/ppermute | solution.py:614
  28.8 0.0 copy-start.1
  28.8 0.0 copy-start.2
  28.8 0.0 copy-start.5
  28.8 0.0 copy-start.6
  28.8 0.0 copy-start.10
  28.8 2.9 %collective-permute-start.2 = (bf16[10,16,384]{2,1,0:T(8,128)(2,1)S(1)}, bf16[10,16,384]{2,1,0:T(8,128)(2,1)S(1)}, u32[]{:S(2)}, u32[]{:S(2)}) collective-permute-start(bf16[10,16,384]{2,1,0:T(8,128)(2,1)S(1)} %pad_maximum_fusion), channel_id=1, source_target_pairs={{0,1},{1,2},{2,3},{4,5},{5,6},{6,7},{8,9},{9,10},{10,11},{12,13},{... | collective-permute-start | bytes 368648 | tf_op jit(solution)/shard_map/ppermute | solution.py:614
  31.7 0.0 copy-done.4
  31.7 0.0 copy-done.9
  31.7 2.5 %end_windows.1 = (bf16[2,8,16,768]{3,2,1,0:T(8,128)(2,1)S(1)}, bf16[2,8,16,384]{3,2,1,0:T(8,128)(2,1)S(1)}) custom-call(bf16[8,8,16,1152]{3,2,1,0:T(8,128)(2,1)S(1)} %get-tuple-element.15.joint_ref.joint_out_ref, bf16[8,16,384]{2,1,0:T(8,128)(2,1)} %collective-permute-done.up_ref, bf16[8,16,384]{2,1,0:T(8,128)(2,1)} %collective-permute-done.1.down_ref, ...), custom_call_target="tpu_custom_call" | custom-call | flops 2147483648 | bytes 4194304 | tf_op jit(solution)/shard_map/end_windows/pallas_call | solution.py:572
  34.3 0.0 collective-permute-done.3.right_ref
  34.3 1.0 %collective-permute-done.2.left_ref = bf16[10,16,384]{2,1,0:T(8,128)(2,1)S(1)} collective-permute-done((bf16[10,16,384]{2,1,0:T(8,128)(2,1)S(1)}, bf16[10,16,384]{2,1,0:T(8,128)(2,1)S(1)}, u32[]{:S(2)}, u32[]{:S(2)}) %collective-permute-start.2) | collective-permute-done | bytes 122912 | tf_op jit(solution)/shard_map/ppermute | solution.py:614
  35.3 0.0 copy-done.2
  35.3 0.0 copy-done.6
  35.3 0.0 slice-start.1
  35.3 0.0 copy-start.7
  35.3 0.0 copy-start.11
  35.4 9.5 %side_windows.1.features_ref = bf16[32,32,256]{2,1,0:T(8,128)(2,1)} custom-call(bf16[8,8,16,384]{3,2,1,0:T(8,128)(2,1)S(1)} %get-tuple-element.14.ordered_ref, bf16[8,8,16,1152]{3,2,1,0:T(8,128)(2,1)S(1)} %get-tuple-element.15.joint_ref.joint_out_ref, bf16[8,8,16,384]{3,2,1,0:T(8,128)(2,1)S(1)} %inner_windows.1.inner_ref, ...), custom_call_target="tpu_custom_call" | custom-call | tf_op jit(solution)/shard_map/side_windows/pallas_call | solution.py:589
  44.9 0.0 copy-start
  44.9 1.0 %copy-done = bf16[32,32,256]{2,1,0:T(8,128)(2,1)S(1)} copy-done((bf16[32,32,256]{2,1,0:T(8,128)(2,1)S(1)}, bf16[32,32,256]{2,1,0:T(8,128)(2,1)}, u32[]{:S(2)}) %copy-start) | copy-done | bytes 524312
  46.0 39.2 %mask_head.1 = (f32[14,224]{1,0:T(8,128)S(1)}, f32[32,32,256]{2,1,0:T(8,128)}) custom-call(s32[1,1,16,4]{3,2,1,0:T(8,128)S(1)} %copy-done.7, s32[1,1]{1,0:T(1,128)} %copy.28.count_ref, bf16[32,32,256]{2,1,0:T(8,128)(2,1)S(1)} %copy-done, bf16[4,2304,256]{2,1,0:T(8,128)(2,1)S(1)} %bitcast.10, bf16[256]{0:T(256)(128)(2,1)S(1)} %copy-done.11, ...), custom_call_target="tpu_custom_call" | custom-call | tf_op jit(solution)/shard_map/mask_head/pallas_call | solution.py:204
  85.2 0.1 reshape.77
  85.3 0.2 fusion
  85.5 0.1 reshape.78
  85.5 13.3 %all_to_all.5 = f32[8,2,197]{2,1,0:T(2,128)S(1)} all-to-all(f32[8,2,197]{2,1,0:T(2,128)S(1)} %reshape.78), channel_id=1, replica_groups=mesh['row'=8,'col'=4] {'row'}, dimensions={0} | all-to-all | bytes 25216 | tf_op jit(solution)/shard_map/all_to_all | solution.py:659
  98.9 0.2 fusion.13
  99.1 0.1 add_reduce_fusion
  99.2 0.7 convolution_bitcast_fusion
  (25 shorter events, 0.1 us)
Async XLA Ops:
  0.6 1.2 %copy-start.3 = (bf16[384,1152]{1,0:T(8,128)(2,1)S(1)}, bf16[384,1152]{1,0:T(8,128)(2,1)}, u32[]{:S(2)}) copy-start(bf16[384,1152]{1,0:T(8,128)(2,1)} %joint_ref.5) | copy-start | bytes 2654212
  1.8 0.7 copy-start.8
  2.5 1.1 %copy-start.12 = (bf16[32,32,384]{2,1,0:T(8,128)(2,1)S(1)}, bf16[32,32,384]{2,1,0:T(8,128)(2,1)}, u32[]{:S(2)}) copy-start(bf16[32,32,384]{2,1,0:T(8,128)(2,1)} %tokens_ref.1) | copy-start | bytes 2359300
  3.6 1.0 copy-start.13
  4.6 11.1 %copy-start.14 = (bf16[1,1,16,196]{3,2,1,0:T(8,128)(2,1)S(1)}, bf16[1,1,16,196]{3,2,1,0:T(8,128)(2,1)}, u32[]{:S(2)}) copy-start(bf16[1,1,16,196]{3,2,1,0:T(8,128)(2,1)} %param.29) | copy-start | bytes 18820
  9.7 15.6 %collective-permute-start = (bf16[8,16,384]{2,1,0:T(8,128)(2,1)}, bf16[8,16,384]{2,1,0:T(8,128)(2,1)}, u32[]{:S(2)}, u32[]{:S(2)}) collective-permute-start(bf16[8,16,384]{2,1,0:T(8,128)(2,1)} %get-tuple-element.17), channel_id=1, source_target_pairs={{0,4},{4,8},{8,12},{12,16},{16,20},{20,24},{24,28},{1,5},{5,9},{9,... | collective-permute-start | bytes 294920 | tf_op jit(solution)/shard_map/ppermute | solution.py:614
  13.7 12.3 %collective-permute-start.1 = (bf16[8,16,384]{2,1,0:T(8,128)(2,1)}, bf16[8,16,384]{2,1,0:T(8,128)(2,1)}, u32[]{:S(2)}, u32[]{:S(2)}) collective-permute-start(bf16[8,16,384]{2,1,0:T(8,128)(2,1)} %get-tuple-element.18), channel_id=1, source_target_pairs={{4,0},{8,4},{12,8},{16,12},{20,16},{24,20},{28,24},{5,1},{9,5},{13... | collective-permute-start | bytes 294920 | tf_op jit(solution)/shard_map/ppermute | solution.py:614
  22.6 9.1 %copy-start.4 = (bf16[384,1152]{1,0:T(8,128)(2,1)S(1)}, bf16[384,1152]{1,0:T(8,128)(2,1)}, u32[]{:S(2)}) copy-start(bf16[384,1152]{1,0:T(8,128)(2,1)} %joint_ref.5) | copy-start | bytes 2654212
  22.6 9.1 %copy-start.9 = (f32[384]{0:T(512)S(1)}, f32[384]{0:T(512)}, u32[]{:S(2)}) copy-start(f32[384]{0:T(512)} %first_ref.1) | copy-start | bytes 4612
  26.8 7.4 %collective-permute-start.3 = (bf16[10,16,384]{2,1,0:T(8,128)(2,1)S(1)}, bf16[10,16,384]{2,1,0:T(8,128)(2,1)S(1)}, u32[]{:S(2)}, u32[]{:S(2)}) collective-permute-start(bf16[10,16,384]{2,1,0:T(8,128)(2,1)S(1)} %pad_maximum_fusion.1), channel_id=1, source_target_pairs={{1,0},{2,1},{3,2},{5,4},{6,5},{7,6},{9,8},{10,9},{11,10},{13,12},{... | collective-permute-start | bytes 368648 | tf_op jit(solution)/shard_map/ppermute | solution.py:614
  28.8 6.5 %copy-start.1 = (bf16[384,1536]{1,0:T(8,128)(2,1)S(1)}, bf16[384,1536]{1,0:T(8,128)(2,1)}, u32[]{:S(2)}) copy-start(bf16[384,1536]{1,0:T(8,128)(2,1)} %expand_ref.1) | copy-start | bytes 3538948
  28.8 6.5 %copy-start.2 = (bf16[1536,384]{1,0:T(8,128)(2,1)S(1)}, bf16[1536,384]{1,0:T(8,128)(2,1)}, u32[]{:S(2)}) copy-start(bf16[1536,384]{1,0:T(8,128)(2,1)} %shrink_ref.1) | copy-start | bytes 3538948
  28.8 6.5 %copy-start.5 = (bf16[384,384]{1,0:T(8,128)(2,1)S(1)}, bf16[384,384]{1,0:T(8,128)(2,1)}, u32[]{:S(2)}) copy-start(bf16[384,384]{1,0:T(8,128)(2,1)} %merge_ref.1) | copy-start | bytes 884740
  28.8 6.5 %copy-start.6 = (bf16[384,256]{1,0:T(8,128)(2,1)S(1)}, bf16[384,256]{1,0:T(8,128)(2,1)}, u32[]{:S(2)}) copy-start(bf16[384,256]{1,0:T(8,128)(2,1)} %lateral_ref.1) | copy-start | bytes 589828
  28.8 6.5 %copy-start.10 = (f32[384]{0:T(512)S(1)}, f32[384]{0:T(512)}, u32[]{:S(2)}) copy-start(f32[384]{0:T(512)} %second_ref.1) | copy-start | bytes 4612
  28.8 6.5 %collective-permute-start.2 = (bf16[10,16,384]{2,1,0:T(8,128)(2,1)S(1)}, bf16[10,16,384]{2,1,0:T(8,128)(2,1)S(1)}, u32[]{:S(2)}, u32[]{:S(2)}) collective-permute-start(bf16[10,16,384]{2,1,0:T(8,128)(2,1)S(1)} %pad_maximum_fusion), channel_id=1, source_target_pairs={{0,1},{1,2},{2,3},{4,5},{5,6},{6,7},{8,9},{9,10},{10,11},{12,13},{... | collective-permute-start | bytes 368648 | tf_op jit(solution)/shard_map/ppermute | solution.py:614
  35.3 9.6 %slice-start = ((s8[4718592]{0:T(1024)(128)(4,1)}), s8[4194304]{0:T(1024)(128)(4,1)S(1)}, s32[]{:S(2)}) async-start(s8[4718592]{0:T(1024)(128)(4,1)} %bitcast.9), calls=%async_computation.1 | async-start | bytes 8388608
  35.3 9.6 %slice-start.1 = ((s8[4718592]{0:T(1024)(128)(4,1)}), s8[524288]{0:T(1024)(128)(4,1)S(1)}, s32[]{:S(2)}) async-start(s8[4718592]{0:T(1024)(128)(4,1)} %bitcast.9), calls=%async_computation.2 | async-start | bytes 1048576
  35.3 9.6 %copy-start.7 = (s32[1,1,16,4]{3,2,1,0:T(8,128)S(1)}, s32[1,1,16,4]{3,2,1,0:T(8,128)}, u32[]{:S(2)}) copy-start(s32[1,1,16,4]{3,2,1,0:T(8,128)} %copy.27.geom_ref) | copy-start | bytes 772
  35.3 9.6 %copy-start.11 = (bf16[256]{0:T(256)(128)(2,1)S(1)}, bf16[256]{0:T(256)(128)(2,1)}, u32[]{:S(2)}) copy-start(bf16[256]{0:T(256)(128)(2,1)} %mask_ref.1) | copy-start | bytes 1540
  44.9 1.0 %copy-start = (bf16[32,32,256]{2,1,0:T(8,128)(2,1)S(1)}, bf16[32,32,256]{2,1,0:T(8,128)(2,1)}, u32[]{:S(2)}) copy-start(bf16[32,32,256]{2,1,0:T(8,128)(2,1)} %side_windows.1.features_ref) | copy-start | bytes 1572868
  45.9 39.3 %copy-start.15 = (s32[16]{0:T(128)S(1)}, s32[16]{0:T(128)}, u32[]{:S(2)}) copy-start(s32[16]{0:T(128)} %multiply_add_fusion) | copy-start | bytes 196
  46.0 39.3 %copy-start.16 = (pred[16]{0:T(512)(128)(4,1)S(1)}, pred[16]{0:T(512)(128)(4,1)}, u32[]{:S(2)}) copy-start(pred[16]{0:T(512)(128)(4,1)} %iota_compare_fusion.3) | copy-start | bytes 52

commit v2 on v1

--- a/solution.py
+++ b/solution.py
@@ -13,6 +13,7 @@
 GELU_B = 0.044715
 loss_scale = 128.0
 NT = (((1,), (1,)), ((), ()))
+HIGHEST = lax.Precision.HIGHEST
 TN = (((0,), (0,)), ((), ()))
 VMEM = pl.BlockSpec(memory_space=pltpu.VMEM)
 SMEM = pl.BlockSpec(memory_space=pltpu.SMEM)
@@ -52,55 +53,59 @@
     return pieces
 
 
-def mask_kernel(
-    geom_ref, count_ref, features_ref, weight_ref, mask_ref, soft_ref,
-    logits_ref, grad_ref,
-    a_ref, b_ref, slope_ref, strip_ref, spread_ref, pick_ref, place_ref, before_ref,
+def box_columns(values, shape, axis):
+    index = lax.broadcasted_iota(jnp.int32, shape, axis)
+    spread = jnp.zeros(shape, jnp.int32)
+    for n, value in enumerate(values):
+        spread = jnp.where(index == n, value, spread)
+    return spread
+
+
+def chain(product, finish, before_ref, stages):
+    late = None
+    for number, (layer, source, target) in enumerate(stages):
+        before = before_ref.at[number % 2]
+        for begin in range(0, CROP, ROWS):
+            end = min(begin + ROWS, CROP)
+            before[begin:end] = product(layer, source, begin, end).reshape(
+                (end - begin,) + before.shape[1:]
+            )
+            if late is not None:
+                late()
+            late = functools.partial(finish, layer, before, target, begin, end)
+    late()
+
+
+def forward_kernel(
+    geom_ref, count_ref, owner_ref, features_ref, weight_ref, mask_ref,
+    send_ref, slope_ref,
+    a_ref, b_ref, strip_ref, pick_ref, before_ref,
 ):
     _, boxes, tile_cols, channels = strip_ref.shape
     layers = weight_ref.shape[0]
     lanes = CROP * boxes
     count = count_ref[0, 0]
-    top = [geom_ref[0, 0, n, 0] for n in range(boxes)]
-    left = [geom_ref[0, 0, n, 1] for n in range(boxes)]
-    tall = [jnp.where(n < count, geom_ref[0, 0, n, 2], 0) for n in range(boxes)]
-    broad = [geom_ref[0, 0, n, 3] for n in range(boxes)]
     clear_border(a_ref)
     clear_border(b_ref)
-    lane = lax.broadcasted_iota(jnp.int32, (boxes, boxes * tile_cols), 1)
-    sub = lax.broadcasted_iota(jnp.int32, (boxes, boxes * tile_cols), 0)
-    start = jnp.zeros((boxes, boxes * tile_cols), jnp.int32)
-    width = jnp.zeros((boxes, boxes * tile_cols), jnp.int32)
-    for n in range(boxes):
-        start = jnp.where(sub == n, left[n], start)
-        width = jnp.where(sub == n, broad[n], width)
-    away = jnp.where(lane // tile_cols == sub, lane % tile_cols - start, -1)
+    shape = (boxes, boxes * tile_cols)
+    lane = lax.broadcasted_iota(jnp.int32, shape, 1)
+    start = box_columns([geom_ref[0, 0, n, 1] for n in range(boxes)], shape, 0)
+    width = box_columns([geom_ref[0, 0, n, 3] for n in range(boxes)], shape, 0)
+    mine = lane // tile_cols == lax.broadcasted_iota(jnp.int32, shape, 0)
+    away = jnp.where(mine, lane % tile_cols - start, -1)
     away = jnp.where(away < width, away, -1)
     for v in range(CROP):
         pick_ref[v * boxes : (v + 1) * boxes, :] = (away == v).astype(jnp.bfloat16)
     for n in range(boxes):
-        rows = features_ref[pl.ds(top[n], CROP)]
+        rows = features_ref[pl.ds(geom_ref[0, 0, n, 0], CROP)]
+        tall = jnp.where(n < count, geom_ref[0, 0, n, 2], 0)
         for u in range(CROP):
-            strip_ref[u, n] = jnp.where(u < tall[n], rows[u], jnp.zeros_like(rows[u]))
+            strip_ref[u, n] = jnp.where(u < tall, rows[u], jnp.zeros_like(rows[u]))
     for u in range(CROP):
         crop = jnp.dot(
             pick_ref[...], strip_ref[u].reshape(-1, channels), preferred_element_type=jnp.float32
         )
         a_ref[u + 1, 1 : 1 + CROP] = crop.astype(jnp.bfloat16).reshape(CROP, boxes, channels)
-
-    lane = lax.broadcasted_iota(jnp.int32, (1, lanes), 1)
-    box, col = lane % boxes, lane // boxes
-    height = jnp.zeros((1, lanes), jnp.int32)
-    for n in range(boxes):
-        height = jnp.where((box == n) & (col < broad[n]), tall[n], height)
-    cell = lax.broadcasted_iota(jnp.int32, (tile_cols, lanes), 0)
-    for n in range(boxes):
-        place_ref[n * tile_cols : (n + 1) * tile_cols, :] = (
-            (cell == col + left[n]) & (box == n) & (col < broad[n])
-        ).astype(jnp.bfloat16)
-    vector = jnp.broadcast_to(
-        mask_ref[...].astype(jnp.float32).reshape(1, channels), (8, channels)
-    ).astype(jnp.bfloat16)
 
     def forward(layer, source, begin, end):
         return jnp.dot(
@@ -114,8 +119,67 @@
             for v in range(CROP):
                 piece = slice(v * boxes, (v + 1) * boxes)
                 value, slope = gelu_parts(before[u, piece])
-                slope_ref[layer + 1, u, piece] = slope.astype(jnp.bfloat16)
+                slope_ref[layer, u, piece] = slope.astype(jnp.bfloat16)
                 target[u + 1, 1 + v] = value.astype(jnp.bfloat16)
+
+    def up(pair, carry):
+        stages = [(2 * pair, a_ref, b_ref), (2 * pair + 1, b_ref, a_ref)]
+        chain(forward, activate, before_ref, stages)
+        return carry
+
+    lax.fori_loop(0, layers // 2, up, 0)
+    vector = mask_ref[...].astype(jnp.float32).reshape(1, channels)
+    place = lax.broadcasted_iota(jnp.int32, send_ref.shape, 1)
+    sums = [jnp.zeros(send_ref.shape, jnp.float32) for _ in range(2)]
+    for cell in range(CROP * CROP):
+        u, v = divmod(cell, CROP)
+        line = jnp.sum(a_ref[u + 1, v + 1].astype(jnp.float32) * vector, axis=-1, keepdims=True)
+        sums[cell % 2] = jnp.where(place == cell, line, sums[cell % 2])
+    owner = box_columns(
+        [jnp.where(n < count, owner_ref[0, 0, n], -1) for n in range(boxes)], send_ref.shape, 0
+    )
+    send_ref[...] = jnp.where(
+        place == CROP * CROP, owner.astype(jnp.float32), sums[0] + sums[1]
+    )
+
+
+def backward_kernel(
+    geom_ref, count_ref, send_ref, soft_ref, slope_ref, weight_ref, mask_ref,
+    grad_ref,
+    a_ref, b_ref, spread_ref, place_ref, before_ref,
+):
+    boxes, channels = a_ref.shape[2:]
+    tile_cols = grad_ref.shape[1]
+    layers = weight_ref.shape[0]
+    lanes = CROP * boxes
+    cells = CROP * CROP
+    count = count_ref[0, 0]
+    clear_border(a_ref)
+    clear_border(b_ref)
+    broad = [geom_ref[0, 0, n, 3] for n in range(boxes)]
+    tall = [jnp.where(n < count, geom_ref[0, 0, n, 2], 0) for n in range(boxes)]
+    lane = lax.broadcasted_iota(jnp.int32, (tile_cols, lanes), 1)
+    cell = lax.broadcasted_iota(jnp.int32, (tile_cols, lanes), 0)
+    box, col = lane % boxes, lane // boxes
+    for n in range(boxes):
+        place_ref[n * tile_cols : (n + 1) * tile_cols, :] = (
+            (cell == col + geom_ref[0, 0, n, 1]) & (box == n) & (col < broad[n])
+        ).astype(jnp.bfloat16)
+    shape = (boxes, cells)
+    where = lax.broadcasted_iota(jnp.int32, shape, 1)
+    inside = (where // CROP < box_columns(tall, shape, 0)) & (
+        where % CROP < box_columns(broad, shape, 0)
+    )
+    soft = soft_ref[0, 0].astype(jnp.float32)
+    lead = loss_scale * (jax.nn.sigmoid(send_ref[:, :cells]) - soft)
+    lead = jnp.where(inside, lead, 0.0)
+    vector = mask_ref[...].astype(jnp.float32).reshape(1, channels)
+    for u in range(CROP):
+        for v in range(CROP):
+            piece = slice(v * boxes, (v + 1) * boxes)
+            grad = lead[:, u * CROP + v : u * CROP + v + 1] * vector
+            slope = slope_ref[layers - 1, u, piece].astype(jnp.float32)
+            b_ref[u + 1, 1 + v] = (grad * slope).astype(jnp.bfloat16)
 
     def backward(layer, source, begin, end):
         total = None
@@ -130,58 +194,20 @@
         return total
 
     def descend(layer, before, target, begin, end):
+        first = layer == 0
         for u in range(begin, end):
             for v in range(CROP):
                 piece = slice(v * boxes, (v + 1) * boxes)
-                slope = slope_ref[layer, u, piece].astype(jnp.float32)
+                slope = slope_ref[jnp.maximum(layer - 1, 0), u, piece].astype(jnp.float32)
+                slope = jnp.where(first, 1.0, slope)
                 target[u + 1, 1 + v] = (before[u, piece] * slope).astype(jnp.bfloat16)
-
-    def chain(product, finish, stages):
-        late = None
-        for number, (layer, source, target) in enumerate(stages):
-            before = before_ref.at[number % 2]
-            for begin in range(0, CROP, ROWS):
-                end = min(begin + ROWS, CROP)
-                before[begin:end] = product(layer, source, begin, end).reshape(
-                    end - begin, lanes, channels
-                )
-                if late is not None:
-                    late()
-                late = functools.partial(finish, layer, before, target, begin, end)
-        late()
-
-    def up(pair, carry):
-        chain(forward, activate, [(2 * pair, a_ref, b_ref), (2 * pair + 1, b_ref, a_ref)])
-        return carry
 
     def down(pair, carry):
         layer = layers - 1 - 2 * pair
-        chain(backward, descend, [(layer, b_ref, a_ref), (layer - 1, a_ref, b_ref)])
+        stages = [(layer, b_ref, a_ref), (layer - 1, a_ref, b_ref)]
+        chain(backward, descend, before_ref, stages)
         return carry
 
-    slope_ref[0] = jnp.ones(slope_ref.shape[1:], slope_ref.dtype)
-    lax.fori_loop(0, layers // 2, up, 0)
-    for u in range(CROP):
-        line = lax.dot_general(
-            vector, a_ref[u + 1, 1 : 1 + CROP].reshape(lanes, channels), NT,
-            preferred_element_type=jnp.float32,
-        )[0:1]
-        logits_ref[u : u + 1, :] = line
-    grad = loss_scale * (jax.nn.sigmoid(logits_ref[...]) - soft_ref[...])
-    grad = jnp.where(lax.broadcasted_iota(jnp.int32, (CROP, lanes), 0) < height, grad, 0.0)
-    high = grad.astype(jnp.bfloat16).astype(jnp.float32)
-    for u in range(CROP):
-        pair = jnp.concatenate(
-            [high[u : u + 1], (grad - high)[u : u + 1], jnp.zeros((6, lanes), jnp.float32)], axis=0
-        )
-        lead = lax.dot_general(
-            pair.astype(jnp.bfloat16), vector, TN, preferred_element_type=jnp.float32
-        )
-        b_ref[u + 1, 1 : 1 + CROP] = (
-            (lead * slope_ref[layers, u].astype(jnp.float32))
-            .astype(jnp.bfloat16)
-            .reshape(CROP, boxes, channels)
-        )
     lax.fori_loop(0, layers // 2, down, 0)
     for u in range(CROP):
         spread_ref[u] = jnp.dot(
@@ -192,36 +218,89 @@
     grad_ref[...] = jnp.zeros_like(grad_ref)
     for n in range(boxes):
         kept = lax.broadcasted_iota(jnp.int32, (CROP, 1, 1), 0) < tall[n]
-        rows = pl.ds(top[n], CROP)
+        rows = pl.ds(geom_ref[0, 0, n, 0], CROP)
         grad_ref[rows] = grad_ref[rows] + jnp.where(kept, spread_ref[:, n], 0.0)
 
 
-def mask_head(features, geometry, count, weight, mask, soft):
+def collect_kernel(sent_ref, out_ref):
+    boxes = sent_ref.shape[0]
+    keep, cells = out_ref.shape[2:]
+    owner = sent_ref[:, cells : cells + 1]
+    mine = (owner == lax.axis_index("row").astype(jnp.float32)).astype(jnp.float32)
+    row = lax.broadcasted_iota(jnp.int32, (boxes, boxes), 0)
+    col = lax.broadcasted_iota(jnp.int32, (boxes, boxes), 1)
+    earlier = (col < row).astype(jnp.float32).astype(jnp.bfloat16)
+    many = jnp.broadcast_to(mine, (boxes, 128)).astype(jnp.bfloat16)
+    position = jnp.dot(earlier, many, preferred_element_type=jnp.float32)[:, :keep]
+    slot = lax.broadcasted_iota(jnp.int32, (boxes, keep), 1).astype(jnp.float32)
+    picker = jnp.where(position == slot, mine, 0.0)
+    out_ref[0, 0] = lax.dot_general(
+        picker, sent_ref[:, :cells], TN, precision=HIGHEST, preferred_element_type=jnp.float32
+    )
+
+
+def mask_cost(weight):
+    return pl.CostEstimate(flops=25 * 10**9, bytes_accessed=2 * weight.size, transcendentals=0)
+
+
+def mask_forward(features, geometry, count, owner, weight, mask):
     tile_rows, tile_cols, channels = features.shape
     boxes = geometry.shape[2]
     layers = weight.shape[0]
     lanes = CROP * boxes
+    padded = pltpu.VMEM((PAD, PAD, boxes, channels), jnp.bfloat16)
     return pl.pallas_call(
-        mask_kernel,
+        forward_kernel,
         out_shape=(
-            jax.ShapeDtypeStruct((CROP, lanes), jnp.float32),
-            jax.ShapeDtypeStruct((tile_rows, tile_cols, channels), jnp.float32),
+            jax.ShapeDtypeStruct((boxes, 256), jnp.float32),
+            jax.ShapeDtypeStruct((layers, CROP, lanes, channels), jnp.bfloat16),
         ),
-        in_specs=[SMEM, SMEM, VMEM, VMEM, VMEM, VMEM],
+        in_specs=[SMEM, SMEM, SMEM, VMEM, VMEM, VMEM],
         out_specs=(VMEM, VMEM),
         scratch_shapes=[
-            pltpu.VMEM((PAD, PAD, boxes, channels), jnp.bfloat16),
-            pltpu.VMEM((PAD, PAD, boxes, channels), jnp.bfloat16),
-            pltpu.VMEM((layers + 1, CROP, lanes, channels), jnp.bfloat16),
+            padded,
+            padded,
             pltpu.VMEM((CROP, boxes, tile_cols, channels), jnp.bfloat16),
-            pltpu.VMEM((CROP, boxes, tile_cols, channels), jnp.float32),
             pltpu.VMEM((lanes, boxes * tile_cols), jnp.bfloat16),
-            pltpu.VMEM((boxes * tile_cols, lanes), jnp.bfloat16),
             pltpu.VMEM((2, CROP, lanes, channels), jnp.float32),
         ],
-        compiler_params=pltpu.CompilerParams(vmem_limit_bytes=48 * 2**20),
-        name="mask_head",
-    )(geometry, count, features, weight, mask, soft)
+        compiler_params=pltpu.CompilerParams(vmem_limit_bytes=32 * 2**20),
+        cost_estimate=mask_cost(weight),
+        name="mask_forward",
+    )(geometry, count, owner, features, weight, mask)
+
+
+def mask_backward(send, soft, slope, geometry, count, weight, mask, tile):
+    layers, _, lanes, channels = slope.shape
+    boxes = geometry.shape[2]
+    padded = pltpu.VMEM((PAD, PAD, boxes, channels), jnp.bfloat16)
+    return pl.pallas_call(
+        backward_kernel,
+        out_shape=jax.ShapeDtypeStruct(tile + (channels,), jnp.float32),
+        in_specs=[SMEM, SMEM, VMEM, VMEM, VMEM, VMEM, VMEM],
+        out_specs=VMEM,
+        scratch_shapes=[
+            padded,
+            padded,
+            pltpu.VMEM((CROP, boxes, tile[1], channels), jnp.float32),
+            pltpu.VMEM((boxes * tile[1], lanes), jnp.bfloat16),
+            pltpu.VMEM((2, CROP, lanes, channels), jnp.float32),
+        ],
+        compiler_params=pltpu.CompilerParams(vmem_limit_bytes=38 * 2**20),
+        cost_estimate=mask_cost(weight),
+        name="mask_backward",
+    )(geometry, count, send, soft, slope, weight, mask)
+
+
+def collect(sent, keep, cells):
+    return pl.pallas_call(
+        collect_kernel,
+        out_shape=jax.ShapeDtypeStruct((1, 1, keep, cells), jnp.float32),
+        in_specs=[VMEM],
+        out_specs=VMEM,
+        compiler_params=pltpu.CompilerParams(vmem_limit_bytes=8 * 2**20),
+        name="collect",
+    )(sent)
 
 
 HEADS = 12
@@ -232,7 +311,6 @@
 GROUP = 4
 EPSILON = 1e-05
 BLOCKED = -1000000000.0
-HIGHEST = lax.Precision.HIGHEST
 
 
 def norm_rows(values, gain):
@@ -416,7 +494,7 @@
 def sides_kernel(
     ordered_ref, joint_out_ref, inner_ref, pairs_ref, ends_ref, left_ref, right_ref,
     bias_ref, first_ref, second_ref, joint_ref, merge_ref, expand_ref, shrink_ref, lateral_ref,
-    features_ref, mixed_ref, halo_ref, order_ref, residual_ref, normed_ref, wide_ref, hidden_ref,
+    features_ref, copy_ref, mixed_ref, halo_ref, order_ref, residual_ref, normed_ref, wide_ref, hidden_ref,
 ):
     cells_down, cells_across, _, triple = joint_out_ref.shape
     model = triple // 3
@@ -506,7 +584,9 @@
                 preferred_element_type=jnp.float32,
             ).astype(jnp.bfloat16)
             first = (step * group + part) * SUB
-            features_ref[first : first + SUB] = natural.reshape((SUB,) + features_ref.shape[1:])
+            natural = natural.reshape((SUB,) + features_ref.shape[1:])
+            features_ref[first : first + SUB] = natural
+            copy_ref[first : first + SUB] = natural
 
     merge(0)
     expand(0)
@@ -586,11 +666,12 @@
     strip = CELL * across
     rows = 2 * strip
     wide = weights[2].shape[1]
+    tile = jax.ShapeDtypeStruct((down * SUB, across * SUB, weights[-1].shape[1]), jnp.bfloat16)
     return pl.pallas_call(
         sides_kernel,
-        out_shape=jax.ShapeDtypeStruct((down * SUB, across * SUB, weights[-1].shape[1]), jnp.bfloat16),
+        out_shape=(tile, tile),
         in_specs=[VMEM] * 15,
-        out_specs=VMEM,
+        out_specs=(VMEM, VMEM),
         scratch_shapes=[
             pltpu.VMEM((down, across, CELL, model), jnp.bfloat16),
             pltpu.VMEM((2, down + 2, CELL, 2 * model), jnp.bfloat16),
@@ -620,7 +701,6 @@
     soft_target,
 ):
     tile_rows, tile_cols, model = tokens.shape
-    rows_size = lax.axis_size("row")
     joint, bias, ordered, north, south, west, east = joint_rows(
         tokens, first_gain, joint_weight, relative_bias
     )
@@ -630,41 +710,19 @@
     left = shift(jnp.concatenate([up[-1:], east, down[-1:]], axis=0), "col", 1)
     right = shift(jnp.concatenate([up[:1], west, down[:1]], axis=0), "col", -1)
     pairs, ends = end_windows(joint, up, down, bias, first_gain, joint_weight)
-    features = side_windows(
+    features, features_here = side_windows(
         ordered, joint, inner, pairs, ends, left, right, bias, (first_gain, second_gain),
         (joint_weight, merge_weight, expand_weight, shrink_weight, lateral_weight),
     )
-    capacity = box_geometry.shape[2]
-    count = box_counts.reshape(1)
-    soft = soft_target.reshape(capacity, CROP, CROP).transpose(1, 2, 0).astype(jnp.float32)
-    logits, feature_grad = mask_head(
-        features, box_geometry, box_counts, conv_weight, mask_weight, soft.reshape(CROP, -1)
-    )
-    local = logits.reshape(CROP * CROP, capacity)
-    slots = jnp.arange(capacity, dtype=jnp.int32)
-    valid = slots < count
-    owner = box_owner.reshape(-1)
-    rank = jnp.sum((owner[:, None] == owner[None, :]) & (slots[None, :] < slots[:, None]), axis=1)
-    each = max(1, capacity // rows_size)
-    send = rows_size * each
-    routing = (
-        (owner * each + rank)[None, :] == jnp.arange(send, dtype=jnp.int32)[:, None]
-    ) & valid[None, :]
-    packed = jnp.concatenate(
-        [local, jnp.ones((1, capacity), jnp.float32)], axis=0
-    )
-    outgoing = lax.dot_general(
-        routing.astype(jnp.float32), packed, NT, precision=HIGHEST
-    ).reshape(rows_size, each, -1)
-    arriving = lax.all_to_all(outgoing, "row", split_axis=0, concat_axis=0, tiled=True)
-    arriving = arriving.reshape(send, -1)
-    present = arriving[:, -1] > 0.5
-    position = jnp.cumsum(present.astype(jnp.int32)) - 1
-    picker = (
-        position[None, :] == jnp.arange(BOX_OWN, dtype=jnp.int32)[:, None]
-    ) & present[None, :]
-    mask_logits = jnp.dot(picker.astype(jnp.float32), arriving[:, :-1], precision=HIGHEST)
-    return features, feature_grad, mask_logits.reshape(1, 1, BOX_OWN, -1)
+    send, slope = mask_forward(
+        features_here, box_geometry, box_counts, box_owner, conv_weight, mask_weight
+    )
+    sent = lax.all_gather(send, "row", axis=0, tiled=True)
+    feature_grad = mask_backward(
+        send, soft_target, slope, box_geometry, box_counts, conv_weight, mask_weight,
+        (tile_rows, tile_cols),
+    )
+    return features, feature_grad, collect(sent, BOX_OWN, CROP * CROP)
 
 
 def solution(mesh):

time: 101 us -> 114 us (1.13)
  blocking collectives: 13.3 us -> 31.4 us
  local copies, waits for them, and re-layouts: 11.5 us -> 6.51 us
  other arithmetic: 3.06 us -> 0.94 us
  Pallas kernels: 58.5 us -> 60.4 us
    all_gather x0 -> x1, blocking collectives: none -> 31.4 us  [shards(): sent = lax.all_gather(send, 'row', axis=0, tiled=True)]
    all_to_all x1 -> x0, blocking collectives: 13.3 us -> none  [shards(): lax.all_to_all(outgoing, 'row', split_axis=0, concat_axis=0, tiled=True)]
    reshape x6 -> x0, local copies, waits for them, and re-layouts: 3.64 us -> none  [the longest x3 3.46 us: shards(): soft.reshape(CROP, -1)]
    pallas_call x2 -> x4, Pallas kernels: 48.7 us -> 50.5 us  [the longest x1 20.1 us: mask_forward(): pl.pallas_call(forward_kernel, out_shape=(jax.ShapeDtypeStruct((boxes, 25...]
    unnamed x39 -> x45, local copies, waits for them, and re-layouts: 6.44 us -> 5.06 us
    add x1 -> x0, other arithmetic: 1.18 us -> none  [shards(): owner * each + rank]
  transfers between devices with their start and end apart: 4 -> 4, of which waited for: 1 -> 1; matrix products, arithmetic and copies ran while one was open for 8% -> 1% of each run, Pallas kernels for 5% -> 4%
where the time goes in v2:
time: 114 us; the launch traced here: 113 us
  Pallas kernels  60.4 us (53%)
  blocking collectives  31.4 us (28%)
  starting transfers between devices  11.1 us (10%)
  local copies, waits for them, and re-layouts  6.51 us (6%)
  between operations  1.6 us (1%)
    all_gather x1, blocking collectives, shards(): sent = lax.all_gather(send, 'row', axis=0, tiled=True)  31.4 us
    pallas_call x1, Pallas kernels, mask_forward(): pl.pallas_call(forward_kernel, out_shape=(jax.ShapeDtypeStruct((boxes, 25...  20.1 us
    pallas_call x1, Pallas kernels, mask_backward(): pl.pallas_call(backward_kernel, out_shape=jax.ShapeDtypeStruct(tile + (ch...  19.9 us
    ppermute x4, starting transfers between devices, shift(): return lax.ppermute(x, axis, pairs)  11.1 us
    pallas_call x1, Pallas kernels, side_windows(): pl.pallas_call(sides_kernel, out_shape=(tile, tile), in_specs=[VMEM] * 15...  9.47 us
    pallas_call x1, Pallas kernels, joint_rows(): pl.pallas_call(joint_kernel, out_shape=(cells_of(down, across, weight.sha...  5.09 us
    unnamed x45, local copies, waits for them, and re-layouts  5.06 us
    pallas_call x1, Pallas kernels, end_windows(): pl.pallas_call(ends_kernel, out_shape=(cells_of(2, across, triple * 2 //...  2.68 us
  transfers between devices with their start and end apart: 4, of which 1 were waited for; matrix products, arithmetic and copies ran while one was open for 1% of the time, Pallas kernels for 4%

profile of v2, /device:TPU:4, one launch (start us, length us, event | category | flops | bytes accessed | tf_op | source)
XLA Modules:
  0.0 113.0 jit_solution(6442123744160185449)
XLA Ops:
  0.6 0.0 copy-start.2
  0.6 1.2 %copy-done.2 = bf16[384,1152]{1,0:T(8,128)(2,1)S(1)} copy-done((bf16[384,1152]{1,0:T(8,128)(2,1)S(1)}, bf16[384,1152]{1,0:T(8,128)(2,1)}, u32[]{:S(2)}) %copy-start.2) | copy-done | bytes 884760
  1.8 0.7 copy-done.11
  2.5 1.1 %copy-done.14 = bf16[32,32,384]{2,1,0:T(8,128)(2,1)S(1)} copy-done((bf16[32,32,384]{2,1,0:T(8,128)(2,1)S(1)}, bf16[32,32,384]{2,1,0:T(8,128)(2,1)}, u32[]{:S(2)}) %copy-start.14) | copy-done | bytes 786456
  3.6 1.0 copy-done.15
  4.6 5.1 %joint_rows.1 = (bf16[8,8,16,1152]{3,2,1,0:T(8,128)(2,1)S(1)}, f32[3,64,256]{2,1,0:T(8,128)S(1)}, bf16[8,8,16,384]{3,2,1,0:T(8,128)(2,1)S(1)}, bf16[8,16,384]{2,...) custom-call(bf16[32,32,384]{2,1,0:T(8,128)(2,1)S(1)} %copy-done.14, ...), custom_call_target="tpu_custom_call" | custom-call | flops 1811939328 | bytes 4194304 | tf_op jit(solution)/shard_map/joint_rows/pallas_call | solution.py:617
  9.7 4.0 %collective-permute-start = (bf16[8,16,384]{2,1,0:T(8,128)(2,1)}, bf16[8,16,384]{2,1,0:T(8,128)(2,1)}, u32[]{:S(2)}, u32[]{:S(2)}) collective-permute-start(bf16[8,16,384]{2,1,0:T(8,128)(2,1)} %get-tuple-element.19), channel_id=1, source_target_pairs={{0,4},{4,8},{8,12},{12,16},{16,20},{20,24},{24,28},{1,5},{5,9},{9,... | collective-permute-start | bytes 294920 | tf_op jit(solution)/shard_map/ppermute | solution.py:695
  13.7 1.3 %collective-permute-start.1 = (bf16[8,16,384]{2,1,0:T(8,128)(2,1)}, bf16[8,16,384]{2,1,0:T(8,128)(2,1)}, u32[]{:S(2)}, u32[]{:S(2)}) collective-permute-start(bf16[8,16,384]{2,1,0:T(8,128)(2,1)} %get-tuple-element.20), channel_id=1, source_target_pairs={{4,0},{8,4},{12,8},{16,12},{20,16},{24,20},{28,24},{5,1},{9,5},{13... | collective-permute-start | bytes 294920 | tf_op jit(solution)/shard_map/ppermute | solution.py:695
  15.0 0.0 copy-start.19
  15.0 0.0 copy-start.3
  15.0 0.0 copy-start.12
  15.1 2.1 %inner_windows.1.inner_ref = bf16[8,8,16,384]{3,2,1,0:T(8,128)(2,1)S(1)} custom-call(bf16[8,8,16,1152]{3,2,1,0:T(8,128)(2,1)S(1)} %get-tuple-element.17.joint_ref.joint_out_ref, f32[3,64,256]{2,1,0:T(8,128)S(1)} %get-tuple-element.18.bias_ref), custom_call_target="tpu_custom_call" | custom-call | flops 2147483648 | bytes 4194304 | tf_op jit(solution)/shard_map/inner_windows/pallas_call | solution.py:639
  17.2 0.9 copy-done.6
  18.8 0.0 copy-done.19
  18.8 0.1 copy.19.geom_ref
  18.9 0.0 collective-permute-done.up_ref
  18.9 0.7 fusion
  19.6 0.9 collective-permute-done.1.down_ref
  20.5 0.7 fusion.1
  21.3 0.9 pad_maximum_fusion
  22.2 1.9 %collective-permute-start.2 = (bf16[10,16,384]{2,1,0:T(8,128)(2,1)S(1)}, bf16[10,16,384]{2,1,0:T(8,128)(2,1)S(1)}, u32[]{:S(2)}, u32[]{:S(2)}) collective-permute-start(bf16[10,16,384]{2,1,0:T(8,128)(2,1)S(1)} %pad_maximum_fusion), channel_id=1, source_target_pairs={{0,1},{1,2},{2,3},{4,5},{5,6},{6,7},{8,9},{9,10},{10,11},{12,13},{... | collective-permute-start | bytes 368648 | tf_op jit(solution)/shard_map/ppermute | solution.py:695
  24.2 0.0 copy-start
  24.2 0.0 copy-start.1
  24.2 0.0 copy-start.5
  24.2 0.0 copy-start.8
  24.2 0.0 copy-start.9
  24.2 0.0 copy-start.13
  24.2 3.9 %collective-permute-start.3 = (bf16[10,16,384]{2,1,0:T(8,128)(2,1)S(1)}, bf16[10,16,384]{2,1,0:T(8,128)(2,1)S(1)}, u32[]{:S(2)}, u32[]{:S(2)}) collective-permute-start(bf16[10,16,384]{2,1,0:T(8,128)(2,1)S(1)} %pad_maximum_fusion.1), channel_id=1, source_target_pairs={{1,0},{2,1},{3,2},{5,4},{6,5},{7,6},{9,8},{10,9},{11,10},{13,12},{... | collective-permute-start | bytes 368648 | tf_op jit(solution)/shard_map/ppermute | solution.py:695
  28.1 0.0 copy-done.3
  28.2 0.0 copy-done.12
  28.2 0.0 slice-start
  28.2 2.7 %end_windows.1 = (bf16[2,8,16,768]{3,2,1,0:T(8,128)(2,1)S(1)}, bf16[2,8,16,384]{3,2,1,0:T(8,128)(2,1)S(1)}) custom-call(bf16[8,8,16,1152]{3,2,1,0:T(8,128)(2,1)S(1)} %get-tuple-element.17.joint_ref.joint_out_ref, bf16[8,16,384]{2,1,0:T(8,128)(2,1)} %collective-permute-done.up_ref, bf16[8,16,384]{2,1,0:T(8,128)(2,1)} %collective-permute-done.1.down_ref, ...), custom_call_target="tpu_custom_call" | custom-call | flops 2147483648 | bytes 4194304 | tf_op jit(solution)/shard_map/end_windows/pallas_call | solution.py:652
  30.9 0.0 collective-permute-done.2.left_ref
  30.9 0.0 collective-permute-done.3.right_ref
  30.9 0.0 copy-done
  30.9 0.0 copy-done.1
  30.9 0.0 copy-done.5
  30.9 0.0 copy-done.7
  30.9 0.0 copy-done.8
  31.0 0.0 slice-start.1
  31.0 0.0 copy-start.17
  31.0 0.0 copy-start.18
  31.0 9.5 %side_windows.1 = (bf16[32,32,256]{2,1,0:T(8,128)(2,1)}, bf16[32,32,256]{2,1,0:T(8,128)(2,1)S(1)}) custom-call(bf16[8,8,16,384]{3,2,1,0:T(8,128)(2,1)S(1)} %copy-done.5, bf16[8,8,16,1152]{3,2,1,0:T(8,128)(2,1)S(1)} %get-tuple-element.17.joint_ref.joint_out_ref, bf16[8,8,16,384]{3,2,1,0:T(8,128)(2,1)S(1)} %copy-done.7, ...), custom_call_target="tpu_custom_call" | custom-call | tf_op jit(solution)/shard_map/side_windows/pallas_call | solution.py:670
  40.5 0.0 copy-start.16
  40.5 20.1 %mask_forward.1 = (f32[16,256]{1,0:T(8,128)S(1)}, bf16[4,14,224,256]{3,2,1,0:T(8,128)(2,1)S(1)}) custom-call(s32[1,1,16,4]{3,2,1,0:T(8,128)S(1)} %copy.19.geom_ref, s32[1,1]{1,0:T(1,128)S(6)} %copy.20.count_ref, s32[1,1,16]{2,1,0:T(1,128)S(1)} %copy-done.17, bf16[32,32,256]{2,1,0:T(8,128)(2,1)S(1)} %get-tuple-element.26.features_ref, ...), custom_call_target="tpu_custom_call" | custom-call | flops 24999999488 | bytes 4718592 | tf_op jit(solution)/shard_map/mask_forward/pallas_call | solution.py:252
  60.6 31.4 %all_gather.3.sent_ref = f32[128,256]{1,0:T(8,128)S(1)} all-gather(f32[16,256]{1,0:T(8,128)S(1)} %get-tuple-element.27.send_ref), channel_id=1, replica_groups=mesh['row'=8,'col'=4] {'row'}, dimensions={0}, use_global_device_ids=true | all-gather | bytes 147456 | tf_op jit(solution)/shard_map/all_gather | solution.py:720
  92.1 1.0 collect.1
  93.1 19.9 %mask_backward.1 = f32[32,32,256]{2,1,0:T(8,128)} custom-call(s32[1,1,16,4]{3,2,1,0:T(8,128)S(1)} %copy.19.geom_ref, s32[1,1]{1,0:T(1,128)S(6)} %copy.20.count_ref, f32[16,256]{1,0:T(8,128)S(1)} %get-tuple-element.27.send_ref, bf16[1,1,16,196]{3,2,1,0:T(8,128)(2,1)S(1)} %copy-done.16, bf16[4,14,224,256]{3,2,1,0:T(8,128)(2,1)S(1)} %get-tuple-element.28.slope_ref, ...), custom_call_target="tpu_custom_call" | custom-call | flops 24999999488 | bytes 4718592 | tf_op jit(solution)/shard_map/mask_backward/pallas_call | solution.py:277
  (18 shorter events, 0.1 us)
Async XLA Ops:
  0.6 1.2 %copy-start.2 = (bf16[384,1152]{1,0:T(8,128)(2,1)S(1)}, bf16[384,1152]{1,0:T(8,128)(2,1)}, u32[]{:S(2)}) copy-start(bf16[384,1152]{1,0:T(8,128)(2,1)} %joint_ref.5) | copy-start | bytes 2654212
  1.8 0.7 copy-start.11
  2.5 1.1 %copy-start.14 = (bf16[32,32,384]{2,1,0:T(8,128)(2,1)S(1)}, bf16[32,32,384]{2,1,0:T(8,128)(2,1)}, u32[]{:S(2)}) copy-start(bf16[32,32,384]{2,1,0:T(8,128)(2,1)} %tokens_ref.1) | copy-start | bytes 2359300
  3.6 1.0 copy-start.15
  9.7 7.5 %copy-start.4 = (bf16[8,8,16,384]{3,2,1,0:T(8,128)(2,1)}, bf16[8,8,16,384]{3,2,1,0:T(8,128)(2,1)S(1)}, u32[]{:S(2)}) copy-start(bf16[8,8,16,384]{3,2,1,0:T(8,128)(2,1)S(1)} %get-tuple-element.16.ordered_ref) | copy-start | bytes 2359300
  9.7 7.5 %copy-start.10 = (bf16[8,16,384]{2,1,0:T(8,128)(2,1)}, bf16[8,16,384]{2,1,0:T(8,128)(2,1)S(1)}, u32[]{:S(2)}) copy-start(bf16[8,16,384]{2,1,0:T(8,128)(2,1)S(1)} %get-tuple-element.23) | copy-start | bytes 294916
  9.7 9.2 %collective-permute-start = (bf16[8,16,384]{2,1,0:T(8,128)(2,1)}, bf16[8,16,384]{2,1,0:T(8,128)(2,1)}, u32[]{:S(2)}, u32[]{:S(2)}) collective-permute-start(bf16[8,16,384]{2,1,0:T(8,128)(2,1)} %get-tuple-element.19), channel_id=1, source_target_pairs={{0,4},{4,8},{8,12},{12,16},{16,20},{20,24},{24,28},{1,5},{5,9},{9,... | collective-permute-start | bytes 294920 | tf_op jit(solution)/shard_map/ppermute | solution.py:695
  13.7 6.8 %collective-permute-start.1 = (bf16[8,16,384]{2,1,0:T(8,128)(2,1)}, bf16[8,16,384]{2,1,0:T(8,128)(2,1)}, u32[]{:S(2)}, u32[]{:S(2)}) collective-permute-start(bf16[8,16,384]{2,1,0:T(8,128)(2,1)} %get-tuple-element.20), channel_id=1, source_target_pairs={{4,0},{8,4},{12,8},{16,12},{20,16},{24,20},{28,24},{5,1},{9,5},{13... | collective-permute-start | bytes 294920 | tf_op jit(solution)/shard_map/ppermute | solution.py:695
  15.0 3.8 %copy-start.19 = (s32[1,1,16,4]{2,3,1,0:T(4,128)S(1)}, s32[1,1,16,4]{2,3,1,0:T(4,128)}, u32[]{:S(2)}) copy-start(s32[1,1,16,4]{2,3,1,0:T(4,128)} %param.26) | copy-start | bytes 772
  15.0 13.1 %copy-start.3 = (bf16[384,1152]{1,0:T(8,128)(2,1)S(1)}, bf16[384,1152]{1,0:T(8,128)(2,1)}, u32[]{:S(2)}) copy-start(bf16[384,1152]{1,0:T(8,128)(2,1)} %joint_ref.5) | copy-start | bytes 2654212
  15.0 13.1 %copy-start.12 = (f32[384]{0:T(512)S(1)}, f32[384]{0:T(512)}, u32[]{:S(2)}) copy-start(f32[384]{0:T(512)} %first_ref.1) | copy-start | bytes 4612
  17.2 0.9 copy-start.6
  22.2 8.7 %collective-permute-start.2 = (bf16[10,16,384]{2,1,0:T(8,128)(2,1)S(1)}, bf16[10,16,384]{2,1,0:T(8,128)(2,1)S(1)}, u32[]{:S(2)}, u32[]{:S(2)}) collective-permute-start(bf16[10,16,384]{2,1,0:T(8,128)(2,1)S(1)} %pad_maximum_fusion), channel_id=1, source_target_pairs={{0,1},{1,2},{2,3},{4,5},{5,6},{6,7},{8,9},{9,10},{10,11},{12,13},{... | collective-permute-start | bytes 368648 | tf_op jit(solution)/shard_map/ppermute | solution.py:695
  24.2 6.7 %copy-start = (bf16[384,1536]{1,0:T(8,128)(2,1)S(1)}, bf16[384,1536]{1,0:T(8,128)(2,1)}, u32[]{:S(2)}) copy-start(bf16[384,1536]{1,0:T(8,128)(2,1)} %expand_ref.1) | copy-start | bytes 3538948
  24.2 6.7 %copy-start.1 = (bf16[1536,384]{1,0:T(8,128)(2,1)S(1)}, bf16[1536,384]{1,0:T(8,128)(2,1)}, u32[]{:S(2)}) copy-start(bf16[1536,384]{1,0:T(8,128)(2,1)} %shrink_ref.1) | copy-start | bytes 3538948
  24.2 6.7 %copy-start.5 = (bf16[8,8,16,384]{3,2,1,0:T(8,128)(2,1)S(1)}, bf16[8,8,16,384]{3,2,1,0:T(8,128)(2,1)}, u32[]{:S(2)}) copy-start(bf16[8,8,16,384]{3,2,1,0:T(8,128)(2,1)} %copy-done.4) | copy-start | bytes 2359300
  24.2 6.7 %copy-start.7 = (bf16[8,8,16,384]{3,2,1,0:T(8,128)(2,1)S(1)}, bf16[8,8,16,384]{3,2,1,0:T(8,128)(2,1)}, u32[]{:S(2)}) copy-start(bf16[8,8,16,384]{3,2,1,0:T(8,128)(2,1)} %copy-done.6) | copy-start | bytes 2359300
  24.2 6.7 %copy-start.8 = (bf16[384,384]{1,0:T(8,128)(2,1)S(1)}, bf16[384,384]{1,0:T(8,128)(2,1)}, u32[]{:S(2)}) copy-start(bf16[384,384]{1,0:T(8,128)(2,1)} %merge_ref.1) | copy-start | bytes 884740
  24.2 6.7 %copy-start.9 = (bf16[384,256]{1,0:T(8,128)(2,1)S(1)}, bf16[384,256]{1,0:T(8,128)(2,1)}, u32[]{:S(2)}) copy-start(bf16[384,256]{1,0:T(8,128)(2,1)} %lateral_ref.1) | copy-start | bytes 589828
  24.2 6.7 %copy-start.13 = (f32[384]{0:T(512)S(1)}, f32[384]{0:T(512)}, u32[]{:S(2)}) copy-start(f32[384]{0:T(512)} %second_ref.1) | copy-start | bytes 4612
  24.2 6.6 %collective-permute-start.3 = (bf16[10,16,384]{2,1,0:T(8,128)(2,1)S(1)}, bf16[10,16,384]{2,1,0:T(8,128)(2,1)S(1)}, u32[]{:S(2)}, u32[]{:S(2)}) collective-permute-start(bf16[10,16,384]{2,1,0:T(8,128)(2,1)S(1)} %pad_maximum_fusion.1), channel_id=1, source_target_pairs={{1,0},{2,1},{3,2},{5,4},{6,5},{7,6},{9,8},{10,9},{11,10},{13,12},{... | collective-permute-start | bytes 368648 | tf_op jit(solution)/shard_map/ppermute | solution.py:695
  28.2 12.3 %slice-start = ((s8[4718592]{0:T(1024)(128)(4,1)}), s8[4194304]{0:T(1024)(128)(4,1)S(1)}, s32[]{:S(2)}) async-start(s8[4718592]{0:T(1024)(128)(4,1)} %bitcast), calls=%async_computation | async-start | bytes 8388608
  31.0 9.5 %slice-start.1 = ((s8[4718592]{0:T(1024)(128)(4,1)}), s8[524288]{0:T(1024)(128)(4,1)S(1)}, s32[]{:S(2)}) async-start(s8[4718592]{0:T(1024)(128)(4,1)} %bitcast), calls=%async_computation.1 | async-start | bytes 1048576
  31.0 9.5 %copy-start.17 = (s32[1,1,16]{2,1,0:T(1,128)S(1)}, s32[1,1,16]{2,1,0:T(1,128)}, u32[]{:S(2)}) copy-start(s32[1,1,16]{2,1,0:T(1,128)} %owner_ref.1) | copy-start | bytes 196
  31.0 9.5 %copy-start.18 = (bf16[256]{0:T(256)(128)(2,1)S(1)}, bf16[256]{0:T(256)(128)(2,1)}, u32[]{:S(2)}) copy-start(bf16[256]{0:T(256)(128)(2,1)} %mask_ref.3) | copy-start | bytes 1540
  40.5 52.6 %copy-start.16 = (bf16[1,1,16,196]{3,2,1,0:T(8,128)(2,1)S(1)}, bf16[1,1,16,196]{3,2,1,0:T(8,128)(2,1)}, u32[]{:S(2)}) copy-start(bf16[1,1,16,196]{3,2,1,0:T(8,128)(2,1)} %soft_ref.1) | copy-start | bytes 18820

commit v3 on v2

--- a/solution.py
+++ b/solution.py
@@ -8,6 +8,8 @@
 
 CROP = 14
 ROWS = 2
+FORWARD_MIB = 16
+BACKWARD_MIB = 20
 PAD = CROP + 2
 GELU_A = 0.7978845608028654
 GELU_B = 0.044715
@@ -63,11 +65,13 @@
 
 def chain(product, finish, before_ref, stages):
     late = None
-    for number, (layer, source, target) in enumerate(stages):
-        before = before_ref.at[number % 2]
+    count = 0
+    for layer, source, target in stages:
         for begin in range(0, CROP, ROWS):
             end = min(begin + ROWS, CROP)
-            before[begin:end] = product(layer, source, begin, end).reshape(
+            before = before_ref.at[count % before_ref.shape[0]]
+            count += 1
+            before[: end - begin] = product(layer, source, begin, end).reshape(
                 (end - begin,) + before.shape[1:]
             )
             if late is not None:
@@ -89,16 +93,16 @@
     clear_border(b_ref)
     shape = (boxes, boxes * tile_cols)
     lane = lax.broadcasted_iota(jnp.int32, shape, 1)
-    start = box_columns([geom_ref[0, 0, n, 1] for n in range(boxes)], shape, 0)
-    width = box_columns([geom_ref[0, 0, n, 3] for n in range(boxes)], shape, 0)
+    start = box_columns([geom_ref[0, 0, 1, n] for n in range(boxes)], shape, 0)
+    width = box_columns([geom_ref[0, 0, 3, n] for n in range(boxes)], shape, 0)
     mine = lane // tile_cols == lax.broadcasted_iota(jnp.int32, shape, 0)
     away = jnp.where(mine, lane % tile_cols - start, -1)
     away = jnp.where(away < width, away, -1)
     for v in range(CROP):
         pick_ref[v * boxes : (v + 1) * boxes, :] = (away == v).astype(jnp.bfloat16)
     for n in range(boxes):
-        rows = features_ref[pl.ds(geom_ref[0, 0, n, 0], CROP)]
-        tall = jnp.where(n < count, geom_ref[0, 0, n, 2], 0)
+        rows = features_ref[pl.ds(geom_ref[0, 0, 0, n], CROP)]
+        tall = jnp.where(n < count, geom_ref[0, 0, 2, n], 0)
         for u in range(CROP):
             strip_ref[u, n] = jnp.where(u < tall, rows[u], jnp.zeros_like(rows[u]))
     for u in range(CROP):
@@ -118,7 +122,7 @@
         for u in range(begin, end):
             for v in range(CROP):
                 piece = slice(v * boxes, (v + 1) * boxes)
-                value, slope = gelu_parts(before[u, piece])
+                value, slope = gelu_parts(before[u - begin, piece])
                 slope_ref[layer, u, piece] = slope.astype(jnp.bfloat16)
                 target[u + 1, 1 + v] = value.astype(jnp.bfloat16)
 
@@ -156,14 +160,14 @@
     count = count_ref[0, 0]
     clear_border(a_ref)
     clear_border(b_ref)
-    broad = [geom_ref[0, 0, n, 3] for n in range(boxes)]
-    tall = [jnp.where(n < count, geom_ref[0, 0, n, 2], 0) for n in range(boxes)]
+    broad = [geom_ref[0, 0, 3, n] for n in range(boxes)]
+    tall = [jnp.where(n < count, geom_ref[0, 0, 2, n], 0) for n in range(boxes)]
     lane = lax.broadcasted_iota(jnp.int32, (tile_cols, lanes), 1)
     cell = lax.broadcasted_iota(jnp.int32, (tile_cols, lanes), 0)
     box, col = lane % boxes, lane // boxes
     for n in range(boxes):
         place_ref[n * tile_cols : (n + 1) * tile_cols, :] = (
-            (cell == col + geom_ref[0, 0, n, 1]) & (box == n) & (col < broad[n])
+            (cell == col + geom_ref[0, 0, 1, n]) & (box == n) & (col < broad[n])
         ).astype(jnp.bfloat16)
     shape = (boxes, cells)
     where = lax.broadcasted_iota(jnp.int32, shape, 1)
@@ -200,7 +204,7 @@
                 piece = slice(v * boxes, (v + 1) * boxes)
                 slope = slope_ref[jnp.maximum(layer - 1, 0), u, piece].astype(jnp.float32)
                 slope = jnp.where(first, 1.0, slope)
-                target[u + 1, 1 + v] = (before[u, piece] * slope).astype(jnp.bfloat16)
+                target[u + 1, 1 + v] = (before[u - begin, piece] * slope).astype(jnp.bfloat16)
 
     def down(pair, carry):
         layer = layers - 1 - 2 * pair
@@ -218,24 +222,49 @@
     grad_ref[...] = jnp.zeros_like(grad_ref)
     for n in range(boxes):
         kept = lax.broadcasted_iota(jnp.int32, (CROP, 1, 1), 0) < tall[n]
-        rows = pl.ds(geom_ref[0, 0, n, 0], CROP)
+        rows = pl.ds(geom_ref[0, 0, 0, n], CROP)
         grad_ref[rows] = grad_ref[rows] + jnp.where(kept, spread_ref[:, n], 0.0)
 
 
-def collect_kernel(sent_ref, out_ref):
-    boxes = sent_ref.shape[0]
+def pair_kernel(own_ref, other_ref, out_ref):
+    boxes = own_ref.shape[0]
+    second = lax.axis_index("row") % 2
+    out_ref[pl.ds(pl.multiple_of(second * boxes, boxes), boxes)] = own_ref[...]
+    out_ref[pl.ds(pl.multiple_of((1 - second) * boxes, boxes), boxes)] = other_ref[...]
+
+
+def join_pair(own, other):
+    return pl.pallas_call(
+        pair_kernel,
+        out_shape=jax.ShapeDtypeStruct((2 * own.shape[0], own.shape[1]), own.dtype),
+        in_specs=[VMEM, VMEM],
+        out_specs=VMEM,
+        compiler_params=pltpu.CompilerParams(vmem_limit_bytes=4 * 2**20),
+        name="join_pair",
+    )(own, other)
+
+
+def collect_kernel(*refs):
+    blocks, out_ref = refs[:-2], refs[-1]
     keep, cells = out_ref.shape[2:]
-    owner = sent_ref[:, cells : cells + 1]
-    mine = (owner == lax.axis_index("row").astype(jnp.float32)).astype(jnp.float32)
-    row = lax.broadcasted_iota(jnp.int32, (boxes, boxes), 0)
-    col = lax.broadcasted_iota(jnp.int32, (boxes, boxes), 1)
-    earlier = (col < row).astype(jnp.float32).astype(jnp.bfloat16)
-    many = jnp.broadcast_to(mine, (boxes, 128)).astype(jnp.bfloat16)
+    pairs, rows = len(blocks), blocks[0].shape[0]
+    sent = jnp.concatenate([ref[...] for ref in blocks], axis=0)
+    me = lax.axis_index("row")
+    mine = (sent[:, cells : cells + 1] == me.astype(jnp.float32)).astype(jnp.float32)
+
+    def order(axis):
+        index = lax.broadcasted_iota(jnp.int32, (pairs * rows, pairs * rows), axis)
+        source = me // 2 - index // rows
+        source = jnp.where(source < 0, source + pairs, source)
+        return source * rows + index % rows
+
+    earlier = (order(1) < order(0)).astype(jnp.float32).astype(jnp.bfloat16)
+    many = jnp.broadcast_to(mine, (pairs * rows, 128)).astype(jnp.bfloat16)
     position = jnp.dot(earlier, many, preferred_element_type=jnp.float32)[:, :keep]
-    slot = lax.broadcasted_iota(jnp.int32, (boxes, keep), 1).astype(jnp.float32)
+    slot = lax.broadcasted_iota(jnp.int32, (pairs * rows, keep), 1).astype(jnp.float32)
     picker = jnp.where(position == slot, mine, 0.0)
     out_ref[0, 0] = lax.dot_general(
-        picker, sent_ref[:, :cells], TN, precision=HIGHEST, preferred_element_type=jnp.float32
+        picker, sent[:, :cells], TN, precision=HIGHEST, preferred_element_type=jnp.float32
     )
 
 
@@ -245,7 +274,7 @@
 
 def mask_forward(features, geometry, count, owner, weight, mask):
     tile_rows, tile_cols, channels = features.shape
-    boxes = geometry.shape[2]
+    boxes = geometry.shape[3]
     layers = weight.shape[0]
     lanes = CROP * boxes
     padded = pltpu.VMEM((PAD, PAD, boxes, channels), jnp.bfloat16)
@@ -262,9 +291,9 @@
             padded,
             pltpu.VMEM((CROP, boxes, tile_cols, channels), jnp.bfloat16),
             pltpu.VMEM((lanes, boxes * tile_cols), jnp.bfloat16),
-            pltpu.VMEM((2, CROP, lanes, channels), jnp.float32),
+            pltpu.VMEM((3, ROWS, lanes, channels), jnp.float32),
         ],
-        compiler_params=pltpu.CompilerParams(vmem_limit_bytes=32 * 2**20),
+        compiler_params=pltpu.CompilerParams(vmem_limit_bytes=FORWARD_MIB * 2**20),
         cost_estimate=mask_cost(weight),
         name="mask_forward",
     )(geometry, count, owner, features, weight, mask)
@@ -272,7 +301,7 @@
 
 def mask_backward(send, soft, slope, geometry, count, weight, mask, tile):
     layers, _, lanes, channels = slope.shape
-    boxes = geometry.shape[2]
+    boxes = geometry.shape[3]
     padded = pltpu.VMEM((PAD, PAD, boxes, channels), jnp.bfloat16)
     return pl.pallas_call(
         backward_kernel,
@@ -284,23 +313,23 @@
             padded,
             pltpu.VMEM((CROP, boxes, tile[1], channels), jnp.float32),
             pltpu.VMEM((boxes * tile[1], lanes), jnp.bfloat16),
-            pltpu.VMEM((2, CROP, lanes, channels), jnp.float32),
+            pltpu.VMEM((3, ROWS, lanes, channels), jnp.float32),
         ],
-        compiler_params=pltpu.CompilerParams(vmem_limit_bytes=38 * 2**20),
+        compiler_params=pltpu.CompilerParams(vmem_limit_bytes=BACKWARD_MIB * 2**20),
         cost_estimate=mask_cost(weight),
         name="mask_backward",
     )(geometry, count, send, soft, slope, weight, mask)
 
 
-def collect(sent, keep, cells):
+def collect(blocks, after, keep, cells):
     return pl.pallas_call(
         collect_kernel,
         out_shape=jax.ShapeDtypeStruct((1, 1, keep, cells), jnp.float32),
-        in_specs=[VMEM],
+        in_specs=[VMEM] * len(blocks) + [pl.BlockSpec(memory_space=pl.ANY)],
         out_specs=VMEM,
         compiler_params=pltpu.CompilerParams(vmem_limit_bytes=8 * 2**20),
         name="collect",
-    )(sent)
+    )(*blocks, after)
 
 
 HEADS = 12
@@ -372,28 +401,12 @@
 
 
 def joint_kernel(
-    tokens_ref, gain_ref, joint_ref, relative_ref,
-    out_ref, bias_ref, ordered_ref, north_ref, south_ref, west_ref, east_ref, order_ref,
+    tokens_ref, gain_ref, joint_ref,
+    out_ref, ordered_ref, west_ref, east_ref, order_ref,
 ):
     cells_down, cells_across, _, model = ordered_ref.shape
     strip = order_ref.shape[0]
     order_ref[...] = strip_order(strip // SUB)
-    place = window_order()
-    turned = lax.dot_general(
-        relative_ref[...].reshape(-1, AREA), place, NT,
-        precision=HIGHEST, preferred_element_type=jnp.float32,
-    )
-    for group in range(HEADS // GROUP):
-        rows = [
-            turned[(group * GROUP + h) * AREA : (group * GROUP + h + 1) * AREA]
-            for h in range(GROUP)
-        ]
-        bias_ref[group] = jnp.dot(
-            place,
-            jnp.concatenate(rows, axis=1),
-            precision=HIGHEST,
-            preferred_element_type=jnp.float32,
-        )
     gain = gain_ref[...].reshape(1, model)
 
     def body(step, carry):
@@ -417,13 +430,27 @@
         return carry
 
     lax.fori_loop(0, cells_down // 2, body, 0)
-    north_ref[...] = ordered_ref[0]
-    south_ref[...] = ordered_ref[cells_down - 1]
     west_ref[...] = ordered_ref[:, 0]
     east_ref[...] = ordered_ref[:, cells_across - 1]
 
 
-def inner_kernel(joint_ref, bias_ref, out_ref):
+def inner_kernel(joint_ref, relative_ref, after_ref, out_ref, bias_ref):
+    place = window_order()
+    turned = lax.dot_general(
+        relative_ref[...].reshape(-1, AREA), place, NT,
+        precision=HIGHEST, preferred_element_type=jnp.float32,
+    )
+    for group in range(HEADS // GROUP):
+        rows = [
+            turned[(group * GROUP + h) * AREA : (group * GROUP + h + 1) * AREA]
+            for h in range(GROUP)
+        ]
+        bias_ref[group] = jnp.dot(
+            place,
+            jnp.concatenate(rows, axis=1),
+            precision=HIGHEST,
+            preferred_element_type=jnp.float32,
+        )
     cells_down, cells_across, _, triple = joint_ref.shape
     model = triple // 3
     blocks = head_blocks(GROUP * model // HEADS)
@@ -439,6 +466,36 @@
         return carry
 
     lax.fori_loop(0, cells_down // 2 - 1, body, 0)
+
+
+def lengthen_kernel(
+    up_ref, down_ref, west_ref, east_ref, up_out_ref, down_out_ref, west_out_ref, east_out_ref
+):
+    width = up_ref.shape[1]
+    order = strip_order(width)
+    for source, target in ((up_ref, up_out_ref), (down_ref, down_out_ref)):
+        ordered = jnp.dot(
+            order, source[...].reshape(SUB * width, -1), preferred_element_type=jnp.float32
+        )
+        target[...] = ordered.astype(jnp.bfloat16).reshape(target.shape)
+    last = up_out_ref.shape[0] - 1
+    for cell, own, out in ((0, west_ref, west_out_ref), (last, east_ref, east_out_ref)):
+        out[0] = up_out_ref[cell]
+        out[1:-1] = own[...]
+        out[out.shape[0] - 1] = down_out_ref[cell]
+
+
+def lengthen(up, down, west, east):
+    across = jax.ShapeDtypeStruct((up.shape[1] // SUB, CELL, up.shape[2]), up.dtype)
+    out = jax.ShapeDtypeStruct((west.shape[0] + 2,) + west.shape[1:], west.dtype)
+    return pl.pallas_call(
+        lengthen_kernel,
+        out_shape=(across, across, out, out),
+        in_specs=[VMEM] * 4,
+        out_specs=(VMEM,) * 4,
+        compiler_params=params(8),
+        name="lengthen",
+    )(up, down, west, east)
 
 
 def hidden_keys(down_side, down_edge, across_side, across_edge):
@@ -610,7 +667,7 @@
     return jax.ShapeDtypeStruct((count_down, count_across, CELL, channels), dtype)
 
 
-def joint_rows(tokens, gain, weight, relative):
+def joint_rows(tokens, gain, weight):
     tile_rows, tile_cols, model = tokens.shape
     down, across = tile_rows // SUB, tile_cols // SUB
     lone = lambda n: jax.ShapeDtypeStruct((n, CELL, model), jnp.bfloat16)
@@ -618,33 +675,37 @@
         joint_kernel,
         out_shape=(
             cells_of(down, across, weight.shape[1]),
-            jax.ShapeDtypeStruct((HEADS // GROUP, AREA, GROUP * AREA), jnp.float32),
             cells_of(down, across, model),
-            lone(across), lone(across), lone(down), lone(down),
+            lone(down), lone(down),
         ),
-        in_specs=[VMEM] * 4,
-        out_specs=(VMEM,) * 7,
-        scratch_shapes=[pltpu.VMEM((SUB * tile_cols, SUB * tile_cols), jnp.bfloat16)],
+        in_specs=[VMEM] * 3,
+        out_specs=(VMEM,) * 4,
+        scratch_shapes=[
+            pltpu.VMEM((SUB * tile_cols, SUB * tile_cols), jnp.bfloat16),
+        ],
         compiler_params=params(20),
         cost_estimate=cost(tokens.shape[0] * tile_cols, model * weight.shape[1]),
         name="joint_rows",
-    )(tokens, gain, weight, relative)
+    )(tokens, gain, weight)
 
 
 def cost(rows, weights):
     return pl.CostEstimate(flops=4 * rows * weights, bytes_accessed=4 * 2**20, transcendentals=0)
 
 
-def inner_windows(joint, bias):
+def inner_windows(joint, relative, after):
     return pl.pallas_call(
         inner_kernel,
-        out_shape=jax.ShapeDtypeStruct(joint.shape[:3] + (joint.shape[3] // 3,), jnp.bfloat16),
-        in_specs=[VMEM] * 2,
-        out_specs=VMEM,
+        out_shape=(
+            jax.ShapeDtypeStruct(joint.shape[:3] + (joint.shape[3] // 3,), jnp.bfloat16),
+            jax.ShapeDtypeStruct((HEADS // GROUP, AREA, GROUP * AREA), jnp.float32),
+        ),
+        in_specs=[VMEM, VMEM, pl.BlockSpec(memory_space=pl.ANY)],
+        out_specs=(VMEM, VMEM),
         compiler_params=params(20),
         cost_estimate=cost(joint.shape[0] * joint.shape[1] * CELL, 2**19),
         name="inner_windows",
-    )(joint, bias)
+    )(joint, relative, after)
 
 
 def end_windows(joint, up, down, bias, gain, weight):
@@ -701,28 +762,34 @@
     soft_target,
 ):
     tile_rows, tile_cols, model = tokens.shape
-    joint, bias, ordered, north, south, west, east = joint_rows(
-        tokens, first_gain, joint_weight, relative_bias
-    )
-    up = shift(south, "row", 1)
-    down = shift(north, "row", -1)
-    inner = inner_windows(joint, bias)
-    left = shift(jnp.concatenate([up[-1:], east, down[-1:]], axis=0), "col", 1)
-    right = shift(jnp.concatenate([up[:1], west, down[:1]], axis=0), "col", -1)
+    up = shift(tokens[-SUB:], "row", 1)
+    down = shift(tokens[:SUB], "row", -1)
+    joint, ordered, west, east = joint_rows(tokens, first_gain, joint_weight)
+    up, down, west, east = lengthen(up, down, west, east)
+    left = shift(east, "col", 1)
+    right = shift(west, "col", -1)
+    inner, bias = inner_windows(joint, relative_bias, west)
     pairs, ends = end_windows(joint, up, down, bias, first_gain, joint_weight)
     features, features_here = side_windows(
         ordered, joint, inner, pairs, ends, left, right, bias, (first_gain, second_gain),
         (joint_weight, merge_weight, expand_weight, shrink_weight, lateral_weight),
     )
+    rows_size = lax.axis_size("row")
+    geometry = box_geometry.transpose(0, 1, 3, 2)
     send, slope = mask_forward(
-        features_here, box_geometry, box_counts, box_owner, conv_weight, mask_weight
-    )
-    sent = lax.all_gather(send, "row", axis=0, tiled=True)
+        features_here, geometry, box_counts, box_owner, conv_weight, mask_weight
+    )
+    both = join_pair(send, lax.ppermute(send, "row", [(i, i ^ 1) for i in range(rows_size)]))
+    blocks = [both]
+    for back in range(2, rows_size, 2):
+        blocks.append(
+            lax.ppermute(both, "row", [(i, (i + back) % rows_size) for i in range(rows_size)])
+        )
     feature_grad = mask_backward(
-        send, soft_target, slope, box_geometry, box_counts, conv_weight, mask_weight,
+        send, soft_target, slope, geometry, box_counts, conv_weight, mask_weight,
         (tile_rows, tile_cols),
     )
-    return features, feature_grad, collect(sent, BOX_OWN, CROP * CROP)
+    return features, feature_grad, collect(blocks, feature_grad, BOX_OWN, CROP * CROP)
 
 
 def solution(mesh):

time: 114 us -> 87.2 us (0.76)
  blocking collectives: 31.4 us -> 0 us
  starting transfers between devices: 11.1 us -> 18.5 us
  Pallas kernels: 60.4 us -> 59 us
    all_gather x1 -> x0, blocking collectives: 31.4 us -> none  [shards(): sent = lax.all_gather(send, 'row', axis=0, tiled=True)]
    ppermute x0 -> x4, starting transfers between devices: none -> 7.07 us  [the longest x3 4.61 us: shards(): lax.ppermute(both, 'row', [(i, (i + back) % rows_size) for i in range(row...]
    ppermute x0 -> x4, waiting for transfers between devices: none -> 1.73 us  [the longest x1 1.72 us: shards(): lax.ppermute(send, 'row', [(i, i ^ 1) for i in range(rows_size)])]
    pallas_call x1, Pallas kernels: 5.09 us -> 3.38 us  [joint_rows(): pl.pallas_call(joint_kernel, out_shape=(cells_of(down, across, weight.sha...]
    pallas_call x1 -> x3, Pallas kernels: 2.14 us -> 3.38 us  [the longest x1 3.17 us: inner_windows(): pl.pallas_call(inner_kernel, out_shape=(jax.ShapeDtypeStruct(joint.shape[...]
    unnamed x45 -> x36, local copies, waits for them, and re-layouts: 5.06 us -> 4.53 us
  transfers between devices with their start and end apart: 4 -> 8, of which waited for: 1 -> 1; matrix products, arithmetic and copies ran while one was open for 1% -> 0% of each run, Pallas kernels for 4% -> 33%
where the time goes in v3:
time: 87.2 us; the launch traced here: 86.3 us
  Pallas kernels  59 us (68%)
  starting transfers between devices  18.5 us (21%)
  local copies, waits for them, and re-layouts  5.49 us (6%)
  waiting for transfers between devices  1.74 us (2%)
  between operations  1.55 us (2%)
    pallas_call x1, Pallas kernels, mask_forward(): pl.pallas_call(forward_kernel, out_shape=(jax.ShapeDtypeStruct((boxes, 25...  20.2 us
    pallas_call x1, Pallas kernels, mask_backward(): pl.pallas_call(backward_kernel, out_shape=jax.ShapeDtypeStruct(tile + (ch...  19.9 us
    ppermute x4, starting transfers between devices, shift(): return lax.ppermute(x, axis, pairs)  11.4 us
    pallas_call x1, Pallas kernels, side_windows(): pl.pallas_call(sides_kernel, out_shape=(tile, tile), in_specs=[VMEM] * 15...  9.48 us
    ppermute x3, starting transfers between devices, shards(): lax.ppermute(both, 'row', [(i, (i + back) % rows_size) for i in range(row...  4.61 us
    unnamed x36, local copies, waits for them, and re-layouts  4.53 us
    pallas_call x1, Pallas kernels, joint_rows(): pl.pallas_call(joint_kernel, out_shape=(cells_of(down, across, weight.sha...  3.38 us
    pallas_call x1, Pallas kernels, inner_windows(): pl.pallas_call(inner_kernel, out_shape=(jax.ShapeDtypeStruct(joint.shape[...  3.17 us
  transfers between devices with their start and end apart: 8, of which 1 were waited for; matrix products, arithmetic and copies ran while one was open for 0% of the time, Pallas kernels for 33%

profile of v3, /device:TPU:4, one launch (start us, length us, event | category | flops | bytes accessed | tf_op | source)
XLA Modules:
  0.0 86.3 jit_solution(5110855704503482315)
XLA Ops:
  0.6 1.0 %fusion = (bf16[4,32,384]{2,1,0:T(8,128)(2,1)S(1)}, bf16[4,32,384]{2,1,0:T(8,128)(2,1)S(1)}) fusion(bf16[32,32,384]{2,1,0:T(8,128)(2,1)} %tokens_ref.1), kind=kLoop, calls=%fused_computation | loop fusion | bytes 393216 | tf_op jit(solution)/shard_map/slice | solution.py:766
  1.6 1.3 %collective-permute-start.1 = (bf16[4,32,384]{2,1,0:T(8,128)(2,1)S(1)}, bf16[4,32,384]{2,1,0:T(8,128)(2,1)S(1)}, u32[]{:S(2)}, u32[]{:S(2)}) collective-permute-start(bf16[4,32,384]{2,1,0:T(8,128)(2,1)S(1)} %get-tuple-element.35), channel_id=1, source_target_pairs={{4,0},{8,4},{12,8},{16,12},{20,16},{24,20},{28,24},{5,1},{9,5},{13... | collective-permute-start | bytes 294920 | tf_op jit(solution)/shard_map/ppermute | solution.py:756
  2.9 4.6 %collective-permute-start = (bf16[4,32,384]{2,1,0:T(8,128)(2,1)S(1)}, bf16[4,32,384]{2,1,0:T(8,128)(2,1)S(1)}, u32[]{:S(2)}, u32[]{:S(2)}) collective-permute-start(bf16[4,32,384]{2,1,0:T(8,128)(2,1)S(1)} %get-tuple-element.36), channel_id=1, source_target_pairs={{0,4},{4,8},{8,12},{12,16},{16,20},{20,24},{24,28},{1,5},{5,9},{9,... | collective-permute-start | bytes 294920 | tf_op jit(solution)/shard_map/ppermute | solution.py:756
  8.1 0.0 copy-start.3
  8.1 1.2 %copy-done.3 = bf16[384,1152]{1,0:T(8,128)(2,1)S(1)} copy-done((bf16[384,1152]{1,0:T(8,128)(2,1)S(1)}, bf16[384,1152]{1,0:T(8,128)(2,1)}, u32[]{:S(2)}) %copy-start.3) | copy-done | bytes 884760
  9.3 1.1 %copy-done.7 = bf16[32,32,384]{2,1,0:T(8,128)(2,1)S(1)} copy-done((bf16[32,32,384]{2,1,0:T(8,128)(2,1)S(1)}, bf16[32,32,384]{2,1,0:T(8,128)(2,1)}, u32[]{:S(2)}) %copy-start.7) | copy-done | bytes 786456
  10.4 0.7 copy-done.8
  11.1 3.4 %joint_rows.1 = (bf16[8,8,16,1152]{3,2,1,0:T(8,128)(2,1)S(1)}, bf16[8,8,16,384]{3,2,1,0:T(8,128)(2,1)S(1)}, bf16[8,16,384]{2,1,0:T(8,128)(2,1)S(1)}, bf16[8,16,384]{2,1,0:T(8,128)(2,1)S(1)}) custom-call(bf16[32,32,384]{2,1,0:T(8,128)(2,1)S(1)} %copy-done.7, f32[384]{0:T(512)S(1)} %copy-done.8, bf16[384,1152]{1,0:T(8,128)(2,1)S(1)} %copy-done.3), custom_call_target="tpu_custom_call" | custom-call | flops 1811939328 | bytes 4194304 | tf_op jit(solution)/shard_map/joint_rows/pallas_call | solution.py:674
  14.5 0.0 collective-permute-done.1.down_ref
  14.5 0.0 collective-permute-done.up_ref
  14.5 0.2 lengthen.1
  14.7 1.9 %collective-permute-start.2 = (bf16[10,16,384]{2,1,0:T(8,128)(2,1)S(1)}, bf16[10,16,384]{2,1,0:T(8,128)(2,1)S(1)}, u32[]{:S(2)}, u32[]{:S(2)}) collective-permute-start(bf16[10,16,384]{2,1,0:T(8,128)(2,1)S(1)} %get-tuple-element.30), channel_id=1, source_target_pairs={{0,1},{1,2},{2,3},{4,5},{5,6},{6,7},{8,9},{9,10},{10,11},{12,13},{... | collective-permute-start | bytes 368648 | tf_op jit(solution)/shard_map/ppermute | solution.py:756
  16.6 3.6 %collective-permute-start.3 = (bf16[10,16,384]{2,1,0:T(8,128)(2,1)S(1)}, bf16[10,16,384]{2,1,0:T(8,128)(2,1)S(1)}, u32[]{:S(2)}, u32[]{:S(2)}) collective-permute-start(bf16[10,16,384]{2,1,0:T(8,128)(2,1)S(1)} %get-tuple-element.23.after_ref), channel_id=1, source_target_pairs={{1,0},{2,1},{3,2},{5,4},{6,5},{7,6},{9,8},{10,9},{11,10},{13,12},{... | collective-permute-start | bytes 368648 | tf_op jit(solution)/shard_map/ppermute | solution.py:756
  20.3 0.0 copy-done.11
  20.3 3.2 %inner_windows.1 = (bf16[8,8,16,384]{3,2,1,0:T(8,128)(2,1)S(1)}, f32[3,64,256]{2,1,0:T(8,128)S(1)}) custom-call(bf16[8,8,16,1152]{3,2,1,0:T(8,128)(2,1)S(1)} %get-tuple-element.20.joint_ref.joint_out_ref, f32[12,64,64]{2,1,0:T(8,128)S(1)} %copy-done.11, bf16[10,16,384]{2,1,0:T(8,128)(2,1)S(1)} %get-tuple-element.23.after_ref), custom_call_target="tpu_custom_call" | custom-call | flops 2147483648 | bytes 4194304 | tf_op jit(solution)/shard_map/inner_windows/pallas_call | solution.py:697
  23.5 0.0 copy-start
  23.5 0.0 copy-start.1
  23.5 0.0 copy-start.4
  23.5 0.0 copy-start.5
  23.5 0.0 copy-start.6
  23.5 0.0 copy-start.9
  23.5 0.0 copy-start.10
  23.6 0.0 slice-start
  23.6 1.6 %end_windows.1 = (bf16[2,8,16,768]{3,2,1,0:T(8,128)(2,1)S(1)}, bf16[2,8,16,384]{3,2,1,0:T(8,128)(2,1)S(1)}) custom-call(bf16[8,8,16,1152]{3,2,1,0:T(8,128)(2,1)S(1)} %get-tuple-element.20.joint_ref.joint_out_ref, bf16[8,16,384]{2,1,0:T(8,128)(2,1)S(1)} %get-tuple-element.25.up_ref, bf16[8,16,384]{2,1,0:T(8,128)(2,1)S(1)} %get-tuple-element.26.down_ref, ...), custom_call_target="tpu_custom_call" | custom-call | flops 2147483648 | bytes 4194304 | tf_op jit(solution)/shard_map/end_windows/pallas_call | solution.py:713
  25.2 0.0 collective-permute-done.2.left_ref
  25.2 0.0 collective-permute-done.3.right_ref
  25.2 0.0 copy-done
  25.2 0.0 copy-done.1
  25.2 0.1 copy-done.4
  25.4 0.1 copy-done.5
  25.4 0.1 copy-done.6
  25.5 0.0 copy-start.14
  25.5 0.0 copy-start.15
  25.5 9.5 %side_windows.1 = (bf16[32,32,256]{2,1,0:T(8,128)(2,1)}, bf16[32,32,256]{2,1,0:T(8,128)(2,1)S(1)}) custom-call(bf16[8,8,16,384]{3,2,1,0:T(8,128)(2,1)S(1)} %get-tuple-element.19.ordered_ref, bf16[8,8,16,1152]{3,2,1,0:T(8,128)(2,1)S(1)} %get-tuple-element.20.joint_ref.joint_out_ref, bf16[8,8,16,384]{3,2,1,0:T(8,128)(2,1)S(1)} %get-tuple-element.24.inner_ref, ...), custom_call_target="tpu_custom_call" | custom-call | tf_op jit(solution)/shard_map/side_windows/pallas_call | solution.py:731
  35.0 0.0 copy-start.12
  35.0 20.2 %mask_forward.1 = (f32[16,256]{1,0:T(8,128)S(1)}, bf16[4,14,224,256]{3,2,1,0:T(8,128)(2,1)S(1)}) custom-call(s32[1,1,4,16]{3,2,1,0:T(4,128)S(1)} %bitcast.3, s32[1,1]{1,0:T(1,128)S(6)} %copy.18.count_ref, s32[1,1,16]{2,1,0:T(1,128)S(1)} %copy-done.14, bf16[32,32,256]{2,1,0:T(8,128)(2,1)S(1)} %get-tuple-element.32.features_ref, ...), custom_call_target="tpu_custom_call" | custom-call | flops 24999999488 | bytes 4718592 | tf_op jit(solution)/shard_map/mask_forward/pallas_call | solution.py:281
  55.3 2.5 %collective-permute-start.4 = (f32[16,256]{1,0:T(8,128)S(1)}, f32[16,256]{1,0:T(8,128)S(1)}, u32[]{:S(2)}, u32[]{:S(2)}) collective-permute-start(f32[16,256]{1,0:T(8,128)S(1)} %get-tuple-element.33.send_ref.own_ref), channel_id=1, source_target_pairs={{0,4},{4,0},{8,12},{12,8},{16,20},{20,16},{24,28},{28,24},{1,5},{5... | collective-permute-start | bytes 49160 | tf_op jit(solution)/shard_map/ppermute | solution.py:782
  57.7 1.7 %collective-permute-done.4.other_ref = f32[16,256]{1,0:T(8,128)S(1)} collective-permute-done((f32[16,256]{1,0:T(8,128)S(1)}, f32[16,256]{1,0:T(8,128)S(1)}, u32[]{:S(2)}, u32[]{:S(2)}) %collective-permute-start.4) | collective-permute-done | bytes 16416 | tf_op jit(solution)/shard_map/ppermute | solution.py:782
  59.4 3.2 %collective-permute-start.7 = (f32[32,256]{1,0:T(8,128)S(1)}, f32[32,256]{1,0:T(8,128)S(1)}, u32[]{:S(2)}, u32[]{:S(2)}) collective-permute-start(f32[32,256]{1,0:T(8,128)S(1)} %join_pair.1.refs_0_), channel_id=1, source_target_pairs={{0,24},{4,28},{8,0},{12,4},{16,8},{20,12},{24,16},{28,20},{1,25},{... | collective-permute-start | bytes 98312 | tf_op jit(solution)/shard_map/ppermute | solution.py:786
  62.7 0.0 collective-permute-start.6
  62.7 1.4 %collective-permute-start.5 = (f32[32,256]{1,0:T(8,128)S(1)}, f32[32,256]{1,0:T(8,128)S(1)}, u32[]{:S(2)}, u32[]{:S(2)}) collective-permute-start(f32[32,256]{1,0:T(8,128)S(1)} %join_pair.1.refs_0_), channel_id=1, source_target_pairs={{0,8},{4,12},{8,16},{12,20},{16,24},{20,28},{24,0},{28,4},{1,9},{5... | collective-permute-start | bytes 98312 | tf_op jit(solution)/shard_map/ppermute | solution.py:786
  64.0 19.9 %mask_backward.1.refs_4_ = f32[32,32,256]{2,1,0:T(8,128)} custom-call(s32[1,1,4,16]{3,2,1,0:T(4,128)S(1)} %bitcast.4, s32[1,1]{1,0:T(1,128)S(6)} %copy.18.count_ref, f32[16,256]{1,0:T(8,128)S(1)} %get-tuple-element.33.send_ref.own_ref, bf16[1,1,16,196]{3,2,1,0:T(8,128)(2,1)S(1)} %copy-done.12, bf16[4,14,224,256]{3,2,1,0:T(8,128)(2,1)S(1)} %get-tuple-element.34.slope_ref, ...), custom_call_target="tpu_custom_call" | custom-call | flops 24999999488 | bytes 4718592 | tf_op jit(solution)/shard_map/mask_backward/pallas_call | solution.py:306
  84.0 0.0 collective-permute-done.7.refs_3_
  84.0 0.0 collective-permute-done.6.refs_2_
  84.0 0.0 collective-permute-done.5.refs_1_
  84.0 0.0 copy-start.2
  84.0 1.2 %copy-done.2 = f32[32,32,256]{2,1,0:T(8,128)S(1)} copy-done((f32[32,32,256]{2,1,0:T(8,128)S(1)}, f32[32,32,256]{2,1,0:T(8,128)}, u32[]{:S(2)}) %copy-start.2) | copy-done | bytes 1048600
  85.2 1.0 %collect.1 = f32[1,1,8,196]{3,2,1,0:T(8,128)} custom-call(f32[32,256]{1,0:T(8,128)S(1)} %join_pair.1.refs_0_, f32[32,256]{1,0:T(8,128)S(1)} %collective-permute-done.5.refs_1_, f32[32,256]{1,0:T(8,128)S(1)} %collective-permute-done.6.refs_2_, f32[32,256]{1,0:T(8,128)S(1)} %collective-permute-done.7.refs_3_, f32[32,32,256]{2,1,0:T(8,128)S(1)} %copy-done.2), custom_call_target="tpu_custom_call" | custom-call | tf_op jit(solution)/shard_map/collect/pallas_call | solution.py:325
  (15 shorter events, 0.0 us)
Async XLA Ops:
  1.6 12.9 %collective-permute-start.1 = (bf16[4,32,384]{2,1,0:T(8,128)(2,1)S(1)}, bf16[4,32,384]{2,1,0:T(8,128)(2,1)S(1)}, u32[]{:S(2)}, u32[]{:S(2)}) collective-permute-start(bf16[4,32,384]{2,1,0:T(8,128)(2,1)S(1)} %get-tuple-element.35), channel_id=1, source_target_pairs={{4,0},{8,4},{12,8},{16,12},{20,16},{24,20},{28,24},{5,1},{9,5},{13... | collective-permute-start | bytes 294920 | tf_op jit(solution)/shard_map/ppermute | solution.py:756
  2.9 11.6 %collective-permute-start = (bf16[4,32,384]{2,1,0:T(8,128)(2,1)S(1)}, bf16[4,32,384]{2,1,0:T(8,128)(2,1)S(1)}, u32[]{:S(2)}, u32[]{:S(2)}) collective-permute-start(bf16[4,32,384]{2,1,0:T(8,128)(2,1)S(1)} %get-tuple-element.36), channel_id=1, source_target_pairs={{0,4},{4,8},{8,12},{12,16},{16,20},{20,24},{24,28},{1,5},{5,9},{9,... | collective-permute-start | bytes 294920 | tf_op jit(solution)/shard_map/ppermute | solution.py:756
  8.1 1.2 %copy-start.3 = (bf16[384,1152]{1,0:T(8,128)(2,1)S(1)}, bf16[384,1152]{1,0:T(8,128)(2,1)}, u32[]{:S(2)}) copy-start(bf16[384,1152]{1,0:T(8,128)(2,1)} %joint_ref.5) | copy-start | bytes 2654212
  9.3 1.1 %copy-start.7 = (bf16[32,32,384]{2,1,0:T(8,128)(2,1)S(1)}, bf16[32,32,384]{2,1,0:T(8,128)(2,1)}, u32[]{:S(2)}) copy-start(bf16[32,32,384]{2,1,0:T(8,128)(2,1)} %tokens_ref.1) | copy-start | bytes 2359300
  10.4 0.7 copy-start.8
  11.1 9.2 %copy-start.11 = (f32[12,64,64]{2,1,0:T(8,128)S(1)}, f32[12,64,64]{2,1,0:T(8,128)}, u32[]{:S(2)}) copy-start(f32[12,64,64]{2,1,0:T(8,128)} %relative_ref.1) | copy-start | bytes 589828
  14.7 10.5 %collective-permute-start.2 = (bf16[10,16,384]{2,1,0:T(8,128)(2,1)S(1)}, bf16[10,16,384]{2,1,0:T(8,128)(2,1)S(1)}, u32[]{:S(2)}, u32[]{:S(2)}) collective-permute-start(bf16[10,16,384]{2,1,0:T(8,128)(2,1)S(1)} %get-tuple-element.30), channel_id=1, source_target_pairs={{0,1},{1,2},{2,3},{4,5},{5,6},{6,7},{8,9},{9,10},{10,11},{12,13},{... | collective-permute-start | bytes 368648 | tf_op jit(solution)/shard_map/ppermute | solution.py:756
  16.6 8.5 %collective-permute-start.3 = (bf16[10,16,384]{2,1,0:T(8,128)(2,1)S(1)}, bf16[10,16,384]{2,1,0:T(8,128)(2,1)S(1)}, u32[]{:S(2)}, u32[]{:S(2)}) collective-permute-start(bf16[10,16,384]{2,1,0:T(8,128)(2,1)S(1)} %get-tuple-element.23.after_ref), channel_id=1, source_target_pairs={{1,0},{2,1},{3,2},{5,4},{6,5},{7,6},{9,8},{10,9},{11,10},{13,12},{... | collective-permute-start | bytes 368648 | tf_op jit(solution)/shard_map/ppermute | solution.py:756
  23.5 1.7 %copy-start = (bf16[384,1536]{1,0:T(8,128)(2,1)S(1)}, bf16[384,1536]{1,0:T(8,128)(2,1)}, u32[]{:S(2)}) copy-start(bf16[384,1536]{1,0:T(8,128)(2,1)} %expand_ref.1) | copy-start | bytes 3538948
  23.5 1.7 %copy-start.1 = (bf16[1536,384]{1,0:T(8,128)(2,1)S(1)}, bf16[1536,384]{1,0:T(8,128)(2,1)}, u32[]{:S(2)}) copy-start(bf16[1536,384]{1,0:T(8,128)(2,1)} %shrink_ref.1) | copy-start | bytes 3538948
  23.5 1.9 %copy-start.4 = (bf16[384,1152]{1,0:T(8,128)(2,1)S(1)}, bf16[384,1152]{1,0:T(8,128)(2,1)}, u32[]{:S(2)}) copy-start(bf16[384,1152]{1,0:T(8,128)(2,1)} %joint_ref.5) | copy-start | bytes 2654212
  23.5 1.9 %copy-start.5 = (bf16[384,384]{1,0:T(8,128)(2,1)S(1)}, bf16[384,384]{1,0:T(8,128)(2,1)}, u32[]{:S(2)}) copy-start(bf16[384,384]{1,0:T(8,128)(2,1)} %merge_ref.1) | copy-start | bytes 884740
  23.5 1.9 %copy-start.6 = (bf16[384,256]{1,0:T(8,128)(2,1)S(1)}, bf16[384,256]{1,0:T(8,128)(2,1)}, u32[]{:S(2)}) copy-start(bf16[384,256]{1,0:T(8,128)(2,1)} %lateral_ref.1) | copy-start | bytes 589828
  23.5 1.9 %copy-start.9 = (f32[384]{0:T(512)S(1)}, f32[384]{0:T(512)}, u32[]{:S(2)}) copy-start(f32[384]{0:T(512)} %first_ref.1) | copy-start | bytes 4612
  23.5 1.9 %copy-start.10 = (f32[384]{0:T(512)S(1)}, f32[384]{0:T(512)}, u32[]{:S(2)}) copy-start(f32[384]{0:T(512)} %second_ref.1) | copy-start | bytes 4612
  23.6 11.4 %slice-start = ((s8[4718592]{0:T(1024)(128)(4,1)}), s8[4194304]{0:T(1024)(128)(4,1)S(1)}, s32[]{:S(2)}) async-start(s8[4718592]{0:T(1024)(128)(4,1)} %bitcast.1), calls=%async_computation | async-start | bytes 8388608
  25.5 9.5 %slice-start.1 = ((s8[4718592]{0:T(1024)(128)(4,1)}), s8[524288]{0:T(1024)(128)(4,1)S(1)}, s32[]{:S(2)}) async-start(s8[4718592]{0:T(1024)(128)(4,1)} %bitcast.1), calls=%async_computation.1 | async-start | bytes 1048576
  25.5 9.5 %copy-start.13 = (s32[1,1,16,4]{2,3,1,0:T(4,128)S(1)}, s32[1,1,16,4]{2,3,1,0:T(4,128)}, u32[]{:S(2)}) copy-start(s32[1,1,16,4]{2,3,1,0:T(4,128)} %param.26) | copy-start | bytes 772
  25.5 9.5 %copy-start.14 = (s32[1,1,16]{2,1,0:T(1,128)S(1)}, s32[1,1,16]{2,1,0:T(1,128)}, u32[]{:S(2)}) copy-start(s32[1,1,16]{2,1,0:T(1,128)} %owner_ref.1) | copy-start | bytes 196
  25.5 9.5 %copy-start.15 = (bf16[256]{0:T(256)(128)(2,1)S(1)}, bf16[256]{0:T(256)(128)(2,1)}, u32[]{:S(2)}) copy-start(bf16[256]{0:T(256)(128)(2,1)} %mask_ref.3) | copy-start | bytes 1540
  35.0 29.0 %copy-start.12 = (bf16[1,1,16,196]{3,2,1,0:T(8,128)(2,1)S(1)}, bf16[1,1,16,196]{3,2,1,0:T(8,128)(2,1)}, u32[]{:S(2)}) copy-start(bf16[1,1,16,196]{3,2,1,0:T(8,128)(2,1)} %soft_ref.1) | copy-start | bytes 18820
  55.3 4.2 %collective-permute-start.4 = (f32[16,256]{1,0:T(8,128)S(1)}, f32[16,256]{1,0:T(8,128)S(1)}, u32[]{:S(2)}, u32[]{:S(2)}) collective-permute-start(f32[16,256]{1,0:T(8,128)S(1)} %get-tuple-element.33.send_ref.own_ref), channel_id=1, source_target_pairs={{0,4},{4,0},{8,12},{12,8},{16,20},{20,16},{24,28},{28,24},{1,5},{5... | collective-permute-start | bytes 49160 | tf_op jit(solution)/shard_map/ppermute | solution.py:782
  59.4 24.5 %collective-permute-start.7 = (f32[32,256]{1,0:T(8,128)S(1)}, f32[32,256]{1,0:T(8,128)S(1)}, u32[]{:S(2)}, u32[]{:S(2)}) collective-permute-start(f32[32,256]{1,0:T(8,128)S(1)} %join_pair.1.refs_0_), channel_id=1, source_target_pairs={{0,24},{4,28},{8,0},{12,4},{16,8},{20,12},{24,16},{28,20},{1,25},{... | collective-permute-start | bytes 98312 | tf_op jit(solution)/shard_map/ppermute | solution.py:786
  62.7 21.3 %collective-permute-start.6 = (f32[32,256]{1,0:T(8,128)S(1)}, f32[32,256]{1,0:T(8,128)S(1)}, u32[]{:S(2)}, u32[]{:S(2)}) collective-permute-start(f32[32,256]{1,0:T(8,128)S(1)} %join_pair.1.refs_0_), channel_id=1, source_target_pairs={{0,16},{4,20},{8,24},{12,28},{16,0},{20,4},{24,8},{28,12},{1,17},{... | collective-permute-start | bytes 98312 | tf_op jit(solution)/shard_map/ppermute | solution.py:786
  62.7 21.3 %collective-permute-start.5 = (f32[32,256]{1,0:T(8,128)S(1)}, f32[32,256]{1,0:T(8,128)S(1)}, u32[]{:S(2)}, u32[]{:S(2)}) collective-permute-start(f32[32,256]{1,0:T(8,128)S(1)} %join_pair.1.refs_0_), channel_id=1, source_target_pairs={{0,8},{4,12},{8,16},{12,20},{16,24},{20,28},{24,0},{28,4},{1,9},{5... | collective-permute-start | bytes 98312 | tf_op jit(solution)/shard_map/ppermute | solution.py:786
  84.0 1.2 %copy-start.2 = (f32[32,32,256]{2,1,0:T(8,128)S(1)}, f32[32,32,256]{2,1,0:T(8,128)}, u32[]{:S(2)}) copy-start(f32[32,32,256]{2,1,0:T(8,128)} %mask_backward.1.refs_4_) | copy-start | bytes 3145732

commit v4 on v3

--- a/solution.py
+++ b/solution.py
@@ -21,18 +21,17 @@
 SMEM = pl.BlockSpec(memory_space=pltpu.SMEM)
 
 
-def gelu_value(x):
-    inner = x * (GELU_A + (GELU_A * GELU_B) * (x * x))
-    return x * (0.5 + 0.5 * jnp.tanh(inner))
-
-
 def gelu_parts(x):
     square = x * x
-    inner = x * (GELU_A + (GELU_A * GELU_B) * square)
-    half = 0.5 + 0.5 * jnp.tanh(inner)
-    value = x * half
-    slope = half + value * (1.0 - half) * (2.0 * GELU_A + (6.0 * GELU_A * GELU_B) * square)
-    return value, slope
+    tanh = jnp.tanh(x * (GELU_A + (GELU_A * GELU_B) * square))
+    above = 1.0 + tanh
+    value = x * above
+    rate = GELU_A + (3.0 * GELU_A * GELU_B) * square
+    return 0.5 * value, above + value * (1.0 - tanh) * rate
+
+
+def gelu_twice(x):
+    return x * (1.0 + jnp.tanh(x * (GELU_A + (GELU_A * GELU_B) * (x * x))))
 
 
 def clear_border(ref):
@@ -44,15 +43,13 @@
         ref[row, PAD - 1] = blank[0]
 
 
-def taps_of(ref, begin, end, flip):
+def tap_of(ref, begin, end, tap, flip):
     boxes, channels = ref.shape[2:]
-    pieces = []
-    for s in range(3):
-        for t in range(3):
-            s0, t0 = (2 - s, 2 - t) if flip else (s, t)
-            part = ref[begin + s0 : end + s0, t0 : t0 + CROP]
-            pieces.append(part.reshape((end - begin) * CROP * boxes, channels))
-    return pieces
+    s, t = divmod(tap, 3)
+    if flip:
+        s, t = 2 - s, 2 - t
+    part = ref[begin + s : end + s, t : t + CROP]
+    return part.reshape((end - begin) * CROP * boxes, channels)
 
 
 def box_columns(values, shape, axis):
@@ -64,20 +61,24 @@
 
 
 def chain(product, finish, before_ref, stages):
-    late = None
+    late = []
     count = 0
     for layer, source, target in stages:
         for begin in range(0, CROP, ROWS):
             end = min(begin + ROWS, CROP)
             before = before_ref.at[count % before_ref.shape[0]]
             count += 1
-            before[: end - begin] = product(layer, source, begin, end).reshape(
-                (end - begin,) + before.shape[1:]
-            )
-            if late is not None:
-                late()
-            late = functools.partial(finish, layer, before, target, begin, end)
-    late()
+            total = product(layer, source, begin, end)
+            before[: end - begin] = total.reshape((end - begin,) + before.shape[1:])
+            for piece in late:
+                piece()
+            late = [
+                functools.partial(finish, layer, before.at[u - begin], target, u, v)
+                for u in range(begin, end)
+                for v in range(CROP)
+            ]
+    for piece in late:
+        piece()
 
 
 def forward_kernel(
@@ -113,18 +114,16 @@
 
     def forward(layer, source, begin, end):
         return jnp.dot(
-            jnp.concatenate(taps_of(source, begin, end, False), axis=1),
+            jnp.concatenate([tap_of(source, begin, end, tap, False) for tap in range(9)], axis=1),
             weight_ref[layer],
             preferred_element_type=jnp.float32,
         )
 
-    def activate(layer, before, target, begin, end):
-        for u in range(begin, end):
-            for v in range(CROP):
-                piece = slice(v * boxes, (v + 1) * boxes)
-                value, slope = gelu_parts(before[u - begin, piece])
-                slope_ref[layer, u, piece] = slope.astype(jnp.bfloat16)
-                target[u + 1, 1 + v] = value.astype(jnp.bfloat16)
+    def activate(layer, before, target, u, v):
+        piece = slice(v * boxes, (v + 1) * boxes)
+        value, slope = gelu_parts(before[piece])
+        slope_ref[layer, u, piece] = slope.astype(jnp.bfloat16)
+        target[u + 1, 1 + v] = value.astype(jnp.bfloat16)
 
     def up(pair, carry):
         stages = [(2 * pair, a_ref, b_ref), (2 * pair + 1, b_ref, a_ref)]
@@ -132,26 +131,36 @@
         return carry
 
     lax.fori_loop(0, layers // 2, up, 0)
-    vector = mask_ref[...].astype(jnp.float32).reshape(1, channels)
+    vector = jnp.broadcast_to(
+        mask_ref[...].astype(jnp.float32).reshape(1, channels), (128, channels)
+    ).astype(jnp.bfloat16)
     place = lax.broadcasted_iota(jnp.int32, send_ref.shape, 1)
-    sums = [jnp.zeros(send_ref.shape, jnp.float32) for _ in range(2)]
-    for cell in range(CROP * CROP):
-        u, v = divmod(cell, CROP)
-        line = jnp.sum(a_ref[u + 1, v + 1].astype(jnp.float32) * vector, axis=-1, keepdims=True)
-        sums[cell % 2] = jnp.where(place == cell, line, sums[cell % 2])
+    lane = lax.broadcasted_iota(jnp.int32, (boxes, 128), 1)
+    halves = [jnp.zeros((boxes, 128), jnp.float32) for _ in range(2)]
+    for u in range(CROP):
+        lines = lax.dot_general(
+            a_ref[u + 1, 1 : 1 + CROP].reshape(lanes, channels), vector, NT,
+            preferred_element_type=jnp.float32,
+        )
+        for v in range(CROP):
+            half, cell = divmod(u * CROP + v, 128)
+            halves[half] = jnp.where(
+                lane == cell, lines[v * boxes : (v + 1) * boxes], halves[half]
+            )
     owner = box_columns(
         [jnp.where(n < count, owner_ref[0, 0, n], -1) for n in range(boxes)], send_ref.shape, 0
     )
     send_ref[...] = jnp.where(
-        place == CROP * CROP, owner.astype(jnp.float32), sums[0] + sums[1]
+        place == CROP * CROP, owner.astype(jnp.float32), jnp.concatenate(halves, axis=1)
     )
 
 
 def backward_kernel(
     geom_ref, count_ref, send_ref, soft_ref, slope_ref, weight_ref, mask_ref,
-    grad_ref,
+    grad_ref, done_ref,
     a_ref, b_ref, spread_ref, place_ref, before_ref,
 ):
+    done_ref[...] = jnp.zeros_like(done_ref)
     boxes, channels = a_ref.shape[2:]
     tile_cols = grad_ref.shape[1]
     layers = weight_ref.shape[0]
@@ -175,7 +184,7 @@
         where % CROP < box_columns(broad, shape, 0)
     )
     soft = soft_ref[0, 0].astype(jnp.float32)
-    lead = loss_scale * (jax.nn.sigmoid(send_ref[:, :cells]) - soft)
+    lead = loss_scale * 0.5**layers * (jax.nn.sigmoid(send_ref[:, :cells]) - soft)
     lead = jnp.where(inside, lead, 0.0)
     vector = mask_ref[...].astype(jnp.float32).reshape(1, channels)
     for u in range(CROP):
@@ -187,9 +196,9 @@
 
     def backward(layer, source, begin, end):
         total = None
-        for tap, piece in enumerate(taps_of(source, begin, end, True)):
+        for tap in range(9):
             part = lax.dot_general(
-                piece,
+                tap_of(source, begin, end, tap, True),
                 weight_ref[layer, tap * channels : (tap + 1) * channels, :],
                 NT,
                 preferred_element_type=jnp.float32,
@@ -197,14 +206,11 @@
             total = part if total is None else total + part
         return total
 
-    def descend(layer, before, target, begin, end):
-        first = layer == 0
-        for u in range(begin, end):
-            for v in range(CROP):
-                piece = slice(v * boxes, (v + 1) * boxes)
-                slope = slope_ref[jnp.maximum(layer - 1, 0), u, piece].astype(jnp.float32)
-                slope = jnp.where(first, 1.0, slope)
-                target[u + 1, 1 + v] = (before[u - begin, piece] * slope).astype(jnp.bfloat16)
+    def descend(layer, before, target, u, v):
+        piece = slice(v * boxes, (v + 1) * boxes)
+        slope = slope_ref[jnp.maximum(layer - 1, 0), u, piece].astype(jnp.float32)
+        slope = jnp.where(layer == 0, 1.0, slope)
+        target[u + 1, 1 + v] = (before[piece] * slope).astype(jnp.bfloat16)
 
     def down(pair, carry):
         layer = layers - 1 - 2 * pair
@@ -218,12 +224,12 @@
             place_ref[...],
             b_ref[u + 1, 1 : 1 + CROP].reshape(lanes, channels),
             preferred_element_type=jnp.float32,
-        ).reshape(boxes, tile_cols, channels)
+        ).astype(jnp.bfloat16).reshape(boxes, tile_cols, channels)
     grad_ref[...] = jnp.zeros_like(grad_ref)
     for n in range(boxes):
         kept = lax.broadcasted_iota(jnp.int32, (CROP, 1, 1), 0) < tall[n]
         rows = pl.ds(geom_ref[0, 0, 0, n], CROP)
-        grad_ref[rows] = grad_ref[rows] + jnp.where(kept, spread_ref[:, n], 0.0)
+        grad_ref[rows] = grad_ref[rows] + jnp.where(kept, spread_ref[:, n].astype(jnp.float32), 0.0)
 
 
 def pair_kernel(own_ref, other_ref, out_ref):
@@ -305,13 +311,16 @@
     padded = pltpu.VMEM((PAD, PAD, boxes, channels), jnp.bfloat16)
     return pl.pallas_call(
         backward_kernel,
-        out_shape=jax.ShapeDtypeStruct(tile + (channels,), jnp.float32),
+        out_shape=(
+            jax.ShapeDtypeStruct(tile + (channels,), jnp.float32),
+            jax.ShapeDtypeStruct((8, 128), jnp.float32),
+        ),
         in_specs=[SMEM, SMEM, VMEM, VMEM, VMEM, VMEM, VMEM],
-        out_specs=VMEM,
+        out_specs=(VMEM, VMEM),
         scratch_shapes=[
             padded,
             padded,
-            pltpu.VMEM((CROP, boxes, tile[1], channels), jnp.float32),
+            pltpu.VMEM((CROP, boxes, tile[1], channels), jnp.bfloat16),
             pltpu.VMEM((boxes * tile[1], lanes), jnp.bfloat16),
             pltpu.VMEM((3, ROWS, lanes, channels), jnp.float32),
         ],
@@ -602,34 +611,37 @@
     steps = cells_down // group
 
     def merge(step):
-        residual = residual_ref.at[step % 2]
+        residual = residual_ref.at[step % 3]
         cells = slice(step * group, (step + 1) * group)
         residual[...] = jnp.dot(
             mixed_ref[cells].reshape(rows, model), merge_ref[...], preferred_element_type=jnp.float32
         )
-        for part in range(0, rows, PART):
-            cut = slice(part, part + PART)
-            c, a = divmod(part // CELL, cells_across)
-            own = ordered_ref[step * group + c, a : a + PART // CELL].reshape(PART, model)
-            total = residual[cut] + own.astype(jnp.float32)
-            residual[cut] = total
-            normed_ref[step % 2, cut] = norm_rows(total, second)
-
-    def expand(step):
-        wide_ref[step % 2] = jnp.dot(
-            normed_ref[step % 2], expand_ref[...], preferred_element_type=jnp.float32
-        )
-
-    def activate(step):
+
+    def normalise(step, part):
+        residual = residual_ref.at[step % 3]
+        cut = slice(part, part + PART)
+        c, a = divmod(part // CELL, cells_across)
+        own = ordered_ref[step * group + c, a : a + PART // CELL].reshape(PART, model)
+        total = residual[cut] + own.astype(jnp.float32)
+        residual[cut] = total
+        normed_ref[step % 2, cut] = norm_rows(total, second)
+
+    def expand(step, lane):
+        cut = slice(lane, lane + LANES)
+        wide_ref[step % 2, :, cut] = jnp.dot(
+            normed_ref[step % 2], expand_ref[:, cut], preferred_element_type=jnp.float32
+        )
+
+    def activate(step, lane):
+        cut = slice(lane, lane + LANES)
         for part in range(0, rows, CELL):
-            cut = slice(part, part + CELL)
-            for lane in range(0, wide_ref.shape[2], 512):
-                hidden_ref[step % 2, cut, lane : lane + 512] = gelu_value(
-                    wide_ref[step % 2, cut, lane : lane + 512]
-                ).astype(jnp.bfloat16)
+            here = slice(part, part + CELL)
+            hidden_ref[step % 2, here, cut] = gelu_twice(wide_ref[step % 2, here, cut]).astype(
+                jnp.bfloat16
+            )
 
     def shrink(step):
-        block_out = residual_ref[step % 2] + jnp.dot(
+        block_out = residual_ref[step % 3] + 0.5 * jnp.dot(
             hidden_ref[step % 2], shrink_ref[...], preferred_element_type=jnp.float32
         )
         features = jnp.dot(
@@ -645,17 +657,28 @@
             features_ref[first : first + SUB] = natural
             copy_ref[first : first + SUB] = natural
 
-    merge(0)
-    expand(0)
+    lanes = range(0, wide_ref.shape[2], LANES)
+    for step in range(min(2, steps)):
+        merge(step)
+        for part in range(0, rows, PART):
+            normalise(step, part)
+        if step == 0:
+            for lane in lanes:
+                expand(0, lane)
     for step in range(steps):
-        if step + 1 < steps:
-            merge(step + 1)
-        activate(step)
-        if step + 1 < steps:
-            expand(step + 1)
+        for lane in lanes:
+            if step + 1 < steps:
+                expand(step + 1, lane)
+            activate(step, lane)
+        if step + 2 < steps:
+            merge(step + 2)
         shrink(step)
-
-
+        if step + 2 < steps:
+            for part in range(0, rows, PART):
+                normalise(step + 2, part)
+
+
+LANES = 256
 PART = 64
 
 
@@ -665,6 +688,24 @@
 
 def cells_of(count_down, count_across, channels, dtype=jnp.bfloat16):
     return jax.ShapeDtypeStruct((count_down, count_across, CELL, channels), dtype)
+
+
+def end_kernel(tokens_ref, first_ref, last_ref):
+    first_ref[...] = tokens_ref[:SUB]
+    last_ref[...] = tokens_ref[tokens_ref.shape[0] - SUB :]
+
+
+def end_rows(tokens):
+    out = jax.ShapeDtypeStruct((SUB,) + tokens.shape[1:], tokens.dtype)
+    return pl.pallas_call(
+        end_kernel,
+        out_shape=(out, out),
+        in_specs=[VMEM],
+        out_specs=(VMEM, VMEM),
+        compiler_params=params(4),
+        cost_estimate=cost(tokens.shape[0] * tokens.shape[1], 2**20),
+        name="end_rows",
+    )(tokens)
 
 
 def joint_rows(tokens, gain, weight):
@@ -737,7 +778,7 @@
             pltpu.VMEM((down, across, CELL, model), jnp.bfloat16),
             pltpu.VMEM((2, down + 2, CELL, 2 * model), jnp.bfloat16),
             pltpu.VMEM((strip, strip), jnp.bfloat16),
-            pltpu.VMEM((2, rows, model), jnp.float32),
+            pltpu.VMEM((3, rows, model), jnp.float32),
             pltpu.VMEM((2, rows, model), jnp.bfloat16),
             pltpu.VMEM((2, rows, wide), jnp.float32),
             pltpu.VMEM((2, rows, wide), jnp.bfloat16),
@@ -762,8 +803,9 @@
     soft_target,
 ):
     tile_rows, tile_cols, model = tokens.shape
-    up = shift(tokens[-SUB:], "row", 1)
-    down = shift(tokens[:SUB], "row", -1)
+    first, last = end_rows(tokens)
+    up = shift(last, "row", 1)
+    down = shift(first, "row", -1)
     joint, ordered, west, east = joint_rows(tokens, first_gain, joint_weight)
     up, down, west, east = lengthen(up, down, west, east)
     left = shift(east, "col", 1)
@@ -785,11 +827,11 @@
         blocks.append(
             lax.ppermute(both, "row", [(i, (i + back) % rows_size) for i in range(rows_size)])
         )
-    feature_grad = mask_backward(
+    feature_grad, done = mask_backward(
         send, soft_target, slope, geometry, box_counts, conv_weight, mask_weight,
         (tile_rows, tile_cols),
     )
-    return features, feature_grad, collect(blocks, feature_grad, BOX_OWN, CROP * CROP)
+    return features, feature_grad, collect(blocks, done, BOX_OWN, CROP * CROP)
 
 
 def solution(mesh):

time: 87.2 us -> 84.2 us (0.966)
  local copies, waits for them, and re-layouts: 5.49 us -> 1.3 us
  waiting for transfers between devices: 1.74 us -> 2.85 us
    unnamed x36 -> x32, local copies, waits for them, and re-layouts: 4.53 us -> 1.3 us
    ppermute x4, waiting for transfers between devices: 0.01 us -> 1.13 us  [shift(): return lax.ppermute(x, axis, pairs)]
    ppermute x4, starting transfers between devices: 11.4 us -> 10.4 us  [shift(): return lax.ppermute(x, axis, pairs)]
    slice x1 -> x0, local copies, waits for them, and re-layouts: 0.96 us -> none  [shards(): down = shift(tokens[:SUB], 'row', -1)]
    pallas_call x1 -> x2, Pallas kernels: 19.9 us -> 19.9 us  [the longest x1 19.8 us: mask_backward(): pl.pallas_call(backward_kernel, out_shape=(jax.ShapeDtypeStruct(tile + (c...]
  transfers between devices with their start and end apart: 8 -> 8, of which waited for: 1 -> 2; matrix products, arithmetic and copies ran while one was open for 0% -> 0% of each run, Pallas kernels for 33% -> 34%
where the time goes in v4:
time: 84.2 us; the launch traced here: 83 us
  Pallas kernels  59.3 us (70%)
  starting transfers between devices  18 us (21%)
  waiting for transfers between devices  2.85 us (3%)
  between operations  1.59 us (2%)
  local copies, waits for them, and re-layouts  1.3 us (2%)
    pallas_call x1, Pallas kernels, mask_forward(): pl.pallas_call(forward_kernel, out_shape=(jax.ShapeDtypeStruct((boxes, 25...  21 us
    pallas_call x1, Pallas kernels, mask_backward(): pl.pallas_call(backward_kernel, out_shape=(jax.ShapeDtypeStruct(tile + (c...  19.8 us
    ppermute x4, starting transfers between devices, shift(): return lax.ppermute(x, axis, pairs)  10.4 us
    pallas_call x1, Pallas kernels, side_windows(): pl.pallas_call(sides_kernel, out_shape=(tile, tile), in_specs=[VMEM] * 15...  9.04 us
    ppermute x3, starting transfers between devices, shards(): lax.ppermute(both, 'row', [(i, (i + back) % rows_size) for i in range(row...  5.13 us
    pallas_call x1, Pallas kernels, joint_rows(): pl.pallas_call(joint_kernel, out_shape=(cells_of(down, across, weight.sha...  3.38 us
    pallas_call x1, Pallas kernels, inner_windows(): pl.pallas_call(inner_kernel, out_shape=(jax.ShapeDtypeStruct(joint.shape[...  3.17 us
    ppermute x1, starting transfers between devices, shards(): lax.ppermute(send, 'row', [(i, i ^ 1) for i in range(rows_size)])  2.51 us
  transfers between devices with their start and end apart: 8, of which 2 were waited for; matrix products, arithmetic and copies ran while one was open for 0% of the time, Pallas kernels for 34%

profile of v4, /device:TPU:4, one launch (start us, length us, event | category | flops | bytes accessed | tf_op | source)
XLA Modules:
  0.0 83.0 jit_solution(7749038577683088829)
XLA Ops:
  0.6 0.0 copy-start.2
  0.6 0.0 copy-start.5
  0.7 0.0 copy-start.7
  0.7 1.2 %copy-done.7 = bf16[32,32,384]{2,1,0:T(8,128)(2,1)S(1)} copy-done((bf16[32,32,384]{2,1,0:T(8,128)(2,1)S(1)}, bf16[32,32,384]{2,1,0:T(8,128)(2,1)}, u32[]{:S(2)}) %copy-start.7) | copy-done | bytes 786456
  1.9 3.5 %collective-permute-start = (bf16[4,32,384]{2,1,0:T(8,128)(2,1)S(1)}, bf16[4,32,384]{2,1,0:T(8,128)(2,1)S(1)}, u32[]{:S(2)}, u32[]{:S(2)}) collective-permute-start(bf16[4,32,384]{2,1,0:T(8,128)(2,1)S(1)} %get-tuple-element.25), channel_id=1, source_target_pairs={{0,4},{4,8},{8,12},{12,16},{16,20},{20,24},{24,28},{1,5},{5,9},{9,... | collective-permute-start | bytes 294920 | tf_op jit(solution)/shard_map/ppermute | solution.py:797
  5.4 1.3 %collective-permute-start.1 = (bf16[4,32,384]{2,1,0:T(8,128)(2,1)S(1)}, bf16[4,32,384]{2,1,0:T(8,128)(2,1)S(1)}, u32[]{:S(2)}, u32[]{:S(2)}) collective-permute-start(bf16[4,32,384]{2,1,0:T(8,128)(2,1)S(1)} %get-tuple-element.26), channel_id=1, source_target_pairs={{4,0},{8,4},{12,8},{16,12},{20,16},{24,20},{28,24},{5,1},{9,5},{13... | collective-permute-start | bytes 294920 | tf_op jit(solution)/shard_map/ppermute | solution.py:797
  7.4 0.0 copy-done.2
  7.4 0.0 copy-done.5
  7.4 0.0 copy-done.8
  7.4 0.0 copy-start.9
  7.4 3.4 %joint_rows.1 = (bf16[8,8,16,1152]{3,2,1,0:T(8,128)(2,1)S(1)}, bf16[8,8,16,384]{3,2,1,0:T(8,128)(2,1)S(1)}, bf16[8,16,384]{2,1,0:T(8,128)(2,1)S(1)}, bf16[8,16,384]{2,1,0:T(8,128)(2,1)S(1)}) custom-call(bf16[32,32,384]{2,1,0:T(8,128)(2,1)S(1)} %copy-done.8, f32[384]{0:T(512)S(1)} %copy-done.5, bf16[384,1152]{1,0:T(8,128)(2,1)S(1)} %copy-done.2), custom_call_target="tpu_custom_call" | custom-call | flops 1811939328 | bytes 4194304 | tf_op jit(solution)/shard_map/joint_rows/pallas_call | solution.py:715
  10.8 0.0 collective-permute-done.up_ref
  10.8 1.1 %collective-permute-done.1.down_ref = bf16[4,32,384]{2,1,0:T(8,128)(2,1)S(1)} collective-permute-done((bf16[4,32,384]{2,1,0:T(8,128)(2,1)S(1)}, bf16[4,32,384]{2,1,0:T(8,128)(2,1)S(1)}, u32[]{:S(2)}, u32[]{:S(2)}) %collective-permute-start.1) | collective-permute-done | bytes 98336 | tf_op jit(solution)/shard_map/ppermute | solution.py:797
  11.9 0.2 lengthen.1
  12.1 1.9 %collective-permute-start.2 = (bf16[10,16,384]{2,1,0:T(8,128)(2,1)S(1)}, bf16[10,16,384]{2,1,0:T(8,128)(2,1)S(1)}, u32[]{:S(2)}, u32[]{:S(2)}) collective-permute-start(bf16[10,16,384]{2,1,0:T(8,128)(2,1)S(1)} %get-tuple-element.36), channel_id=1, source_target_pairs={{0,1},{1,2},{2,3},{4,5},{5,6},{6,7},{8,9},{9,10},{10,11},{12,13},{... | collective-permute-start | bytes 368648 | tf_op jit(solution)/shard_map/ppermute | solution.py:797
  14.1 3.6 %collective-permute-start.3 = (bf16[10,16,384]{2,1,0:T(8,128)(2,1)S(1)}, bf16[10,16,384]{2,1,0:T(8,128)(2,1)S(1)}, u32[]{:S(2)}, u32[]{:S(2)}) collective-permute-start(bf16[10,16,384]{2,1,0:T(8,128)(2,1)S(1)} %get-tuple-element.29.after_ref), channel_id=1, source_target_pairs={{1,0},{2,1},{3,2},{5,4},{6,5},{7,6},{9,8},{10,9},{11,10},{13,12},{... | collective-permute-start | bytes 368648 | tf_op jit(solution)/shard_map/ppermute | solution.py:797
  17.7 0.0 copy-done.9
  17.7 3.2 %inner_windows.1 = (bf16[8,8,16,384]{3,2,1,0:T(8,128)(2,1)S(1)}, f32[3,64,256]{2,1,0:T(8,128)S(1)}) custom-call(bf16[8,8,16,1152]{3,2,1,0:T(8,128)(2,1)S(1)} %get-tuple-element.24.joint_ref.joint_out_ref, f32[12,64,64]{2,1,0:T(8,128)S(1)} %copy-done.9, bf16[10,16,384]{2,1,0:T(8,128)(2,1)S(1)} %get-tuple-element.29.after_ref), custom_call_target="tpu_custom_call" | custom-call | flops 2147483648 | bytes 4194304 | tf_op jit(solution)/shard_map/inner_windows/pallas_call | solution.py:738
  20.9 0.0 copy-start
  20.9 0.0 copy-start.1
  20.9 0.0 copy-start.3
  20.9 0.0 copy-start.4
  21.0 0.0 copy-start.6
  21.0 0.0 slice-start
  21.0 1.6 %end_windows.1 = (bf16[2,8,16,768]{3,2,1,0:T(8,128)(2,1)S(1)}, bf16[2,8,16,384]{3,2,1,0:T(8,128)(2,1)S(1)}) custom-call(bf16[8,8,16,1152]{3,2,1,0:T(8,128)(2,1)S(1)} %get-tuple-element.24.joint_ref.joint_out_ref, bf16[8,16,384]{2,1,0:T(8,128)(2,1)S(1)} %get-tuple-element.31.up_ref, bf16[8,16,384]{2,1,0:T(8,128)(2,1)S(1)} %get-tuple-element.32.down_ref, ...), custom_call_target="tpu_custom_call" | custom-call | flops 2147483648 | bytes 4194304 | tf_op jit(solution)/shard_map/end_windows/pallas_call | solution.py:754
  22.6 0.0 collective-permute-done.2.left_ref
  22.6 0.0 collective-permute-done.3.right_ref
  22.6 0.0 copy-done
  22.6 0.0 copy-done.1
  22.6 0.0 copy-done.4
  22.7 0.0 slice-start.1
  22.7 0.0 copy-start.11
  22.7 0.0 copy-start.12
  22.7 0.0 copy-start.13
  22.7 9.0 %side_windows.1 = (bf16[32,32,256]{2,1,0:T(8,128)(2,1)}, bf16[32,32,256]{2,1,0:T(8,128)(2,1)S(1)}) custom-call(bf16[8,8,16,384]{3,2,1,0:T(8,128)(2,1)S(1)} %get-tuple-element.23.ordered_ref, bf16[8,8,16,1152]{3,2,1,0:T(8,128)(2,1)S(1)} %get-tuple-element.24.joint_ref.joint_out_ref, bf16[8,8,16,384]{3,2,1,0:T(8,128)(2,1)S(1)} %get-tuple-element.30.inner_ref, ...), custom_call_target="tpu_custom_call" | custom-call | tf_op jit(solution)/shard_map/side_windows/pallas_call | solution.py:772
  31.7 0.0 copy-done.11
  31.8 0.0 copy-start.10
  31.8 21.0 %mask_forward.1 = (f32[16,256]{1,0:T(8,128)S(1)}, bf16[4,14,224,256]{3,2,1,0:T(8,128)(2,1)S(1)}) custom-call(s32[1,1,4,16]{3,2,1,0:T(4,128)S(1)} %bitcast.3, s32[1,1]{1,0:T(1,128)S(6)} %copy.18.count_ref, s32[1,1,16]{2,1,0:T(1,128)S(1)} %copy-done.12, bf16[32,32,256]{2,1,0:T(8,128)(2,1)S(1)} %get-tuple-element.38.features_ref, ...), custom_call_target="tpu_custom_call" | custom-call | flops 24999999488 | bytes 4718592 | tf_op jit(solution)/shard_map/mask_forward/pallas_call | solution.py:287
  52.8 2.5 %collective-permute-start.4 = (f32[16,256]{1,0:T(8,128)S(1)}, f32[16,256]{1,0:T(8,128)S(1)}, u32[]{:S(2)}, u32[]{:S(2)}) collective-permute-start(f32[16,256]{1,0:T(8,128)S(1)} %get-tuple-element.39.send_ref.own_ref), channel_id=1, source_target_pairs={{0,4},{4,0},{8,12},{12,8},{16,20},{20,16},{24,28},{28,24},{1,5},{5... | collective-permute-start | bytes 49160 | tf_op jit(solution)/shard_map/ppermute | solution.py:824
  55.3 1.7 %collective-permute-done.4.other_ref = f32[16,256]{1,0:T(8,128)S(1)} collective-permute-done((f32[16,256]{1,0:T(8,128)S(1)}, f32[16,256]{1,0:T(8,128)S(1)}, u32[]{:S(2)}, u32[]{:S(2)}) %collective-permute-start.4) | collective-permute-done | bytes 16416 | tf_op jit(solution)/shard_map/ppermute | solution.py:824
  57.0 4.1 %collective-permute-start.7 = (f32[32,256]{1,0:T(8,128)S(1)}, f32[32,256]{1,0:T(8,128)S(1)}, u32[]{:S(2)}, u32[]{:S(2)}) collective-permute-start(f32[32,256]{1,0:T(8,128)S(1)} %join_pair.1.refs_0_), channel_id=1, source_target_pairs={{0,24},{4,28},{8,0},{12,4},{16,8},{20,12},{24,16},{28,20},{1,25},{... | collective-permute-start | bytes 98312 | tf_op jit(solution)/shard_map/ppermute | solution.py:828
  61.1 0.0 collective-permute-start.6
  61.1 1.0 %collective-permute-start.5 = (f32[32,256]{1,0:T(8,128)S(1)}, f32[32,256]{1,0:T(8,128)S(1)}, u32[]{:S(2)}, u32[]{:S(2)}) collective-permute-start(f32[32,256]{1,0:T(8,128)S(1)} %join_pair.1.refs_0_), channel_id=1, source_target_pairs={{0,8},{4,12},{8,16},{12,20},{16,24},{20,28},{24,0},{28,4},{1,9},{5... | collective-permute-start | bytes 98312 | tf_op jit(solution)/shard_map/ppermute | solution.py:828
  62.1 19.8 %mask_backward.1 = (f32[32,32,256]{2,1,0:T(8,128)}, f32[8,128]{1,0:T(8,128)S(1)}) custom-call(s32[1,1,4,16]{3,2,1,0:T(4,128)S(1)} %bitcast.4, s32[1,1]{1,0:T(1,128)S(6)} %copy.18.count_ref, f32[16,256]{1,0:T(8,128)S(1)} %get-tuple-element.39.send_ref.own_ref, bf16[1,1,16,196]{3,2,1,0:T(8,128)(2,1)S(1)} %copy-done.10, ...), custom_call_target="tpu_custom_call" | custom-call | flops 24999999488 | bytes 4718592 | tf_op jit(solution)/shard_map/mask_backward/pallas_call | solution.py:312
  82.0 0.0 collective-permute-done.7.refs_3_
  82.0 0.0 collective-permute-done.6.refs_2_
  82.0 0.0 collective-permute-done.5.refs_1_
  82.0 1.0 %collect.1 = f32[1,1,8,196]{3,2,1,0:T(8,128)} custom-call(f32[32,256]{1,0:T(8,128)S(1)} %join_pair.1.refs_0_, f32[32,256]{1,0:T(8,128)S(1)} %collective-permute-done.5.refs_1_, f32[32,256]{1,0:T(8,128)S(1)} %collective-permute-done.6.refs_2_, f32[32,256]{1,0:T(8,128)S(1)} %collective-permute-done.7.refs_3_, f32[8,128]{1,0:T(8,128)S(1)} %get-tuple-element.42.refs_4_), custom_call_target="tpu_custom_call" | custom-call | tf_op jit(solution)/shard_map/collect/pallas_call | solution.py:334
  (11 shorter events, 0.0 us)
Async XLA Ops:
  0.6 6.7 %copy-start.2 = (bf16[384,1152]{1,0:T(8,128)(2,1)S(1)}, bf16[384,1152]{1,0:T(8,128)(2,1)}, u32[]{:S(2)}) copy-start(bf16[384,1152]{1,0:T(8,128)(2,1)} %joint_ref.5) | copy-start | bytes 2654212
  0.6 6.7 %copy-start.5 = (f32[384]{0:T(512)S(1)}, f32[384]{0:T(512)}, u32[]{:S(2)}) copy-start(f32[384]{0:T(512)} %first_ref.1) | copy-start | bytes 4612
  0.7 1.2 %copy-start.7 = (bf16[32,32,384]{2,1,0:T(8,128)(2,1)S(1)}, bf16[32,32,384]{2,1,0:T(8,128)(2,1)}, u32[]{:S(2)}) copy-start(bf16[32,32,384]{2,1,0:T(8,128)(2,1)} %tokens_ref.3) | copy-start | bytes 2359300
  1.9 5.5 %copy-start.8 = (bf16[32,32,384]{2,1,0:T(8,128)(2,1)S(1)}, bf16[32,32,384]{2,1,0:T(8,128)(2,1)}, u32[]{:S(2)}) copy-start(bf16[32,32,384]{2,1,0:T(8,128)(2,1)} %tokens_ref.3) | copy-start | bytes 2359300
  1.9 8.9 %collective-permute-start = (bf16[4,32,384]{2,1,0:T(8,128)(2,1)S(1)}, bf16[4,32,384]{2,1,0:T(8,128)(2,1)S(1)}, u32[]{:S(2)}, u32[]{:S(2)}) collective-permute-start(bf16[4,32,384]{2,1,0:T(8,128)(2,1)S(1)} %get-tuple-element.25), channel_id=1, source_target_pairs={{0,4},{4,8},{8,12},{12,16},{16,20},{20,24},{24,28},{1,5},{5,9},{9,... | collective-permute-start | bytes 294920 | tf_op jit(solution)/shard_map/ppermute | solution.py:797
  5.4 6.5 %collective-permute-start.1 = (bf16[4,32,384]{2,1,0:T(8,128)(2,1)S(1)}, bf16[4,32,384]{2,1,0:T(8,128)(2,1)S(1)}, u32[]{:S(2)}, u32[]{:S(2)}) collective-permute-start(bf16[4,32,384]{2,1,0:T(8,128)(2,1)S(1)} %get-tuple-element.26), channel_id=1, source_target_pairs={{4,0},{8,4},{12,8},{16,12},{20,16},{24,20},{28,24},{5,1},{9,5},{13... | collective-permute-start | bytes 294920 | tf_op jit(solution)/shard_map/ppermute | solution.py:797
  7.4 10.3 %copy-start.9 = (f32[12,64,64]{2,1,0:T(8,128)S(1)}, f32[12,64,64]{2,1,0:T(8,128)}, u32[]{:S(2)}) copy-start(f32[12,64,64]{2,1,0:T(8,128)} %relative_ref.1) | copy-start | bytes 589828
  12.1 10.4 %collective-permute-start.2 = (bf16[10,16,384]{2,1,0:T(8,128)(2,1)S(1)}, bf16[10,16,384]{2,1,0:T(8,128)(2,1)S(1)}, u32[]{:S(2)}, u32[]{:S(2)}) collective-permute-start(bf16[10,16,384]{2,1,0:T(8,128)(2,1)S(1)} %get-tuple-element.36), channel_id=1, source_target_pairs={{0,1},{1,2},{2,3},{4,5},{5,6},{6,7},{8,9},{9,10},{10,11},{12,13},{... | collective-permute-start | bytes 368648 | tf_op jit(solution)/shard_map/ppermute | solution.py:797
  14.1 8.5 %collective-permute-start.3 = (bf16[10,16,384]{2,1,0:T(8,128)(2,1)S(1)}, bf16[10,16,384]{2,1,0:T(8,128)(2,1)S(1)}, u32[]{:S(2)}, u32[]{:S(2)}) collective-permute-start(bf16[10,16,384]{2,1,0:T(8,128)(2,1)S(1)} %get-tuple-element.29.after_ref), channel_id=1, source_target_pairs={{1,0},{2,1},{3,2},{5,4},{6,5},{7,6},{9,8},{10,9},{11,10},{13,12},{... | collective-permute-start | bytes 368648 | tf_op jit(solution)/shard_map/ppermute | solution.py:797
  20.9 1.7 %copy-start = (bf16[384,1536]{1,0:T(8,128)(2,1)S(1)}, bf16[384,1536]{1,0:T(8,128)(2,1)}, u32[]{:S(2)}) copy-start(bf16[384,1536]{1,0:T(8,128)(2,1)} %expand_ref.1) | copy-start | bytes 3538948
  20.9 1.7 %copy-start.1 = (bf16[1536,384]{1,0:T(8,128)(2,1)S(1)}, bf16[1536,384]{1,0:T(8,128)(2,1)}, u32[]{:S(2)}) copy-start(bf16[1536,384]{1,0:T(8,128)(2,1)} %shrink_ref.1) | copy-start | bytes 3538948
  20.9 1.7 %copy-start.3 = (bf16[384,384]{1,0:T(8,128)(2,1)S(1)}, bf16[384,384]{1,0:T(8,128)(2,1)}, u32[]{:S(2)}) copy-start(bf16[384,384]{1,0:T(8,128)(2,1)} %merge_ref.1) | copy-start | bytes 884740
  20.9 1.7 %copy-start.4 = (bf16[384,256]{1,0:T(8,128)(2,1)S(1)}, bf16[384,256]{1,0:T(8,128)(2,1)}, u32[]{:S(2)}) copy-start(bf16[384,256]{1,0:T(8,128)(2,1)} %lateral_ref.1) | copy-start | bytes 589828
  21.0 1.7 %copy-start.6 = (f32[384]{0:T(512)S(1)}, f32[384]{0:T(512)}, u32[]{:S(2)}) copy-start(f32[384]{0:T(512)} %second_ref.1) | copy-start | bytes 4612
  21.0 10.8 %slice-start = ((s8[4718592]{0:T(1024)(128)(4,1)}), s8[4194304]{0:T(1024)(128)(4,1)S(1)}, s32[]{:S(2)}) async-start(s8[4718592]{0:T(1024)(128)(4,1)} %bitcast.1), calls=%async_computation | async-start | bytes 8388608
  22.7 9.1 %slice-start.1 = ((s8[4718592]{0:T(1024)(128)(4,1)}), s8[524288]{0:T(1024)(128)(4,1)S(1)}, s32[]{:S(2)}) async-start(s8[4718592]{0:T(1024)(128)(4,1)} %bitcast.1), calls=%async_computation.1 | async-start | bytes 1048576
  22.7 9.1 %copy-start.11 = (s32[1,1,16,4]{2,3,1,0:T(4,128)S(1)}, s32[1,1,16,4]{2,3,1,0:T(4,128)}, u32[]{:S(2)}) copy-start(s32[1,1,16,4]{2,3,1,0:T(4,128)} %param.26) | copy-start | bytes 772
  22.7 9.1 %copy-start.12 = (s32[1,1,16]{2,1,0:T(1,128)S(1)}, s32[1,1,16]{2,1,0:T(1,128)}, u32[]{:S(2)}) copy-start(s32[1,1,16]{2,1,0:T(1,128)} %owner_ref.1) | copy-start | bytes 196
  22.7 9.1 %copy-start.13 = (bf16[256]{0:T(256)(128)(2,1)S(1)}, bf16[256]{0:T(256)(128)(2,1)}, u32[]{:S(2)}) copy-start(bf16[256]{0:T(256)(128)(2,1)} %mask_ref.3) | copy-start | bytes 1540
  31.8 30.4 %copy-start.10 = (bf16[1,1,16,196]{3,2,1,0:T(8,128)(2,1)S(1)}, bf16[1,1,16,196]{3,2,1,0:T(8,128)(2,1)}, u32[]{:S(2)}) copy-start(bf16[1,1,16,196]{3,2,1,0:T(8,128)(2,1)} %soft_ref.1) | copy-start | bytes 18820
  52.8 4.2 %collective-permute-start.4 = (f32[16,256]{1,0:T(8,128)S(1)}, f32[16,256]{1,0:T(8,128)S(1)}, u32[]{:S(2)}, u32[]{:S(2)}) collective-permute-start(f32[16,256]{1,0:T(8,128)S(1)} %get-tuple-element.39.send_ref.own_ref), channel_id=1, source_target_pairs={{0,4},{4,0},{8,12},{12,8},{16,20},{20,16},{24,28},{28,24},{1,5},{5... | collective-permute-start | bytes 49160 | tf_op jit(solution)/shard_map/ppermute | solution.py:824
  57.0 25.0 %collective-permute-start.7 = (f32[32,256]{1,0:T(8,128)S(1)}, f32[32,256]{1,0:T(8,128)S(1)}, u32[]{:S(2)}, u32[]{:S(2)}) collective-permute-start(f32[32,256]{1,0:T(8,128)S(1)} %join_pair.1.refs_0_), channel_id=1, source_target_pairs={{0,24},{4,28},{8,0},{12,4},{16,8},{20,12},{24,16},{28,20},{1,25},{... | collective-permute-start | bytes 98312 | tf_op jit(solution)/shard_map/ppermute | solution.py:828
  61.1 20.9 %collective-permute-start.6 = (f32[32,256]{1,0:T(8,128)S(1)}, f32[32,256]{1,0:T(8,128)S(1)}, u32[]{:S(2)}, u32[]{:S(2)}) collective-permute-start(f32[32,256]{1,0:T(8,128)S(1)} %join_pair.1.refs_0_), channel_id=1, source_target_pairs={{0,16},{4,20},{8,24},{12,28},{16,0},{20,4},{24,8},{28,12},{1,17},{... | collective-permute-start | bytes 98312 | tf_op jit(solution)/shard_map/ppermute | solution.py:828
  61.1 20.9 %collective-permute-start.5 = (f32[32,256]{1,0:T(8,128)S(1)}, f32[32,256]{1,0:T(8,128)S(1)}, u32[]{:S(2)}, u32[]{:S(2)}) collective-permute-start(f32[32,256]{1,0:T(8,128)S(1)} %join_pair.1.refs_0_), channel_id=1, source_target_pairs={{0,8},{4,12},{8,16},{12,20},{16,24},{20,28},{24,0},{28,4},{1,9},{5... | collective-permute-start | bytes 98312 | tf_op jit(solution)/shard_map/ppermute | solution.py:828

commit v5 on v4

--- a/solution.py
+++ b/solution.py
@@ -23,11 +23,11 @@
 
 def gelu_parts(x):
     square = x * x
-    tanh = jnp.tanh(x * (GELU_A + (GELU_A * GELU_B) * square))
-    above = 1.0 + tanh
-    value = x * above
-    rate = GELU_A + (3.0 * GELU_A * GELU_B) * square
-    return 0.5 * value, above + value * (1.0 - tanh) * rate
+    inner = x * (GELU_A + (GELU_A * GELU_B) * square)
+    half = 0.5 + 0.5 * jnp.tanh(inner)
+    value = x * half
+    slope = half + value * (1.0 - half) * (2.0 * GELU_A + (6.0 * GELU_A * GELU_B) * square)
+    return value, slope
 
 
 def gelu_twice(x):
@@ -184,7 +184,7 @@
         where % CROP < box_columns(broad, shape, 0)
     )
     soft = soft_ref[0, 0].astype(jnp.float32)
-    lead = loss_scale * 0.5**layers * (jax.nn.sigmoid(send_ref[:, :cells]) - soft)
+    lead = loss_scale * (jax.nn.sigmoid(send_ref[:, :cells]) - soft)
     lead = jnp.where(inside, lead, 0.0)
     vector = mask_ref[...].astype(jnp.float32).reshape(1, channels)
     for u in range(CROP):
@@ -373,7 +373,17 @@
     place = lax.broadcasted_iota(jnp.int32, (AREA, AREA), 0)
     token = lax.broadcasted_iota(jnp.int32, (AREA, AREA), 1)
     cell, row, col = place // CELL, place // SUB % SUB, place % SUB
-    return one_hot(token == (cell // 2 * SUB + row) * WIN + cell % 2 * SUB + col, jnp.float32)
+    return one_hot(token == (cell // 2 * SUB + row) * WIN + cell % 2 * SUB + col)
+
+
+def exact(permute, values):
+    total = None
+    for _ in range(3):
+        part = values.astype(jnp.bfloat16)
+        values = values - part.astype(jnp.float32)
+        moved = permute(part)
+        total = moved if total is None else total + moved
+    return total
 
 
 def head_blocks(lanes):
@@ -410,71 +420,60 @@
 
 
 def joint_kernel(
-    tokens_ref, gain_ref, joint_ref,
-    out_ref, ordered_ref, west_ref, east_ref, order_ref,
+    tokens_ref, gain_ref, joint_ref, relative_ref,
+    out_ref, bias_ref, ordered_ref, west_ref, east_ref, order_ref,
 ):
     cells_down, cells_across, _, model = ordered_ref.shape
     strip = order_ref.shape[0]
     order_ref[...] = strip_order(strip // SUB)
     gain = gain_ref[...].reshape(1, model)
 
-    def body(step, carry):
+    for step in range(cells_down // 2):
         normed = []
-        for part in range(2):
-            down = 2 * step + part
+        for down in (2 * step, 2 * step + 1):
             ordered = jnp.dot(
                 order_ref[...],
-                tokens_ref[pl.ds(down * SUB, SUB)].reshape(strip, model),
+                tokens_ref[down * SUB : (down + 1) * SUB].reshape(strip, model),
                 preferred_element_type=jnp.float32,
             )
             ordered_ref[down] = ordered.astype(jnp.bfloat16).reshape(cells_across, CELL, model)
             normed.append(norm_rows(ordered, gain))
-        out_ref[pl.ds(2 * step, 2)] = (
+        out_ref[2 * step : 2 * step + 2] = (
             jnp.dot(
                 jnp.concatenate(normed, axis=0), joint_ref[...], preferred_element_type=jnp.float32
             )
             .astype(jnp.bfloat16)
             .reshape(2, cells_across, CELL, 3 * model)
         )
-        return carry
-
-    lax.fori_loop(0, cells_down // 2, body, 0)
-    west_ref[...] = ordered_ref[:, 0]
-    east_ref[...] = ordered_ref[:, cells_across - 1]
-
-
-def inner_kernel(joint_ref, relative_ref, after_ref, out_ref, bias_ref):
     place = window_order()
-    turned = lax.dot_general(
-        relative_ref[...].reshape(-1, AREA), place, NT,
-        precision=HIGHEST, preferred_element_type=jnp.float32,
-    )
+    turned = exact(lambda part: lax.dot_general(part, place, NT, preferred_element_type=jnp.float32),
+                   relative_ref[...].reshape(-1, AREA))
     for group in range(HEADS // GROUP):
         rows = [
             turned[(group * GROUP + h) * AREA : (group * GROUP + h + 1) * AREA]
             for h in range(GROUP)
         ]
-        bias_ref[group] = jnp.dot(
-            place,
+        bias_ref[group] = exact(
+            lambda part: jnp.dot(place, part, preferred_element_type=jnp.float32),
             jnp.concatenate(rows, axis=1),
-            precision=HIGHEST,
-            preferred_element_type=jnp.float32,
-        )
+        )
+    west_ref[...] = ordered_ref[:, 0]
+    east_ref[...] = ordered_ref[:, cells_across - 1]
+
+
+def inner_kernel(joint_ref, bias_ref, after_ref, out_ref):
     cells_down, cells_across, _, triple = joint_ref.shape
     model = triple // 3
     blocks = head_blocks(GROUP * model // HEADS)
     bias = [bias_ref[group] for group in range(bias_ref.shape[0])]
 
-    def body(i, carry):
-        for j in range(cells_across // 2 - 1):
-            rows = joint_ref[pl.ds(2 * i + 1, 2), 2 * j + 1 : 2 * j + 3].reshape(AREA, triple)
+    for i in range(1, cells_down - 1, 2):
+        for j in range(1, cells_across - 1, 2):
+            rows = joint_ref[i : i + 2, j : j + 2].reshape(AREA, triple)
             mixed = attend(
                 rows[:, :model], rows[:, model : 2 * model], rows[:, 2 * model :], bias, blocks, None
             )
-            out_ref[pl.ds(2 * i + 1, 2), 2 * j + 1 : 2 * j + 3] = mixed.reshape(2, 2, CELL, model)
-        return carry
-
-    lax.fori_loop(0, cells_down // 2 - 1, body, 0)
+            out_ref[i : i + 2, j : j + 2] = mixed.reshape(2, 2, CELL, model)
 
 
 def lengthen_kernel(
@@ -708,7 +707,7 @@
     )(tokens)
 
 
-def joint_rows(tokens, gain, weight):
+def joint_rows(tokens, gain, weight, relative):
     tile_rows, tile_cols, model = tokens.shape
     down, across = tile_rows // SUB, tile_cols // SUB
     lone = lambda n: jax.ShapeDtypeStruct((n, CELL, model), jnp.bfloat16)
@@ -716,37 +715,35 @@
         joint_kernel,
         out_shape=(
             cells_of(down, across, weight.shape[1]),
+            jax.ShapeDtypeStruct((HEADS // GROUP, AREA, GROUP * AREA), jnp.float32),
             cells_of(down, across, model),
             lone(down), lone(down),
         ),
-        in_specs=[VMEM] * 3,
-        out_specs=(VMEM,) * 4,
+        in_specs=[VMEM] * 4,
+        out_specs=(VMEM,) * 5,
         scratch_shapes=[
             pltpu.VMEM((SUB * tile_cols, SUB * tile_cols), jnp.bfloat16),
         ],
         compiler_params=params(20),
         cost_estimate=cost(tokens.shape[0] * tile_cols, model * weight.shape[1]),
         name="joint_rows",
-    )(tokens, gain, weight)
+    )(tokens, gain, weight, relative)
 
 
 def cost(rows, weights):
     return pl.CostEstimate(flops=4 * rows * weights, bytes_accessed=4 * 2**20, transcendentals=0)
 
 
-def inner_windows(joint, relative, after):
+def inner_windows(joint, bias, after):
     return pl.pallas_call(
         inner_kernel,
-        out_shape=(
-            jax.ShapeDtypeStruct(joint.shape[:3] + (joint.shape[3] // 3,), jnp.bfloat16),
-            jax.ShapeDtypeStruct((HEADS // GROUP, AREA, GROUP * AREA), jnp.float32),
-        ),
+        out_shape=jax.ShapeDtypeStruct(joint.shape[:3] + (joint.shape[3] // 3,), jnp.bfloat16),
         in_specs=[VMEM, VMEM, pl.BlockSpec(memory_space=pl.ANY)],
-        out_specs=(VMEM, VMEM),
+        out_specs=VMEM,
         compiler_params=params(20),
         cost_estimate=cost(joint.shape[0] * joint.shape[1] * CELL, 2**19),
         name="inner_windows",
-    )(joint, relative, after)
+    )(joint, bias, after)
 
 
 def end_windows(joint, up, down, bias, gain, weight):
@@ -766,7 +763,7 @@
     down, across, _, triple = joint.shape
     model = triple // 3
     strip = CELL * across
-    rows = 2 * strip
+    rows = 4 * strip
     wide = weights[2].shape[1]
     tile = jax.ShapeDtypeStruct((down * SUB, across * SUB, weights[-1].shape[1]), jnp.bfloat16)
     return pl.pallas_call(
@@ -783,7 +780,7 @@
             pltpu.VMEM((2, rows, wide), jnp.float32),
             pltpu.VMEM((2, rows, wide), jnp.bfloat16),
         ],
-        compiler_params=params(28),
+        compiler_params=params(34),
         name="side_windows",
     )(ordered, joint, inner, pairs, ends, left, right, bias, *gains, *weights)
 
@@ -806,11 +803,13 @@
     first, last = end_rows(tokens)
     up = shift(last, "row", 1)
     down = shift(first, "row", -1)
-    joint, ordered, west, east = joint_rows(tokens, first_gain, joint_weight)
+    joint, bias, ordered, west, east = joint_rows(
+        tokens, first_gain, joint_weight, relative_bias
+    )
     up, down, west, east = lengthen(up, down, west, east)
     left = shift(east, "col", 1)
     right = shift(west, "col", -1)
-    inner, bias = inner_windows(joint, relative_bias, west)
+    inner = inner_windows(joint, bias, west)
     pairs, ends = end_windows(joint, up, down, bias, first_gain, joint_weight)
     features, features_here = side_windows(
         ordered, joint, inner, pairs, ends, left, right, bias, (first_gain, second_gain),

time: 84.2 us -> 81.7 us (0.970)
  Pallas kernels: 59.3 us -> 56.6 us
    pallas_call x1, Pallas kernels: 3.17 us -> 1.37 us  [inner_windows(): pl.pallas_call(inner_kernel, out_shape=jax.ShapeDtypeStruct(joint.shape[:...]
  transfers between devices with their start and end apart: 8 -> 8, of which waited for: 2 -> 2; matrix products, arithmetic and copies ran while one was open for 0% -> 0% of each run, Pallas kernels for 34% -> 33%
where the time goes in v5:
time: 81.7 us; the launch traced here: 80.5 us
  Pallas kernels  56.6 us (69%)
  starting transfers between devices  18.3 us (22%)
  waiting for transfers between devices  2.71 us (3%)
  between operations  1.58 us (2%)
  local copies, waits for them, and re-layouts  1.29 us (2%)
    pallas_call x1, Pallas kernels, mask_forward(): pl.pallas_call(forward_kernel, out_shape=(jax.ShapeDtypeStruct((boxes, 25...  20.3 us
    pallas_call x1, Pallas kernels, mask_backward(): pl.pallas_call(backward_kernel, out_shape=(jax.ShapeDtypeStruct(tile + (c...  20 us
    ppermute x4, starting transfers between devices, shift(): return lax.ppermute(x, axis, pairs)  10.6 us
    pallas_call x1, Pallas kernels, side_windows(): pl.pallas_call(sides_kernel, out_shape=(tile, tile), in_specs=[VMEM] * 15...  8.51 us
    ppermute x3, starting transfers between devices, shards(): lax.ppermute(both, 'row', [(i, (i + back) % rows_size) for i in range(row...  5.28 us
    pallas_call x1, Pallas kernels, joint_rows(): pl.pallas_call(joint_kernel, out_shape=(cells_of(down, across, weight.sha...  3.54 us
    ppermute x1, starting transfers between devices, shards(): lax.ppermute(send, 'row', [(i, i ^ 1) for i in range(rows_size)])  2.49 us
    ppermute x1, waiting for transfers between devices, shards(): lax.ppermute(send, 'row', [(i, i ^ 1) for i in range(rows_size)])  1.72 us
  transfers between devices with their start and end apart: 8, of which 2 were waited for; matrix products, arithmetic and copies ran while one was open for 0% of the time, Pallas kernels for 33%

profile of v5, /device:TPU:4, one launch (start us, length us, event | category | flops | bytes accessed | tf_op | source)
XLA Modules:
  0.0 80.5 jit_solution(8674457393581284233)
XLA Ops:
  0.6 0.0 copy-start.2
  0.6 0.0 copy-start.5
  0.7 0.0 copy-start.7
  0.7 1.2 %copy-done.7 = bf16[32,32,384]{2,1,0:T(8,128)(2,1)S(1)} copy-done((bf16[32,32,384]{2,1,0:T(8,128)(2,1)S(1)}, bf16[32,32,384]{2,1,0:T(8,128)(2,1)}, u32[]{:S(2)}) %copy-start.7) | copy-done | bytes 786456
  1.9 3.5 %collective-permute-start = (bf16[4,32,384]{2,1,0:T(8,128)(2,1)S(1)}, bf16[4,32,384]{2,1,0:T(8,128)(2,1)S(1)}, u32[]{:S(2)}, u32[]{:S(2)}) collective-permute-start(bf16[4,32,384]{2,1,0:T(8,128)(2,1)S(1)} %get-tuple-element.25), channel_id=1, source_target_pairs={{0,4},{4,8},{8,12},{12,16},{16,20},{20,24},{24,28},{1,5},{5,9},{9,... | collective-permute-start | bytes 294920 | tf_op jit(solution)/shard_map/ppermute | solution.py:794
  5.4 1.3 %collective-permute-start.1 = (bf16[4,32,384]{2,1,0:T(8,128)(2,1)S(1)}, bf16[4,32,384]{2,1,0:T(8,128)(2,1)S(1)}, u32[]{:S(2)}, u32[]{:S(2)}) collective-permute-start(bf16[4,32,384]{2,1,0:T(8,128)(2,1)S(1)} %get-tuple-element.26), channel_id=1, source_target_pairs={{4,0},{8,4},{12,8},{16,12},{20,16},{24,20},{28,24},{5,1},{9,5},{13... | collective-permute-start | bytes 294920 | tf_op jit(solution)/shard_map/ppermute | solution.py:794
  7.4 0.0 copy-done.2
  7.4 0.0 copy-done.5
  7.4 0.0 copy-done.8
  7.4 0.0 copy-done.9
  7.4 3.5 %joint_rows.1 = (bf16[8,8,16,1152]{3,2,1,0:T(8,128)(2,1)S(1)}, f32[3,64,256]{2,1,0:T(8,128)S(1)}, bf16[8,8,16,384]{3,2,1,0:T(8,128)(2,1)S(1)}, bf16[8,16,384]{2,1,0:T(8,128)(2,1)S(1)}, bf16[8,16,384]{2,1,0:T(8,128)(2,1)S(1)}) custom-call(bf16[32,32,384]{2,1,0:T(8,128)(2,1)S(1)} %copy-done.8, f32[384]{0:T(512)S(1)} %copy-done.5, ...), custom_call_target="tpu_custom_call" | custom-call | flops 1811939328 | bytes 4194304 | tf_op jit(solution)/shard_map/joint_rows/pallas_call | solution.py:714
  11.0 0.0 collective-permute-done.up_ref
  11.0 1.0 %collective-permute-done.1.down_ref = bf16[4,32,384]{2,1,0:T(8,128)(2,1)S(1)} collective-permute-done((bf16[4,32,384]{2,1,0:T(8,128)(2,1)S(1)}, bf16[4,32,384]{2,1,0:T(8,128)(2,1)S(1)}, u32[]{:S(2)}, u32[]{:S(2)}) %collective-permute-start.1) | collective-permute-done | bytes 98336 | tf_op jit(solution)/shard_map/ppermute | solution.py:794
  11.9 0.2 lengthen.1
  12.1 1.9 %collective-permute-start.2 = (bf16[10,16,384]{2,1,0:T(8,128)(2,1)S(1)}, bf16[10,16,384]{2,1,0:T(8,128)(2,1)S(1)}, u32[]{:S(2)}, u32[]{:S(2)}) collective-permute-start(bf16[10,16,384]{2,1,0:T(8,128)(2,1)S(1)} %get-tuple-element.34), channel_id=1, source_target_pairs={{0,1},{1,2},{2,3},{4,5},{5,6},{6,7},{8,9},{9,10},{10,11},{12,13},{... | collective-permute-start | bytes 368648 | tf_op jit(solution)/shard_map/ppermute | solution.py:794
  14.1 3.8 %collective-permute-start.3 = (bf16[10,16,384]{2,1,0:T(8,128)(2,1)S(1)}, bf16[10,16,384]{2,1,0:T(8,128)(2,1)S(1)}, u32[]{:S(2)}, u32[]{:S(2)}) collective-permute-start(bf16[10,16,384]{2,1,0:T(8,128)(2,1)S(1)} %get-tuple-element.29.after_ref), channel_id=1, source_target_pairs={{1,0},{2,1},{3,2},{5,4},{6,5},{7,6},{9,8},{10,9},{11,10},{13,12},{... | collective-permute-start | bytes 368648 | tf_op jit(solution)/shard_map/ppermute | solution.py:794
  17.9 1.4 %inner_windows.1.inner_ref = bf16[8,8,16,384]{3,2,1,0:T(8,128)(2,1)S(1)} custom-call(bf16[8,8,16,1152]{3,2,1,0:T(8,128)(2,1)S(1)} %get-tuple-element.23.joint_ref.joint_out_ref, f32[3,64,256]{2,1,0:T(8,128)S(1)} %get-tuple-element.24.bias_ref, bf16[10,16,384]{2,1,0:T(8,128)(2,1)S(1)} %get-tuple-element.29.after_ref), custom_call_target="tpu_custom_call" | custom-call | flops 2147483648 | bytes 4194304 | tf_op jit(solution)/shard_map/inner_windows/pallas_call | solution.py:738
  19.3 0.0 copy-start
  19.3 0.0 copy-start.1
  19.3 0.0 copy-start.3
  19.3 0.0 copy-start.4
  19.3 0.0 copy-start.6
  19.3 0.0 slice-start
  19.4 1.6 %end_windows.1 = (bf16[2,8,16,768]{3,2,1,0:T(8,128)(2,1)S(1)}, bf16[2,8,16,384]{3,2,1,0:T(8,128)(2,1)S(1)}) custom-call(bf16[8,8,16,1152]{3,2,1,0:T(8,128)(2,1)S(1)} %get-tuple-element.23.joint_ref.joint_out_ref, bf16[8,16,384]{2,1,0:T(8,128)(2,1)S(1)} %get-tuple-element.30.up_ref, bf16[8,16,384]{2,1,0:T(8,128)(2,1)S(1)} %get-tuple-element.31.down_ref, ...), custom_call_target="tpu_custom_call" | custom-call | flops 2147483648 | bytes 4194304 | tf_op jit(solution)/shard_map/end_windows/pallas_call | solution.py:751
  21.0 0.0 collective-permute-done.2.left_ref
  21.0 0.0 collective-permute-done.3.right_ref
  21.0 0.0 copy-done
  21.0 0.0 copy-done.1
  21.0 0.0 copy-done.3
  21.0 0.0 copy-done.4
  21.0 0.0 slice-start.1
  21.0 0.0 copy-start.11
  21.1 0.0 copy-start.12
  21.1 0.0 copy-start.13
  21.1 8.5 %side_windows.1 = (bf16[32,32,256]{2,1,0:T(8,128)(2,1)}, bf16[32,32,256]{2,1,0:T(8,128)(2,1)S(1)}) custom-call(bf16[8,8,16,384]{3,2,1,0:T(8,128)(2,1)S(1)} %get-tuple-element.22.ordered_ref, bf16[8,8,16,1152]{3,2,1,0:T(8,128)(2,1)S(1)} %get-tuple-element.23.joint_ref.joint_out_ref, bf16[8,8,16,384]{3,2,1,0:T(8,128)(2,1)S(1)} %inner_windows.1.inner_ref, ...), custom_call_target="tpu_custom_call" | custom-call | tf_op jit(solution)/shard_map/side_windows/pallas_call | solution.py:769
  29.6 0.0 slice-done.1
  29.6 0.0 copy-start.10
  29.6 20.3 %mask_forward.1 = (f32[16,256]{1,0:T(8,128)S(1)}, bf16[4,14,224,256]{3,2,1,0:T(8,128)(2,1)S(1)}) custom-call(s32[1,1,4,16]{3,2,1,0:T(4,128)S(1)} %bitcast.3, s32[1,1]{1,0:T(1,128)S(6)} %copy.18.count_ref, s32[1,1,16]{2,1,0:T(1,128)S(1)} %copy-done.12, bf16[32,32,256]{2,1,0:T(8,128)(2,1)S(1)} %get-tuple-element.36.features_ref, ...), custom_call_target="tpu_custom_call" | custom-call | flops 24999999488 | bytes 4718592 | tf_op jit(solution)/shard_map/mask_forward/pallas_call | solution.py:287
  50.0 2.5 %collective-permute-start.4 = (f32[16,256]{1,0:T(8,128)S(1)}, f32[16,256]{1,0:T(8,128)S(1)}, u32[]{:S(2)}, u32[]{:S(2)}) collective-permute-start(f32[16,256]{1,0:T(8,128)S(1)} %get-tuple-element.37.send_ref.own_ref), channel_id=1, source_target_pairs={{0,4},{4,0},{8,12},{12,8},{16,20},{20,16},{24,28},{28,24},{1,5},{5... | collective-permute-start | bytes 49160 | tf_op jit(solution)/shard_map/ppermute | solution.py:823
  52.5 1.7 %collective-permute-done.4.other_ref = f32[16,256]{1,0:T(8,128)S(1)} collective-permute-done((f32[16,256]{1,0:T(8,128)S(1)}, f32[16,256]{1,0:T(8,128)S(1)}, u32[]{:S(2)}, u32[]{:S(2)}) %collective-permute-start.4) | collective-permute-done | bytes 16416 | tf_op jit(solution)/shard_map/ppermute | solution.py:823
  54.2 4.3 %collective-permute-start.7 = (f32[32,256]{1,0:T(8,128)S(1)}, f32[32,256]{1,0:T(8,128)S(1)}, u32[]{:S(2)}, u32[]{:S(2)}) collective-permute-start(f32[32,256]{1,0:T(8,128)S(1)} %join_pair.1.refs_0_), channel_id=1, source_target_pairs={{0,24},{4,28},{8,0},{12,4},{16,8},{20,12},{24,16},{28,20},{1,25},{... | collective-permute-start | bytes 98312 | tf_op jit(solution)/shard_map/ppermute | solution.py:827
  58.5 0.0 collective-permute-start.6
  58.5 1.0 %collective-permute-start.5 = (f32[32,256]{1,0:T(8,128)S(1)}, f32[32,256]{1,0:T(8,128)S(1)}, u32[]{:S(2)}, u32[]{:S(2)}) collective-permute-start(f32[32,256]{1,0:T(8,128)S(1)} %join_pair.1.refs_0_), channel_id=1, source_target_pairs={{0,8},{4,12},{8,16},{12,20},{16,24},{20,28},{24,0},{28,4},{1,9},{5... | collective-permute-start | bytes 98312 | tf_op jit(solution)/shard_map/ppermute | solution.py:827
  59.5 20.0 %mask_backward.1 = (f32[32,32,256]{2,1,0:T(8,128)}, f32[8,128]{1,0:T(8,128)S(1)}) custom-call(s32[1,1,4,16]{3,2,1,0:T(4,128)S(1)} %bitcast.4, s32[1,1]{1,0:T(1,128)S(6)} %copy.18.count_ref, f32[16,256]{1,0:T(8,128)S(1)} %get-tuple-element.37.send_ref.own_ref, bf16[1,1,16,196]{3,2,1,0:T(8,128)(2,1)S(1)} %copy-done.10, ...), custom_call_target="tpu_custom_call" | custom-call | flops 24999999488 | bytes 4718592 | tf_op jit(solution)/shard_map/mask_backward/pallas_call | solution.py:312
  79.5 0.0 collective-permute-done.7.refs_3_
  79.5 0.0 collective-permute-done.6.refs_2_
  79.5 0.0 collective-permute-done.5.refs_1_
  79.5 1.0 %collect.1 = f32[1,1,8,196]{3,2,1,0:T(8,128)} custom-call(f32[32,256]{1,0:T(8,128)S(1)} %join_pair.1.refs_0_, f32[32,256]{1,0:T(8,128)S(1)} %collective-permute-done.5.refs_1_, f32[32,256]{1,0:T(8,128)S(1)} %collective-permute-done.6.refs_2_, f32[32,256]{1,0:T(8,128)S(1)} %collective-permute-done.7.refs_3_, f32[8,128]{1,0:T(8,128)S(1)} %get-tuple-element.40.refs_4_), custom_call_target="tpu_custom_call" | custom-call | tf_op jit(solution)/shard_map/collect/pallas_call | solution.py:334
  (11 shorter events, 0.0 us)
Async XLA Ops:
  0.6 6.7 %copy-start.2 = (bf16[384,1152]{1,0:T(8,128)(2,1)S(1)}, bf16[384,1152]{1,0:T(8,128)(2,1)}, u32[]{:S(2)}) copy-start(bf16[384,1152]{1,0:T(8,128)(2,1)} %joint_ref.5) | copy-start | bytes 2654212
  0.6 6.7 %copy-start.5 = (f32[384]{0:T(512)S(1)}, f32[384]{0:T(512)}, u32[]{:S(2)}) copy-start(f32[384]{0:T(512)} %first_ref.1) | copy-start | bytes 4612
  0.7 1.2 %copy-start.7 = (bf16[32,32,384]{2,1,0:T(8,128)(2,1)S(1)}, bf16[32,32,384]{2,1,0:T(8,128)(2,1)}, u32[]{:S(2)}) copy-start(bf16[32,32,384]{2,1,0:T(8,128)(2,1)} %tokens_ref.3) | copy-start | bytes 2359300
  1.9 5.5 %copy-start.8 = (bf16[32,32,384]{2,1,0:T(8,128)(2,1)S(1)}, bf16[32,32,384]{2,1,0:T(8,128)(2,1)}, u32[]{:S(2)}) copy-start(bf16[32,32,384]{2,1,0:T(8,128)(2,1)} %tokens_ref.3) | copy-start | bytes 2359300
  1.9 5.5 %copy-start.9 = (f32[12,64,64]{2,1,0:T(8,128)S(1)}, f32[12,64,64]{2,1,0:T(8,128)}, u32[]{:S(2)}) copy-start(f32[12,64,64]{2,1,0:T(8,128)} %relative_ref.1) | copy-start | bytes 589828
  1.9 9.1 %collective-permute-start = (bf16[4,32,384]{2,1,0:T(8,128)(2,1)S(1)}, bf16[4,32,384]{2,1,0:T(8,128)(2,1)S(1)}, u32[]{:S(2)}, u32[]{:S(2)}) collective-permute-start(bf16[4,32,384]{2,1,0:T(8,128)(2,1)S(1)} %get-tuple-element.25), channel_id=1, source_target_pairs={{0,4},{4,8},{8,12},{12,16},{16,20},{20,24},{24,28},{1,5},{5,9},{9,... | collective-permute-start | bytes 294920 | tf_op jit(solution)/shard_map/ppermute | solution.py:794
  5.4 6.5 %collective-permute-start.1 = (bf16[4,32,384]{2,1,0:T(8,128)(2,1)S(1)}, bf16[4,32,384]{2,1,0:T(8,128)(2,1)S(1)}, u32[]{:S(2)}, u32[]{:S(2)}) collective-permute-start(bf16[4,32,384]{2,1,0:T(8,128)(2,1)S(1)} %get-tuple-element.26), channel_id=1, source_target_pairs={{4,0},{8,4},{12,8},{16,12},{20,16},{24,20},{28,24},{5,1},{9,5},{13... | collective-permute-start | bytes 294920 | tf_op jit(solution)/shard_map/ppermute | solution.py:794
  12.1 8.8 %collective-permute-start.2 = (bf16[10,16,384]{2,1,0:T(8,128)(2,1)S(1)}, bf16[10,16,384]{2,1,0:T(8,128)(2,1)S(1)}, u32[]{:S(2)}, u32[]{:S(2)}) collective-permute-start(bf16[10,16,384]{2,1,0:T(8,128)(2,1)S(1)} %get-tuple-element.34), channel_id=1, source_target_pairs={{0,1},{1,2},{2,3},{4,5},{5,6},{6,7},{8,9},{9,10},{10,11},{12,13},{... | collective-permute-start | bytes 368648 | tf_op jit(solution)/shard_map/ppermute | solution.py:794
  14.1 6.9 %collective-permute-start.3 = (bf16[10,16,384]{2,1,0:T(8,128)(2,1)S(1)}, bf16[10,16,384]{2,1,0:T(8,128)(2,1)S(1)}, u32[]{:S(2)}, u32[]{:S(2)}) collective-permute-start(bf16[10,16,384]{2,1,0:T(8,128)(2,1)S(1)} %get-tuple-element.29.after_ref), channel_id=1, source_target_pairs={{1,0},{2,1},{3,2},{5,4},{6,5},{7,6},{9,8},{10,9},{11,10},{13,12},{... | collective-permute-start | bytes 368648 | tf_op jit(solution)/shard_map/ppermute | solution.py:794
  19.3 1.7 %copy-start = (bf16[384,1536]{1,0:T(8,128)(2,1)S(1)}, bf16[384,1536]{1,0:T(8,128)(2,1)}, u32[]{:S(2)}) copy-start(bf16[384,1536]{1,0:T(8,128)(2,1)} %expand_ref.1) | copy-start | bytes 3538948
  19.3 1.7 %copy-start.1 = (bf16[1536,384]{1,0:T(8,128)(2,1)S(1)}, bf16[1536,384]{1,0:T(8,128)(2,1)}, u32[]{:S(2)}) copy-start(bf16[1536,384]{1,0:T(8,128)(2,1)} %shrink_ref.1) | copy-start | bytes 3538948
  19.3 1.7 %copy-start.3 = (bf16[384,384]{1,0:T(8,128)(2,1)S(1)}, bf16[384,384]{1,0:T(8,128)(2,1)}, u32[]{:S(2)}) copy-start(bf16[384,384]{1,0:T(8,128)(2,1)} %merge_ref.1) | copy-start | bytes 884740
  19.3 1.7 %copy-start.4 = (bf16[384,256]{1,0:T(8,128)(2,1)S(1)}, bf16[384,256]{1,0:T(8,128)(2,1)}, u32[]{:S(2)}) copy-start(bf16[384,256]{1,0:T(8,128)(2,1)} %lateral_ref.1) | copy-start | bytes 589828
  19.3 1.7 %copy-start.6 = (f32[384]{0:T(512)S(1)}, f32[384]{0:T(512)}, u32[]{:S(2)}) copy-start(f32[384]{0:T(512)} %second_ref.1) | copy-start | bytes 4612
  19.3 10.2 %slice-start = ((s8[4718592]{0:T(1024)(128)(4,1)}), s8[4194304]{0:T(1024)(128)(4,1)S(1)}, s32[]{:S(2)}) async-start(s8[4718592]{0:T(1024)(128)(4,1)} %bitcast.1), calls=%async_computation | async-start | bytes 8388608
  21.0 8.6 %slice-start.1 = ((s8[4718592]{0:T(1024)(128)(4,1)}), s8[524288]{0:T(1024)(128)(4,1)S(1)}, s32[]{:S(2)}) async-start(s8[4718592]{0:T(1024)(128)(4,1)} %bitcast.1), calls=%async_computation.1 | async-start | bytes 1048576
  21.0 8.6 %copy-start.11 = (s32[1,1,16,4]{2,3,1,0:T(4,128)S(1)}, s32[1,1,16,4]{2,3,1,0:T(4,128)}, u32[]{:S(2)}) copy-start(s32[1,1,16,4]{2,3,1,0:T(4,128)} %param.26) | copy-start | bytes 772
  21.1 8.5 %copy-start.12 = (s32[1,1,16]{2,1,0:T(1,128)S(1)}, s32[1,1,16]{2,1,0:T(1,128)}, u32[]{:S(2)}) copy-start(s32[1,1,16]{2,1,0:T(1,128)} %owner_ref.1) | copy-start | bytes 196
  21.1 8.5 %copy-start.13 = (bf16[256]{0:T(256)(128)(2,1)S(1)}, bf16[256]{0:T(256)(128)(2,1)}, u32[]{:S(2)}) copy-start(bf16[256]{0:T(256)(128)(2,1)} %mask_ref.3) | copy-start | bytes 1540
  29.6 29.9 %copy-start.10 = (bf16[1,1,16,196]{3,2,1,0:T(8,128)(2,1)S(1)}, bf16[1,1,16,196]{3,2,1,0:T(8,128)(2,1)}, u32[]{:S(2)}) copy-start(bf16[1,1,16,196]{3,2,1,0:T(8,128)(2,1)} %soft_ref.1) | copy-start | bytes 18820
  50.0 4.2 %collective-permute-start.4 = (f32[16,256]{1,0:T(8,128)S(1)}, f32[16,256]{1,0:T(8,128)S(1)}, u32[]{:S(2)}, u32[]{:S(2)}) collective-permute-start(f32[16,256]{1,0:T(8,128)S(1)} %get-tuple-element.37.send_ref.own_ref), channel_id=1, source_target_pairs={{0,4},{4,0},{8,12},{12,8},{16,20},{20,16},{24,28},{28,24},{1,5},{5... | collective-permute-start | bytes 49160 | tf_op jit(solution)/shard_map/ppermute | solution.py:823
  54.2 25.3 %collective-permute-start.7 = (f32[32,256]{1,0:T(8,128)S(1)}, f32[32,256]{1,0:T(8,128)S(1)}, u32[]{:S(2)}, u32[]{:S(2)}) collective-permute-start(f32[32,256]{1,0:T(8,128)S(1)} %join_pair.1.refs_0_), channel_id=1, source_target_pairs={{0,24},{4,28},{8,0},{12,4},{16,8},{20,12},{24,16},{28,20},{1,25},{... | collective-permute-start | bytes 98312 | tf_op jit(solution)/shard_map/ppermute | solution.py:827
  58.5 21.0 %collective-permute-start.6 = (f32[32,256]{1,0:T(8,128)S(1)}, f32[32,256]{1,0:T(8,128)S(1)}, u32[]{:S(2)}, u32[]{:S(2)}) collective-permute-start(f32[32,256]{1,0:T(8,128)S(1)} %join_pair.1.refs_0_), channel_id=1, source_target_pairs={{0,16},{4,20},{8,24},{12,28},{16,0},{20,4},{24,8},{28,12},{1,17},{... | collective-permute-start | bytes 98312 | tf_op jit(solution)/shard_map/ppermute | solution.py:827
  58.5 21.0 %collective-permute-start.5 = (f32[32,256]{1,0:T(8,128)S(1)}, f32[32,256]{1,0:T(8,128)S(1)}, u32[]{:S(2)}, u32[]{:S(2)}) collective-permute-start(f32[32,256]{1,0:T(8,128)S(1)} %join_pair.1.refs_0_), channel_id=1, source_target_pairs={{0,8},{4,12},{8,16},{12,20},{16,24},{20,28},{24,0},{28,4},{1,9},{5... | collective-permute-start | bytes 98312 | tf_op jit(solution)/shard_map/ppermute | solution.py:827

commit v6 on v5

--- a/solution.py
+++ b/solution.py
@@ -208,17 +208,16 @@
 
     def descend(layer, before, target, u, v):
         piece = slice(v * boxes, (v + 1) * boxes)
-        slope = slope_ref[jnp.maximum(layer - 1, 0), u, piece].astype(jnp.float32)
-        slope = jnp.where(layer == 0, 1.0, slope)
-        target[u + 1, 1 + v] = (before[piece] * slope).astype(jnp.bfloat16)
-
-    def down(pair, carry):
-        layer = layers - 1 - 2 * pair
-        stages = [(layer, b_ref, a_ref), (layer - 1, a_ref, b_ref)]
-        chain(backward, descend, before_ref, stages)
-        return carry
-
-    lax.fori_loop(0, layers // 2, down, 0)
+        grad = before[piece]
+        if layer > 0:
+            grad = grad * slope_ref[layer - 1, u, piece].astype(jnp.float32)
+        target[u + 1, 1 + v] = grad.astype(jnp.bfloat16)
+
+    stages = []
+    for layer in reversed(range(layers)):
+        refs = (b_ref, a_ref) if (layers - layer) % 2 else (a_ref, b_ref)
+        stages.append((layer,) + refs)
+    chain(backward, descend, before_ref, stages)
     for u in range(CROP):
         spread_ref[u] = jnp.dot(
             place_ref[...],

time: 81.7 us -> 80.3 us (0.983)
  Pallas kernels: 56.6 us -> 55.3 us
    pallas_call x1, Pallas kernels: 20 us -> 18.6 us  [mask_backward(): pl.pallas_call(backward_kernel, out_shape=(jax.ShapeDtypeStruct(tile + (c...]
  transfers between devices with their start and end apart: 8 -> 8, of which waited for: 2 -> 2; matrix products, arithmetic and copies ran while one was open for 0% -> 0% of each run, Pallas kernels for 33% -> 32%
where the time goes in v6:
time: 80.3 us; the launch traced here: 79.2 us
  Pallas kernels  55.3 us (69%)
  starting transfers between devices  18.3 us (23%)
  waiting for transfers between devices  2.71 us (3%)
  between operations  1.58 us (2%)
  local copies, waits for them, and re-layouts  1.29 us (2%)
    pallas_call x1, Pallas kernels, mask_forward(): pl.pallas_call(forward_kernel, out_shape=(jax.ShapeDtypeStruct((boxes, 25...  20.3 us
    pallas_call x1, Pallas kernels, mask_backward(): pl.pallas_call(backward_kernel, out_shape=(jax.ShapeDtypeStruct(tile + (c...  18.6 us
    ppermute x4, starting transfers between devices, shift(): return lax.ppermute(x, axis, pairs)  10.6 us
    pallas_call x1, Pallas kernels, side_windows(): pl.pallas_call(sides_kernel, out_shape=(tile, tile), in_specs=[VMEM] * 15...  8.51 us
    ppermute x3, starting transfers between devices, shards(): lax.ppermute(both, 'row', [(i, (i + back) % rows_size) for i in range(row...  5.28 us
    pallas_call x1, Pallas kernels, joint_rows(): pl.pallas_call(joint_kernel, out_shape=(cells_of(down, across, weight.sha...  3.54 us
    ppermute x1, starting transfers between devices, shards(): lax.ppermute(send, 'row', [(i, i ^ 1) for i in range(rows_size)])  2.49 us
    ppermute x1, waiting for transfers between devices, shards(): lax.ppermute(send, 'row', [(i, i ^ 1) for i in range(rows_size)])  1.72 us
  transfers between devices with their start and end apart: 8, of which 2 were waited for; matrix products, arithmetic and copies ran while one was open for 0% of the time, Pallas kernels for 32%

profile of v6, /device:TPU:4, one launch (start us, length us, event | category | flops | bytes accessed | tf_op | source)
XLA Modules:
  0.0 79.2 jit_solution(5454768442266382411)
XLA Ops:
  0.6 0.0 copy-start.2
  0.6 0.0 copy-start.5
  0.7 0.0 copy-start.7
  0.7 1.2 %copy-done.7 = bf16[32,32,384]{2,1,0:T(8,128)(2,1)S(1)} copy-done((bf16[32,32,384]{2,1,0:T(8,128)(2,1)S(1)}, bf16[32,32,384]{2,1,0:T(8,128)(2,1)}, u32[]{:S(2)}) %copy-start.7) | copy-done | bytes 786456
  1.9 3.5 %collective-permute-start = (bf16[4,32,384]{2,1,0:T(8,128)(2,1)S(1)}, bf16[4,32,384]{2,1,0:T(8,128)(2,1)S(1)}, u32[]{:S(2)}, u32[]{:S(2)}) collective-permute-start(bf16[4,32,384]{2,1,0:T(8,128)(2,1)S(1)} %get-tuple-element.25), channel_id=1, source_target_pairs={{0,4},{4,8},{8,12},{12,16},{16,20},{20,24},{24,28},{1,5},{5,9},{9,... | collective-permute-start | bytes 294920 | tf_op jit(solution)/shard_map/ppermute | solution.py:793
  5.4 1.3 %collective-permute-start.1 = (bf16[4,32,384]{2,1,0:T(8,128)(2,1)S(1)}, bf16[4,32,384]{2,1,0:T(8,128)(2,1)S(1)}, u32[]{:S(2)}, u32[]{:S(2)}) collective-permute-start(bf16[4,32,384]{2,1,0:T(8,128)(2,1)S(1)} %get-tuple-element.26), channel_id=1, source_target_pairs={{4,0},{8,4},{12,8},{16,12},{20,16},{24,20},{28,24},{5,1},{9,5},{13... | collective-permute-start | bytes 294920 | tf_op jit(solution)/shard_map/ppermute | solution.py:793
  7.4 0.0 copy-done.2
  7.4 0.0 copy-done.5
  7.4 0.0 copy-done.8
  7.4 0.0 copy-done.9
  7.4 3.5 %joint_rows.1 = (bf16[8,8,16,1152]{3,2,1,0:T(8,128)(2,1)S(1)}, f32[3,64,256]{2,1,0:T(8,128)S(1)}, bf16[8,8,16,384]{3,2,1,0:T(8,128)(2,1)S(1)}, bf16[8,16,384]{2,1,0:T(8,128)(2,1)S(1)}, bf16[8,16,384]{2,1,0:T(8,128)(2,1)S(1)}) custom-call(bf16[32,32,384]{2,1,0:T(8,128)(2,1)S(1)} %copy-done.8, f32[384]{0:T(512)S(1)} %copy-done.5, ...), custom_call_target="tpu_custom_call" | custom-call | flops 1811939328 | bytes 4194304 | tf_op jit(solution)/shard_map/joint_rows/pallas_call | solution.py:713
  11.0 0.0 collective-permute-done.up_ref
  11.0 1.0 %collective-permute-done.1.down_ref = bf16[4,32,384]{2,1,0:T(8,128)(2,1)S(1)} collective-permute-done((bf16[4,32,384]{2,1,0:T(8,128)(2,1)S(1)}, bf16[4,32,384]{2,1,0:T(8,128)(2,1)S(1)}, u32[]{:S(2)}, u32[]{:S(2)}) %collective-permute-start.1) | collective-permute-done | bytes 98336 | tf_op jit(solution)/shard_map/ppermute | solution.py:793
  11.9 0.2 lengthen.1
  12.1 1.9 %collective-permute-start.2 = (bf16[10,16,384]{2,1,0:T(8,128)(2,1)S(1)}, bf16[10,16,384]{2,1,0:T(8,128)(2,1)S(1)}, u32[]{:S(2)}, u32[]{:S(2)}) collective-permute-start(bf16[10,16,384]{2,1,0:T(8,128)(2,1)S(1)} %get-tuple-element.34), channel_id=1, source_target_pairs={{0,1},{1,2},{2,3},{4,5},{5,6},{6,7},{8,9},{9,10},{10,11},{12,13},{... | collective-permute-start | bytes 368648 | tf_op jit(solution)/shard_map/ppermute | solution.py:793
  14.1 3.8 %collective-permute-start.3 = (bf16[10,16,384]{2,1,0:T(8,128)(2,1)S(1)}, bf16[10,16,384]{2,1,0:T(8,128)(2,1)S(1)}, u32[]{:S(2)}, u32[]{:S(2)}) collective-permute-start(bf16[10,16,384]{2,1,0:T(8,128)(2,1)S(1)} %get-tuple-element.29.after_ref), channel_id=1, source_target_pairs={{1,0},{2,1},{3,2},{5,4},{6,5},{7,6},{9,8},{10,9},{11,10},{13,12},{... | collective-permute-start | bytes 368648 | tf_op jit(solution)/shard_map/ppermute | solution.py:793
  17.9 1.4 %inner_windows.1.inner_ref = bf16[8,8,16,384]{3,2,1,0:T(8,128)(2,1)S(1)} custom-call(bf16[8,8,16,1152]{3,2,1,0:T(8,128)(2,1)S(1)} %get-tuple-element.23.joint_ref.joint_out_ref, f32[3,64,256]{2,1,0:T(8,128)S(1)} %get-tuple-element.24.bias_ref, bf16[10,16,384]{2,1,0:T(8,128)(2,1)S(1)} %get-tuple-element.29.after_ref), custom_call_target="tpu_custom_call" | custom-call | flops 2147483648 | bytes 4194304 | tf_op jit(solution)/shard_map/inner_windows/pallas_call | solution.py:737
  19.3 0.0 copy-start
  19.3 0.0 copy-start.1
  19.3 0.0 copy-start.3
  19.3 0.0 copy-start.4
  19.3 0.0 copy-start.6
  19.3 0.0 slice-start
  19.4 1.6 %end_windows.1 = (bf16[2,8,16,768]{3,2,1,0:T(8,128)(2,1)S(1)}, bf16[2,8,16,384]{3,2,1,0:T(8,128)(2,1)S(1)}) custom-call(bf16[8,8,16,1152]{3,2,1,0:T(8,128)(2,1)S(1)} %get-tuple-element.23.joint_ref.joint_out_ref, bf16[8,16,384]{2,1,0:T(8,128)(2,1)S(1)} %get-tuple-element.30.up_ref, bf16[8,16,384]{2,1,0:T(8,128)(2,1)S(1)} %get-tuple-element.31.down_ref, ...), custom_call_target="tpu_custom_call" | custom-call | flops 2147483648 | bytes 4194304 | tf_op jit(solution)/shard_map/end_windows/pallas_call | solution.py:750
  21.0 0.0 collective-permute-done.2.left_ref
  21.0 0.0 collective-permute-done.3.right_ref
  21.0 0.0 copy-done
  21.0 0.0 copy-done.1
  21.0 0.0 copy-done.4
  21.0 0.0 slice-start.1
  21.0 0.0 copy-start.11
  21.1 0.0 copy-start.12
  21.1 0.0 copy-start.13
  21.1 8.5 %side_windows.1 = (bf16[32,32,256]{2,1,0:T(8,128)(2,1)}, bf16[32,32,256]{2,1,0:T(8,128)(2,1)S(1)}) custom-call(bf16[8,8,16,384]{3,2,1,0:T(8,128)(2,1)S(1)} %get-tuple-element.22.ordered_ref, bf16[8,8,16,1152]{3,2,1,0:T(8,128)(2,1)S(1)} %get-tuple-element.23.joint_ref.joint_out_ref, bf16[8,8,16,384]{3,2,1,0:T(8,128)(2,1)S(1)} %inner_windows.1.inner_ref, ...), custom_call_target="tpu_custom_call" | custom-call | tf_op jit(solution)/shard_map/side_windows/pallas_call | solution.py:768
  29.6 0.0 slice-done.1
  29.6 0.0 copy-done.12
  29.6 0.0 copy-start.10
  29.6 20.3 %mask_forward.1 = (f32[16,256]{1,0:T(8,128)S(1)}, bf16[4,14,224,256]{3,2,1,0:T(8,128)(2,1)S(1)}) custom-call(s32[1,1,4,16]{3,2,1,0:T(4,128)S(1)} %bitcast.3, s32[1,1]{1,0:T(1,128)S(6)} %copy.18.count_ref, s32[1,1,16]{2,1,0:T(1,128)S(1)} %copy-done.12, bf16[32,32,256]{2,1,0:T(8,128)(2,1)S(1)} %get-tuple-element.36.features_ref, ...), custom_call_target="tpu_custom_call" | custom-call | flops 24999999488 | bytes 4718592 | tf_op jit(solution)/shard_map/mask_forward/pallas_call | solution.py:286
  50.0 2.5 %collective-permute-start.4 = (f32[16,256]{1,0:T(8,128)S(1)}, f32[16,256]{1,0:T(8,128)S(1)}, u32[]{:S(2)}, u32[]{:S(2)}) collective-permute-start(f32[16,256]{1,0:T(8,128)S(1)} %get-tuple-element.37.send_ref.own_ref), channel_id=1, source_target_pairs={{0,4},{4,0},{8,12},{12,8},{16,20},{20,16},{24,28},{28,24},{1,5},{5... | collective-permute-start | bytes 49160 | tf_op jit(solution)/shard_map/ppermute | solution.py:822
  52.5 1.7 %collective-permute-done.4.other_ref = f32[16,256]{1,0:T(8,128)S(1)} collective-permute-done((f32[16,256]{1,0:T(8,128)S(1)}, f32[16,256]{1,0:T(8,128)S(1)}, u32[]{:S(2)}, u32[]{:S(2)}) %collective-permute-start.4) | collective-permute-done | bytes 16416 | tf_op jit(solution)/shard_map/ppermute | solution.py:822
  54.2 4.3 %collective-permute-start.7 = (f32[32,256]{1,0:T(8,128)S(1)}, f32[32,256]{1,0:T(8,128)S(1)}, u32[]{:S(2)}, u32[]{:S(2)}) collective-permute-start(f32[32,256]{1,0:T(8,128)S(1)} %join_pair.1.refs_0_), channel_id=1, source_target_pairs={{0,24},{4,28},{8,0},{12,4},{16,8},{20,12},{24,16},{28,20},{1,25},{... | collective-permute-start | bytes 98312 | tf_op jit(solution)/shard_map/ppermute | solution.py:826
  58.5 0.0 collective-permute-start.6
  58.5 1.0 %collective-permute-start.5 = (f32[32,256]{1,0:T(8,128)S(1)}, f32[32,256]{1,0:T(8,128)S(1)}, u32[]{:S(2)}, u32[]{:S(2)}) collective-permute-start(f32[32,256]{1,0:T(8,128)S(1)} %join_pair.1.refs_0_), channel_id=1, source_target_pairs={{0,8},{4,12},{8,16},{12,20},{16,24},{20,28},{24,0},{28,4},{1,9},{5... | collective-permute-start | bytes 98312 | tf_op jit(solution)/shard_map/ppermute | solution.py:826
  59.5 18.6 %mask_backward.1 = (f32[32,32,256]{2,1,0:T(8,128)}, f32[8,128]{1,0:T(8,128)S(1)}) custom-call(s32[1,1,4,16]{3,2,1,0:T(4,128)S(1)} %bitcast.4, s32[1,1]{1,0:T(1,128)S(6)} %copy.18.count_ref, f32[16,256]{1,0:T(8,128)S(1)} %get-tuple-element.37.send_ref.own_ref, bf16[1,1,16,196]{3,2,1,0:T(8,128)(2,1)S(1)} %copy-done.10, ...), custom_call_target="tpu_custom_call" | custom-call | flops 24999999488 | bytes 4718592 | tf_op jit(solution)/shard_map/mask_backward/pallas_call | solution.py:311
  78.1 0.0 collective-permute-done.7.refs_3_
  78.1 0.0 collective-permute-done.6.refs_2_
  78.1 0.0 collective-permute-done.5.refs_1_
  78.1 1.0 %collect.1 = f32[1,1,8,196]{3,2,1,0:T(8,128)} custom-call(f32[32,256]{1,0:T(8,128)S(1)} %join_pair.1.refs_0_, f32[32,256]{1,0:T(8,128)S(1)} %collective-permute-done.5.refs_1_, f32[32,256]{1,0:T(8,128)S(1)} %collective-permute-done.6.refs_2_, f32[32,256]{1,0:T(8,128)S(1)} %collective-permute-done.7.refs_3_, f32[8,128]{1,0:T(8,128)S(1)} %get-tuple-element.40.refs_4_), custom_call_target="tpu_custom_call" | custom-call | tf_op jit(solution)/shard_map/collect/pallas_call | solution.py:333
  (11 shorter events, 0.0 us)
Async XLA Ops:
  0.6 6.7 %copy-start.2 = (bf16[384,1152]{1,0:T(8,128)(2,1)S(1)}, bf16[384,1152]{1,0:T(8,128)(2,1)}, u32[]{:S(2)}) copy-start(bf16[384,1152]{1,0:T(8,128)(2,1)} %joint_ref.5) | copy-start | bytes 2654212
  0.6 6.7 %copy-start.5 = (f32[384]{0:T(512)S(1)}, f32[384]{0:T(512)}, u32[]{:S(2)}) copy-start(f32[384]{0:T(512)} %first_ref.1) | copy-start | bytes 4612
  0.7 1.2 %copy-start.7 = (bf16[32,32,384]{2,1,0:T(8,128)(2,1)S(1)}, bf16[32,32,384]{2,1,0:T(8,128)(2,1)}, u32[]{:S(2)}) copy-start(bf16[32,32,384]{2,1,0:T(8,128)(2,1)} %tokens_ref.3) | copy-start | bytes 2359300
  1.9 5.5 %copy-start.8 = (bf16[32,32,384]{2,1,0:T(8,128)(2,1)S(1)}, bf16[32,32,384]{2,1,0:T(8,128)(2,1)}, u32[]{:S(2)}) copy-start(bf16[32,32,384]{2,1,0:T(8,128)(2,1)} %tokens_ref.3) | copy-start | bytes 2359300
  1.9 5.5 %copy-start.9 = (f32[12,64,64]{2,1,0:T(8,128)S(1)}, f32[12,64,64]{2,1,0:T(8,128)}, u32[]{:S(2)}) copy-start(f32[12,64,64]{2,1,0:T(8,128)} %relative_ref.1) | copy-start | bytes 589828
  1.9 9.1 %collective-permute-start = (bf16[4,32,384]{2,1,0:T(8,128)(2,1)S(1)}, bf16[4,32,384]{2,1,0:T(8,128)(2,1)S(1)}, u32[]{:S(2)}, u32[]{:S(2)}) collective-permute-start(bf16[4,32,384]{2,1,0:T(8,128)(2,1)S(1)} %get-tuple-element.25), channel_id=1, source_target_pairs={{0,4},{4,8},{8,12},{12,16},{16,20},{20,24},{24,28},{1,5},{5,9},{9,... | collective-permute-start | bytes 294920 | tf_op jit(solution)/shard_map/ppermute | solution.py:793
  5.4 6.5 %collective-permute-start.1 = (bf16[4,32,384]{2,1,0:T(8,128)(2,1)S(1)}, bf16[4,32,384]{2,1,0:T(8,128)(2,1)S(1)}, u32[]{:S(2)}, u32[]{:S(2)}) collective-permute-start(bf16[4,32,384]{2,1,0:T(8,128)(2,1)S(1)} %get-tuple-element.26), channel_id=1, source_target_pairs={{4,0},{8,4},{12,8},{16,12},{20,16},{24,20},{28,24},{5,1},{9,5},{13... | collective-permute-start | bytes 294920 | tf_op jit(solution)/shard_map/ppermute | solution.py:793
  12.1 8.8 %collective-permute-start.2 = (bf16[10,16,384]{2,1,0:T(8,128)(2,1)S(1)}, bf16[10,16,384]{2,1,0:T(8,128)(2,1)S(1)}, u32[]{:S(2)}, u32[]{:S(2)}) collective-permute-start(bf16[10,16,384]{2,1,0:T(8,128)(2,1)S(1)} %get-tuple-element.34), channel_id=1, source_target_pairs={{0,1},{1,2},{2,3},{4,5},{5,6},{6,7},{8,9},{9,10},{10,11},{12,13},{... | collective-permute-start | bytes 368648 | tf_op jit(solution)/shard_map/ppermute | solution.py:793
  14.1 6.9 %collective-permute-start.3 = (bf16[10,16,384]{2,1,0:T(8,128)(2,1)S(1)}, bf16[10,16,384]{2,1,0:T(8,128)(2,1)S(1)}, u32[]{:S(2)}, u32[]{:S(2)}) collective-permute-start(bf16[10,16,384]{2,1,0:T(8,128)(2,1)S(1)} %get-tuple-element.29.after_ref), channel_id=1, source_target_pairs={{1,0},{2,1},{3,2},{5,4},{6,5},{7,6},{9,8},{10,9},{11,10},{13,12},{... | collective-permute-start | bytes 368648 | tf_op jit(solution)/shard_map/ppermute | solution.py:793
  19.3 1.7 %copy-start = (bf16[384,1536]{1,0:T(8,128)(2,1)S(1)}, bf16[384,1536]{1,0:T(8,128)(2,1)}, u32[]{:S(2)}) copy-start(bf16[384,1536]{1,0:T(8,128)(2,1)} %expand_ref.1) | copy-start | bytes 3538948
  19.3 1.7 %copy-start.1 = (bf16[1536,384]{1,0:T(8,128)(2,1)S(1)}, bf16[1536,384]{1,0:T(8,128)(2,1)}, u32[]{:S(2)}) copy-start(bf16[1536,384]{1,0:T(8,128)(2,1)} %shrink_ref.1) | copy-start | bytes 3538948
  19.3 1.7 %copy-start.3 = (bf16[384,384]{1,0:T(8,128)(2,1)S(1)}, bf16[384,384]{1,0:T(8,128)(2,1)}, u32[]{:S(2)}) copy-start(bf16[384,384]{1,0:T(8,128)(2,1)} %merge_ref.1) | copy-start | bytes 884740
  19.3 1.7 %copy-start.4 = (bf16[384,256]{1,0:T(8,128)(2,1)S(1)}, bf16[384,256]{1,0:T(8,128)(2,1)}, u32[]{:S(2)}) copy-start(bf16[384,256]{1,0:T(8,128)(2,1)} %lateral_ref.1) | copy-start | bytes 589828
  19.3 1.7 %copy-start.6 = (f32[384]{0:T(512)S(1)}, f32[384]{0:T(512)}, u32[]{:S(2)}) copy-start(f32[384]{0:T(512)} %second_ref.1) | copy-start | bytes 4612
  19.3 10.2 %slice-start = ((s8[4718592]{0:T(1024)(128)(4,1)}), s8[4194304]{0:T(1024)(128)(4,1)S(1)}, s32[]{:S(2)}) async-start(s8[4718592]{0:T(1024)(128)(4,1)} %bitcast.1), calls=%async_computation | async-start | bytes 8388608
  21.0 8.6 %slice-start.1 = ((s8[4718592]{0:T(1024)(128)(4,1)}), s8[524288]{0:T(1024)(128)(4,1)S(1)}, s32[]{:S(2)}) async-start(s8[4718592]{0:T(1024)(128)(4,1)} %bitcast.1), calls=%async_computation.1 | async-start | bytes 1048576
  21.0 8.6 %copy-start.11 = (s32[1,1,16,4]{2,3,1,0:T(4,128)S(1)}, s32[1,1,16,4]{2,3,1,0:T(4,128)}, u32[]{:S(2)}) copy-start(s32[1,1,16,4]{2,3,1,0:T(4,128)} %param.26) | copy-start | bytes 772
  21.1 8.5 %copy-start.12 = (s32[1,1,16]{2,1,0:T(1,128)S(1)}, s32[1,1,16]{2,1,0:T(1,128)}, u32[]{:S(2)}) copy-start(s32[1,1,16]{2,1,0:T(1,128)} %owner_ref.1) | copy-start | bytes 196
  21.1 8.5 %copy-start.13 = (bf16[256]{0:T(256)(128)(2,1)S(1)}, bf16[256]{0:T(256)(128)(2,1)}, u32[]{:S(2)}) copy-start(bf16[256]{0:T(256)(128)(2,1)} %mask_ref.3) | copy-start | bytes 1540
  29.6 29.9 %copy-start.10 = (bf16[1,1,16,196]{3,2,1,0:T(8,128)(2,1)S(1)}, bf16[1,1,16,196]{3,2,1,0:T(8,128)(2,1)}, u32[]{:S(2)}) copy-start(bf16[1,1,16,196]{3,2,1,0:T(8,128)(2,1)} %soft_ref.1) | copy-start | bytes 18820
  50.0 4.2 %collective-permute-start.4 = (f32[16,256]{1,0:T(8,128)S(1)}, f32[16,256]{1,0:T(8,128)S(1)}, u32[]{:S(2)}, u32[]{:S(2)}) collective-permute-start(f32[16,256]{1,0:T(8,128)S(1)} %get-tuple-element.37.send_ref.own_ref), channel_id=1, source_target_pairs={{0,4},{4,0},{8,12},{12,8},{16,20},{20,16},{24,28},{28,24},{1,5},{5... | collective-permute-start | bytes 49160 | tf_op jit(solution)/shard_map/ppermute | solution.py:822
  54.2 23.9 %collective-permute-start.7 = (f32[32,256]{1,0:T(8,128)S(1)}, f32[32,256]{1,0:T(8,128)S(1)}, u32[]{:S(2)}, u32[]{:S(2)}) collective-permute-start(f32[32,256]{1,0:T(8,128)S(1)} %join_pair.1.refs_0_), channel_id=1, source_target_pairs={{0,24},{4,28},{8,0},{12,4},{16,8},{20,12},{24,16},{28,20},{1,25},{... | collective-permute-start | bytes 98312 | tf_op jit(solution)/shard_map/ppermute | solution.py:826
  58.5 19.6 %collective-permute-start.6 = (f32[32,256]{1,0:T(8,128)S(1)}, f32[32,256]{1,0:T(8,128)S(1)}, u32[]{:S(2)}, u32[]{:S(2)}) collective-permute-start(f32[32,256]{1,0:T(8,128)S(1)} %join_pair.1.refs_0_), channel_id=1, source_target_pairs={{0,16},{4,20},{8,24},{12,28},{16,0},{20,4},{24,8},{28,12},{1,17},{... | collective-permute-start | bytes 98312 | tf_op jit(solution)/shard_map/ppermute | solution.py:826
  58.5 19.6 %collective-permute-start.5 = (f32[32,256]{1,0:T(8,128)S(1)}, f32[32,256]{1,0:T(8,128)S(1)}, u32[]{:S(2)}, u32[]{:S(2)}) collective-permute-start(f32[32,256]{1,0:T(8,128)S(1)} %join_pair.1.refs_0_), channel_id=1, source_target_pairs={{0,8},{4,12},{8,16},{12,20},{16,24},{20,28},{24,0},{28,4},{1,9},{5... | collective-permute-start | bytes 98312 | tf_op jit(solution)/shard_map/ppermute | solution.py:826
